TPU v7x, 128 devices: a whole 4x4x4 slice. The times are simulated.
128 devices in a mesh: space: 16 (over z_hi, x, core), cuts: 8 (over z_lo, y).
Axes of the slice: x: 4, y: 4, z: 4 (z_hi: 2, z_lo: 2; z = z_hi * 2 + z_lo), core: 2. Of those that a mesh axis runs over, the one named last changes fastest.
Arguments:
- velocity: float32 [8, 3, 256, 128, 256], P('cuts', None, 'space'), may hold values from -2.5 to 2.5
- atlas_image: float32 [256, 128, 256], P('space', 'cuts'), may hold values from -6 to 6
- target: float32 [256, 128, 256], P('space', 'cuts'), may hold values from -6 to 6
- labels: int32 [256, 128, 256], P('space', 'cuts'), may hold values from 0 to 63
- label_table: float32 [64], replicated, may hold values from -1 to 1
- counts: int32 [128], P(('space', 'cuts')), may hold values from 16384 to 65536, as said below
Outputs:
- gradient: float32 [8, 3, 256, 128, 256], P('cuts', None, 'space')
Inputs may be any that keep to these rules, and one draw needn't show every extreme that they name: counts[k] belongs to the tile of mesh position k, space-major; the masked voxels of a tile are its first counts[k] voxels in first, second, third dimension order.
All inputs are finite; a program needn't handle non-finite values.
Results may differ from a plain program's by a relative error of at most 0.0003.
Values sent between devices are 32-bit elements; how exact they have to be, the bound alone decides.
No kernel may reach another device: no remote copies, remote signals or barrier semaphores. Data moves between devices by JAX's collectives and lax.ppermute only.
A program may use at most 128 MiB of HBM per device.

v0:
```python
import jax
import jax.numpy as jnp
from jax import lax
from jax.sharding import PartitionSpec as P

NT = 8
SMOOTH = 2


DATA_WEIGHT = 4.0
KAPPA = 0.125


def padded_2(value, sides, width):
    for axis, dim in sides:
        size, length = (lax.axis_size(axis), value.shape[dim])
        up = [(i, (i + 1) % size) for i in range(size - 1)]
        down = [(j, i) for i, j in up]
        last = lax.slice_in_dim(value, length - width, length, axis=dim)
        initial = lax.slice_in_dim(value, 0, width, axis=dim)
        before = lax.ppermute(last, axis, up)
        after = lax.ppermute(initial, axis, down)
        value = jnp.concatenate([before, value, after], axis=dim)
    return value


def deepen(padded):
    return jnp.pad(padded, [(0, 0)] * (padded.ndim - 1) + [(1, 1)])


def differences(padded):
    middle = padded[..., 1:-1, 1:-1, 1:-1]
    behind = [
        padded[..., :-2, 1:-1, 1:-1],
        padded[..., 1:-1, :-2, 1:-1],
        padded[..., 1:-1, 1:-1, :-2],
    ]
    beyond = [padded[..., 2:, 1:-1, 1:-1], padded[..., 1:-1, 2:, 1:-1], padded[..., 1:-1, 1:-1, 2:]]
    return (middle, behind, beyond)


def advance(intensity_pad, velocity_now, time_step):
    middle, behind, beyond = differences(intensity_pad)
    outflow = jnp.zeros_like(middle)
    for direction in range(3):
        outflow = (
            outflow
            + jnp.maximum(velocity_now[direction], 0.0) * (middle - behind[direction])
            + jnp.minimum(velocity_now[direction], 0.0) * (beyond[direction] - middle)
        )
    return middle - time_step * outflow


def sensitivity(intensity_pad, velocity_now, costate, time_step):
    middle, behind, beyond = differences(intensity_pad)
    pieces = []
    for direction in range(3):
        slope = jnp.where(
            velocity_now[direction] > 0.0, middle - behind[direction], beyond[direction] - middle
        )
        pieces.append(-time_step * costate * slope)
    return jnp.stack(pieces)


def transposed(costate_pad, velocity_pad, time_step):
    forward_part = jnp.maximum(velocity_pad, 0.0) * costate_pad[None]
    backward_part = jnp.minimum(velocity_pad, 0.0) * costate_pad[None]
    middle_now = costate_pad[1:-1, 1:-1, 1:-1]
    change = jnp.zeros_like(middle_now)
    for direction in range(3):
        f_middle, f_behind, f_beyond = differences(forward_part[direction])
        b_middle, b_behind, b_beyond = differences(backward_part[direction])
        change = change + (f_middle - f_beyond[direction]) + (b_behind[direction] - b_middle)
    return middle_now - time_step * change


def diffuse(padded):
    middle, behind, beyond = differences(padded)
    neighbours = behind[0] + beyond[0] + behind[1] + beyond[1] + behind[2] + beyond[2]
    return middle + KAPPA * (neighbours - 6.0 * middle)


def lookup_labels(labels, label_table):
    template = jnp.zeros(labels.shape, label_table.dtype)
    for label_value in range(label_table.shape[0]):
        template = template + jnp.where(labels == label_value, label_table[label_value], 0.0)
    return template


def tile_positions(rows, cols, depth):
    first = lax.broadcasted_iota(jnp.int32, (rows, cols, depth), 0) * (cols * depth)
    second = lax.broadcasted_iota(jnp.int32, (rows, cols, depth), 1) * depth
    return first + second + lax.broadcasted_iota(jnp.int32, (rows, cols, depth), 2)


def adjoint_step(costate, velocity_pad, time_step):
    costate_pad = deepen(padded_2(costate, (("space", 0), ("cuts", 1)), 1))
    return transposed(costate_pad, velocity_pad, time_step)


def shards(velocity, atlas_image, target, labels, label_table, counts):
    time_step = 1.0 / NT
    tiled = lax.all_to_all(velocity, "cuts", split_axis=3, concat_axis=0, tiled=True)
    rows, cols, depth = atlas_image.shape
    positions = tile_positions(rows, cols, depth)
    masked = (positions < counts[0]).astype(jnp.float32)
    voxel_total = lax.psum(counts.astype(jnp.float32)[0], ("space", "cuts"))
    weighting = rows * cols * depth * lax.axis_size("space") * lax.axis_size("cuts") / voxel_total
    intensity = atlas_image + lookup_labels(labels, label_table)
    states = []
    velocity_pads = []
    for moment in range(NT):
        joined = jnp.concatenate([intensity[None], tiled[moment]], axis=0)
        padded = deepen(padded_2(joined, (("space", 1), ("cuts", 2)), 1))
        states.append(padded[0])
        velocity_pads.append(padded[1:])
        intensity = advance(padded[0], tiled[moment], time_step)
    costate = DATA_WEIGHT * weighting * masked * (intensity - target)
    gradients = [None] * NT
    for moment in range(NT - 1, -1, -1):
        gradients[moment] = sensitivity(states[moment], tiled[moment], costate, time_step)
        if moment > 0:
            costate = adjoint_step(costate, velocity_pads[moment], time_step)
    smoothed = jnp.stack(gradients)
    for sweep in range(SMOOTH):
        smoothed = diffuse(deepen(padded_2(smoothed, (("space", 2), ("cuts", 3)), 1)))
    result = lax.all_to_all(tiled + smoothed, "cuts", split_axis=0, concat_axis=3, tiled=True)
    return result


def solution(mesh):
    in_specs = (
        P("cuts", None, "space", None, None),
        P("space", "cuts", None),
        P("space", "cuts", None),
        P("space", "cuts", None),
        P(),
        P(("space", "cuts")),
    )
    out_specs = P("cuts", None, "space", None, None)
    return jax.shard_map(shards, mesh=mesh, in_specs=in_specs, out_specs=out_specs, check_vma=False)
```

profile of v0, /device:TPU:15, one launch (start us, length us, event | category | flops | bytes accessed | tf_op | source)
XLA Modules:
  0.0 759.4 jit_solution(8624608274450718005)
XLA Ops:
  0.0 9.1 %copy.112 = f32[1,3,16,128,256]{4,2,1,0,3:T(8,128)} copy(f32[1,3,16,128,256]{4,3,2,1,0:T(8,128)} %param.6) | data formatting | bytes 12582912 | tf_op args[0]
  17.9 41.9 %add_bitcast_fusion = f32[1,16,16,256]{3,2,1,0:T(8,128)S(1)} fusion(f32[16,16,256]{2,1,0:T(8,128)S(1)} %copy-done.33, s32[16,16,256]{2,1,0:T(8,128)S(1)} %copy-done.34, f32[]{:T(128)} %bitcast.68, f32[]{:T(128)} %bitcast.67, f32[]{:T(128)} %bitcast.66, f32[]{:T(128)} %bitcast.65, f32[]{:T(128)} %bitcast.64, f32[]{:T(128)} %bitcast.63, f32[]{:T(128)} %bitcast.62, ...), kind=kLoop, calls=%fused_computation.525 | loop fusion | flops 12582912 | bytes 786688 | tf_op jit(solution)/shard_map/broadcast_in_dim | solution.py:113
  59.8 45.2 %all-to-all-done = f32[1,3,16,128,256]{4,2,1,0,3:T(8,128)} async-done(((f32[1,3,16,128,256]{4,2,1,0,3:T(8,128)}), f32[1,3,16,128,256]{4,2,1,0,3:T(8,128)}, u32[]{:S(2)}, u32[]{:S(2)}) %all-to-all-start) | async-done | bytes 6291488 | tf_op jit(solution)/shard_map/all_to_all | solution.py:103
  114.5 6.9 collective-permute-start
  123.6 6.9 collective-permute-done.1
  147.6 7.3 collective-permute-done.5
  172.7 7.3 collective-permute-done.9
  197.9 7.3 collective-permute-done.13
  223.0 7.3 collective-permute-done.17
  248.1 7.3 collective-permute-done.21
  273.3 7.3 collective-permute-done.25
  299.5 64.5 %psum.7 = f32[]{:T(128)} all-reduce(f32[]{:T(128)} %bitcast.4), channel_id=1, replica_groups=mesh['space'=16,'cuts'=8] {'space','cuts'}, use_global_device_ids=true, to_apply=%region_0.0 | all-reduce | flops 1 | bytes 8 | tf_op jit(solution)/shard_map/psum | solution.py:107
  385.2 6.7 collective-permute-done.33
  412.0 6.7 collective-permute-done.37
  435.4 6.7 collective-permute-done.41
  458.6 6.7 collective-permute-done.45
  481.9 6.7 collective-permute-done.49
  556.4 8.0 %collective-permute-done.61 = f32[8,3,1,16,256]{4,3,2,1,0:T(8,128)S(1)} collective-permute-done((f32[8,3,1,16,256]{4,3,2,1,0:T(8,128)S(1)}, f32[8,3,1,16,256]{4,3,2,1,0:T(8,128)S(1)}, u32[]{:S(2)}, u32[]{:S(2)}) %collective-permute-start.61) | collective-permute-done | bytes 393248 | tf_op jit(solution)/shard_map/ppermute | solution.py:22
  578.1 12.7 %select_maximum_fusion.4 = f32[8,3,18,18,258]{4,3,2,1,0:T(8,128)} fusion(f32[8,3,18,1,256]{4,3,2,1,0:T(1,128)S(1)} %collective-permute-done.63, f32[8,3,18,1,256]{4,3,2,1,0:T(1,128)S(1)} %collective-permute-done.62, f32[8,3,1,16,256]{4,3,2,1,0:T(8,128)S(1)} %collective-permute-done.61, f32[8,3,16,16,256]{4,3,2,1,0:T(8,128)S(1)} %fusion.21, ...), kind=kLoop, calls=%fused_computation.6 | loop fusion | flops 24074496 | bytes 15987456 | tf_op jit(solution)/shard_map/concatenate | solution.py:23
  590.7 21.6 %fusion.10 = f32[8,3,16,16,256]{4,3,2,1,0:T(8,128)} fusion(f32[8,3,16,16,256]{4,3,2,1,0:T(8,128)} %copy-done.2, f32[8,3,18,18,258]{4,3,2,1,0:T(8,128)} %select_maximum_fusion.4, f32[8,3,18,1,256]{4,3,2,1,0:T(1,128)S(1)} %collective-permute-done.63, f32[8,3,1,16,256]{4,3,2,1,0:T(8,128)S(1)} %collective-permute-done.61, ...), kind=kLoop, calls=%fused_computation.31 | loop fusion | flops 26738688 | bytes 26836992 | tf_op jit(solution)/shard_map/add | solution.py:80
  621.1 8.3 %collective-permute-done.65 = f32[8,3,1,16,256]{4,3,2,1,0:T(8,128)S(1)} collective-permute-done((f32[8,3,1,16,256]{4,3,2,1,0:T(8,128)S(1)}, f32[8,3,1,16,256]{4,3,2,1,0:T(8,128)S(1)}, u32[]{:S(2)}, u32[]{:S(2)}) %collective-permute-start.65) | collective-permute-done | bytes 393248 | tf_op jit(solution)/shard_map/ppermute | solution.py:22
  647.0 12.7 %select_maximum_fusion = f32[8,3,18,18,258]{4,3,2,1,0:T(8,128)} fusion(f32[8,3,18,1,256]{4,3,2,1,0:T(1,128)S(1)} %collective-permute-done.67, f32[8,3,18,1,256]{4,3,2,1,0:T(1,128)S(1)} %collective-permute-done.66, f32[8,3,1,16,256]{4,3,2,1,0:T(8,128)S(1)} %collective-permute-done.65, f32[8,3,16,16,256]{4,3,2,1,0:T(8,128)S(1)} %copy-done.1, ...), kind=kLoop, calls=%fused_computation.2 | loop fusion | flops 24074496 | bytes 15987456 | tf_op jit(solution)/shard_map/concatenate | solution.py:23
  659.7 22.2 %fusion.4 = f32[8,3,16,16,256]{4,3,2,1,0:T(8,128)} fusion(f32[8,3,16,16,256]{4,3,2,1,0:T(8,128)} %fusion.10, f32[8,3,18,18,258]{4,3,2,1,0:T(8,128)} %select_maximum_fusion, f32[8,3,18,1,256]{4,3,2,1,0:T(1,128)} %copy-done.32, f32[8,3,1,16,256]{4,3,2,1,0:T(8,128)} %copy-done.29, f32[8,3,1,16,256]{4,3,2,1,0:T(8,128)S(1)} %collective-permute-done.64, ...), kind=kLoop, calls=%fused_computation.15 | loop fusion | flops 28311552 | bytes 33128448 | tf_op jit(solution)/shard_map/add | solution.py:127
  681.8 73.7 %all_to_all.36 = f32[8,3,16,16,256]{4,3,2,1,0:T(8,128)S(1)} all-to-all(f32[8,3,16,16,256]{4,3,2,1,0:T(8,128)} %fusion.4), channel_id=1, replica_groups=mesh['space'=16,'cuts'=8] {'cuts'}, dimensions={0} | all-to-all | bytes 12582912 | tf_op jit(solution)/shard_map/all_to_all | solution.py:127
  (313 shorter events, 344.9 us)
Async XLA Ops:
  9.1 95.8 %all-to-all-start = ((f32[1,3,16,128,256]{4,2,1,0,3:T(8,128)}), f32[1,3,16,128,256]{4,2,1,0,3:T(8,128)}, u32[]{:S(2)}, u32[]{:S(2)}) async-start(f32[1,3,16,128,256]{4,2,1,0,3:T(8,128)} %copy.112), calls=%async_computation | async-start | bytes 12582912 | tf_op jit(solution)/shard_map/all_to_all | solution.py:103
  114.5 9.2 %collective-permute-start = (f32[4,1,16,256]{3,2,1,0:T(8,128)S(1)}, f32[4,1,16,256]{3,2,1,0:T(8,128)S(1)}, u32[]{:S(2)}, u32[]{:S(2)}) collective-permute-start(f32[4,1,16,256]{3,2,1,0:T(8,128)S(1)} %get-tuple-element.147), channel_id=1, source_target_pairs={{0,8},{8,16},{16,24},{24,32},{32,40},{40,48},{48,56},{56,64},{64,7... | collective-permute-start | bytes 196616 | tf_op jit(solution)/shard_map/ppermute | solution.py:21
  121.4 9.2 %collective-permute-start.1 = (f32[4,1,16,256]{3,2,1,0:T(8,128)S(1)}, f32[4,1,16,256]{3,2,1,0:T(8,128)S(1)}, u32[]{:S(2)}, u32[]{:S(2)}) collective-permute-start(f32[4,1,16,256]{3,2,1,0:T(8,128)S(1)} %get-tuple-element.148), channel_id=1, source_target_pairs={{8,0},{16,8},{24,16},{32,24},{40,32},{48,40},{56,48},{64,56},{72,6... | collective-permute-start | bytes 196616 | tf_op jit(solution)/shard_map/ppermute | solution.py:22
  145.6 9.2 %collective-permute-start.5 = (f32[4,1,16,256]{3,2,1,0:T(8,128)S(1)}, f32[4,1,16,256]{3,2,1,0:T(8,128)S(1)}, u32[]{:S(2)}, u32[]{:S(2)}) collective-permute-start(f32[4,1,16,256]{3,2,1,0:T(8,128)S(1)} %get-tuple-element.146), channel_id=1, source_target_pairs={{8,0},{16,8},{24,16},{32,24},{40,32},{48,40},{56,48},{64,56},{72,6... | collective-permute-start | bytes 196616 | tf_op jit(solution)/shard_map/ppermute | solution.py:22
  170.8 9.2 %collective-permute-start.9 = (f32[4,1,16,256]{3,2,1,0:T(8,128)S(1)}, f32[4,1,16,256]{3,2,1,0:T(8,128)S(1)}, u32[]{:S(2)}, u32[]{:S(2)}) collective-permute-start(f32[4,1,16,256]{3,2,1,0:T(8,128)S(1)} %get-tuple-element.144), channel_id=1, source_target_pairs={{8,0},{16,8},{24,16},{32,24},{40,32},{48,40},{56,48},{64,56},{72,6... | collective-permute-start | bytes 196616 | tf_op jit(solution)/shard_map/ppermute | solution.py:22
  195.9 9.2 %collective-permute-start.13 = (f32[4,1,16,256]{3,2,1,0:T(8,128)S(1)}, f32[4,1,16,256]{3,2,1,0:T(8,128)S(1)}, u32[]{:S(2)}, u32[]{:S(2)}) collective-permute-start(f32[4,1,16,256]{3,2,1,0:T(8,128)S(1)} %get-tuple-element.142), channel_id=1, source_target_pairs={{8,0},{16,8},{24,16},{32,24},{40,32},{48,40},{56,48},{64,56},{72,6... | collective-permute-start | bytes 196616 | tf_op jit(solution)/shard_map/ppermute | solution.py:22
  221.1 9.2 %collective-permute-start.17 = (f32[4,1,16,256]{3,2,1,0:T(8,128)S(1)}, f32[4,1,16,256]{3,2,1,0:T(8,128)S(1)}, u32[]{:S(2)}, u32[]{:S(2)}) collective-permute-start(f32[4,1,16,256]{3,2,1,0:T(8,128)S(1)} %get-tuple-element.140), channel_id=1, source_target_pairs={{8,0},{16,8},{24,16},{32,24},{40,32},{48,40},{56,48},{64,56},{72,6... | collective-permute-start | bytes 196616 | tf_op jit(solution)/shard_map/ppermute | solution.py:22
  246.2 9.2 %collective-permute-start.21 = (f32[4,1,16,256]{3,2,1,0:T(8,128)S(1)}, f32[4,1,16,256]{3,2,1,0:T(8,128)S(1)}, u32[]{:S(2)}, u32[]{:S(2)}) collective-permute-start(f32[4,1,16,256]{3,2,1,0:T(8,128)S(1)} %get-tuple-element.138), channel_id=1, source_target_pairs={{8,0},{16,8},{24,16},{32,24},{40,32},{48,40},{56,48},{64,56},{72,6... | collective-permute-start | bytes 196616 | tf_op jit(solution)/shard_map/ppermute | solution.py:22
  271.4 9.2 %collective-permute-start.25 = (f32[4,1,16,256]{3,2,1,0:T(8,128)S(1)}, f32[4,1,16,256]{3,2,1,0:T(8,128)S(1)}, u32[]{:S(2)}, u32[]{:S(2)}) collective-permute-start(f32[4,1,16,256]{3,2,1,0:T(8,128)S(1)} %get-tuple-element.136), channel_id=1, source_target_pairs={{8,0},{16,8},{24,16},{32,24},{40,32},{48,40},{56,48},{64,56},{72,6... | collective-permute-start | bytes 196616 | tf_op jit(solution)/shard_map/ppermute | solution.py:22
  293.9 70.8 %collective-permute-start.28 = (f32[4,1,16,256]{3,2,1,0:T(8,128)S(1)}, f32[4,1,16,256]{3,2,1,0:T(8,128)S(1)}, u32[]{:S(2)}, u32[]{:S(2)}) collective-permute-start(f32[4,1,16,256]{3,2,1,0:T(8,128)S(1)} %get-tuple-element.133), channel_id=1, source_target_pairs={{0,8},{8,16},{16,24},{24,32},{32,40},{40,48},{48,56},{56,64},{64,7... | collective-permute-start | bytes 196616 | tf_op jit(solution)/shard_map/ppermute | solution.py:21
  296.9 67.8 %collective-permute-start.29 = (f32[4,1,16,256]{3,2,1,0:T(8,128)S(1)}, f32[4,1,16,256]{3,2,1,0:T(8,128)S(1)}, u32[]{:S(2)}, u32[]{:S(2)}) collective-permute-start(f32[4,1,16,256]{3,2,1,0:T(8,128)S(1)} %get-tuple-element.134), channel_id=1, source_target_pairs={{8,0},{16,8},{24,16},{32,24},{40,32},{48,40},{56,48},{64,56},{72,6... | collective-permute-start | bytes 196616 | tf_op jit(solution)/shard_map/ppermute | solution.py:22
  383.2 8.7 %collective-permute-start.33 = (f32[1,16,256]{2,1,0:T(8,128)S(1)}, f32[1,16,256]{2,1,0:T(8,128)S(1)}, u32[]{:S(2)}, u32[]{:S(2)}) collective-permute-start(f32[1,16,256]{2,1,0:T(8,128)S(1)} %get-tuple-element.176), channel_id=1, source_target_pairs={{8,0},{16,8},{24,16},{32,24},{40,32},{48,40},{56,48},{64,56},{72,6... | collective-permute-start | bytes 49160 | tf_op jit(solution)/shard_map/ppermute | solution.py:22
  410.1 8.7 %collective-permute-start.37 = (f32[1,16,256]{2,1,0:T(8,128)S(1)}, f32[1,16,256]{2,1,0:T(8,128)S(1)}, u32[]{:S(2)}, u32[]{:S(2)}) collective-permute-start(f32[1,16,256]{2,1,0:T(8,128)S(1)} %get-tuple-element.174), channel_id=1, source_target_pairs={{8,0},{16,8},{24,16},{32,24},{40,32},{48,40},{56,48},{64,56},{72,6... | collective-permute-start | bytes 49160 | tf_op jit(solution)/shard_map/ppermute | solution.py:22
  433.4 8.7 %collective-permute-start.41 = (f32[1,16,256]{2,1,0:T(8,128)S(1)}, f32[1,16,256]{2,1,0:T(8,128)S(1)}, u32[]{:S(2)}, u32[]{:S(2)}) collective-permute-start(f32[1,16,256]{2,1,0:T(8,128)S(1)} %get-tuple-element.172), channel_id=1, source_target_pairs={{8,0},{16,8},{24,16},{32,24},{40,32},{48,40},{56,48},{64,56},{72,6... | collective-permute-start | bytes 49160 | tf_op jit(solution)/shard_map/ppermute | solution.py:22
  456.7 8.7 %collective-permute-start.45 = (f32[1,16,256]{2,1,0:T(8,128)S(1)}, f32[1,16,256]{2,1,0:T(8,128)S(1)}, u32[]{:S(2)}, u32[]{:S(2)}) collective-permute-start(f32[1,16,256]{2,1,0:T(8,128)S(1)} %get-tuple-element.170), channel_id=1, source_target_pairs={{8,0},{16,8},{24,16},{32,24},{40,32},{48,40},{56,48},{64,56},{72,6... | collective-permute-start | bytes 49160 | tf_op jit(solution)/shard_map/ppermute | solution.py:22
  480.0 8.7 %collective-permute-start.49 = (f32[1,16,256]{2,1,0:T(8,128)S(1)}, f32[1,16,256]{2,1,0:T(8,128)S(1)}, u32[]{:S(2)}, u32[]{:S(2)}) collective-permute-start(f32[1,16,256]{2,1,0:T(8,128)S(1)} %get-tuple-element.168), channel_id=1, source_target_pairs={{8,0},{16,8},{24,16},{32,24},{40,32},{48,40},{56,48},{64,56},{72,6... | collective-permute-start | bytes 49160 | tf_op jit(solution)/shard_map/ppermute | solution.py:22
  503.3 8.7 %collective-permute-start.53 = (f32[1,16,256]{2,1,0:T(8,128)S(1)}, f32[1,16,256]{2,1,0:T(8,128)S(1)}, u32[]{:S(2)}, u32[]{:S(2)}) collective-permute-start(f32[1,16,256]{2,1,0:T(8,128)S(1)} %get-tuple-element.166), channel_id=1, source_target_pairs={{8,0},{16,8},{24,16},{32,24},{40,32},{48,40},{56,48},{64,56},{72,6... | collective-permute-start | bytes 49160 | tf_op jit(solution)/shard_map/ppermute | solution.py:22
  526.9 8.7 %collective-permute-start.57 = (f32[1,16,256]{2,1,0:T(8,128)S(1)}, f32[1,16,256]{2,1,0:T(8,128)S(1)}, u32[]{:S(2)}, u32[]{:S(2)}) collective-permute-start(f32[1,16,256]{2,1,0:T(8,128)S(1)} %get-tuple-element.164), channel_id=1, source_target_pairs={{8,0},{16,8},{24,16},{32,24},{40,32},{48,40},{56,48},{64,56},{72,6... | collective-permute-start | bytes 49160 | tf_op jit(solution)/shard_map/ppermute | solution.py:22
  551.7 12.7 %collective-permute-start.61 = (f32[8,3,1,16,256]{4,3,2,1,0:T(8,128)S(1)}, f32[8,3,1,16,256]{4,3,2,1,0:T(8,128)S(1)}, u32[]{:S(2)}, u32[]{:S(2)}) collective-permute-start(f32[8,3,1,16,256]{4,3,2,1,0:T(8,128)S(1)} %get-tuple-element.44), channel_id=1, source_target_pairs={{8,0},{16,8},{24,16},{32,24},{40,32},{48,40},{56,48},{64,56},{72,6... | collective-permute-start | bytes 1179656 | tf_op jit(solution)/shard_map/ppermute | solution.py:22
  565.0 9.0 %collective-permute-start.62 = (f32[8,3,18,1,256]{4,3,2,1,0:T(1,128)S(1)}, f32[8,3,18,1,256]{4,3,2,1,0:T(1,128)S(1)}, u32[]{:S(2)}, u32[]{:S(2)}) collective-permute-start(f32[8,3,18,1,256]{4,3,2,1,0:T(1,128)S(1)} %get-tuple-element.39), channel_id=1, source_target_pairs={{0,1},{1,2},{2,3},{3,4},{4,5},{5,6},{6,7},{8,9},{9,10},{10,11},{11... | collective-permute-start | bytes 1327112 | tf_op jit(solution)/shard_map/ppermute | solution.py:21
  568.6 9.4 %collective-permute-start.63 = (f32[8,3,18,1,256]{4,3,2,1,0:T(1,128)S(1)}, f32[8,3,18,1,256]{4,3,2,1,0:T(1,128)S(1)}, u32[]{:S(2)}, u32[]{:S(2)}) collective-permute-start(f32[8,3,18,1,256]{4,3,2,1,0:T(1,128)S(1)} %get-tuple-element.40), channel_id=1, source_target_pairs={{1,0},{2,1},{3,2},{4,3},{5,4},{6,5},{7,6},{9,8},{10,9},{11,10},{12... | collective-permute-start | bytes 1327112 | tf_op jit(solution)/shard_map/ppermute | solution.py:22
  616.4 13.0 %collective-permute-start.65 = (f32[8,3,1,16,256]{4,3,2,1,0:T(8,128)S(1)}, f32[8,3,1,16,256]{4,3,2,1,0:T(8,128)S(1)}, u32[]{:S(2)}, u32[]{:S(2)}) collective-permute-start(f32[8,3,1,16,256]{4,3,2,1,0:T(8,128)S(1)} %get-tuple-element.42), channel_id=1, source_target_pairs={{8,0},{16,8},{24,16},{32,24},{40,32},{48,40},{56,48},{64,56},{72,6... | collective-permute-start | bytes 1179656 | tf_op jit(solution)/shard_map/ppermute | solution.py:22
  633.1 9.0 %collective-permute-start.66 = (f32[8,3,18,1,256]{4,3,2,1,0:T(1,128)S(1)}, f32[8,3,18,1,256]{4,3,2,1,0:T(1,128)S(1)}, u32[]{:S(2)}, u32[]{:S(2)}) collective-permute-start(f32[8,3,18,1,256]{4,3,2,1,0:T(1,128)S(1)} %get-tuple-element.37), channel_id=1, source_target_pairs={{0,1},{1,2},{2,3},{3,4},{4,5},{5,6},{6,7},{8,9},{9,10},{10,11},{11... | collective-permute-start | bytes 1327112 | tf_op jit(solution)/shard_map/ppermute | solution.py:21
  636.7 9.4 %collective-permute-start.67 = (f32[8,3,18,1,256]{4,3,2,1,0:T(1,128)S(1)}, f32[8,3,18,1,256]{4,3,2,1,0:T(1,128)S(1)}, u32[]{:S(2)}, u32[]{:S(2)}) collective-permute-start(f32[8,3,18,1,256]{4,3,2,1,0:T(1,128)S(1)} %get-tuple-element.38), channel_id=1, source_target_pairs={{1,0},{2,1},{3,2},{4,3},{5,4},{6,5},{7,6},{9,8},{10,9},{11,10},{12... | collective-permute-start | bytes 1327112 | tf_op jit(solution)/shard_map/ppermute | solution.py:22
  (83 other events, 580.6 us)
where the time goes:
time: 771 us; the launch traced here: 759 us
  waiting for transfers between devices  227 us (29%)
  starting transfers between devices  194 us (25%)
  other arithmetic  158 us (20%)
  blocking collectives  138 us (18%)
  local copies, waits for them, and re-layouts  38.3 us (5%)
    ppermute x34, waiting for transfers between devices, padded_2(): after = lax.ppermute(initial, axis, down)  170 us
    ppermute x34, starting transfers between devices, padded_2(): before = lax.ppermute(last, axis, up)  119 us
    all_to_all x1, blocking collectives, shards(): lax.all_to_all(tiled + smoothed, 'cuts', split_axis=0, concat_axis=3, til...  73.7 us
    ppermute x34, starting transfers between devices, padded_2(): after = lax.ppermute(initial, axis, down)  69.3 us
    psum x1, blocking collectives, shards(): voxel_total = lax.psum(counts.astype(jnp.float32)[0], ('space', 'cuts'))  64.5 us
    broadcast_in_dim x8, other arithmetic, shards(): joined = jnp.concatenate([intensity[None], tiled[moment]], axis=0)  56.5 us
    all_to_all x1, waiting for transfers between devices, shards(): lax.all_to_all(velocity, 'cuts', split_axis=3, concat_axis=0, tiled=True)  45.2 us
    concatenate x16, other arithmetic, padded_2(): value = jnp.concatenate([before, value, after], axis=dim)  37.3 us
  transfers between devices with their start and end apart: 69, of which 38 were waited for; matrix products, arithmetic and copies ran while one was open for 6% of the time, Pallas kernels for 0%

commit v1 on v0

v1 whole, which is shorter than its diff:
```python
import functools

import jax
import jax.numpy as jnp
from jax import lax
from jax.experimental import pallas as pl
from jax.experimental.pallas import tpu as pltpu
from jax.sharding import PartitionSpec as P

F32 = jnp.float32
NT = 8
STEP = 1.0 / NT
DATA_WEIGHT = 4.0
KAPPA = 0.125
CX, CY, NZ = 16, 16, 256
NY = 128
DEPTH = 4
WX, WY = CX + 2 * DEPTH, CY + 2 * DEPTH
V_SLOTS = ((0, 3, 0), (1, 2, 3), (2, 1, 5))
V_ROWS = 6
VX = CX + 6
VMEM = pltpu.VMEM
ANY = pl.ANY


def whole():
    return pl.BlockSpec(memory_space=VMEM)


def anywhere():
    return pl.BlockSpec(memory_space=ANY)


def scalars():
    return pl.BlockSpec(memory_space=pltpu.SMEM)


def params():
    return pltpu.CompilerParams(vmem_limit_bytes=56 * 1024 * 1024)


def sds(*shape):
    return jax.ShapeDtypeStruct(shape, F32)


def swaps(size, first):
    pairs = []
    for i in range(first, size - 1, 2):
        pairs += [(i, i + 1), (i + 1, i)]
    return pairs


def swap(even, odd, axis):
    size = lax.axis_size(axis)
    return lax.ppermute(even, axis, swaps(size, 0)), lax.ppermute(odd, axis, swaps(size, 1))


def total_of(value):
    for axis in ("cuts", "space"):
        size = lax.axis_size(axis)
        reach = 1
        while reach < size:
            value = value + lax.ppermute(value, axis, [(i, i ^ reach) for i in range(size)])
            reach *= 2
    return value


def rows8():
    return lax.broadcasted_iota(jnp.int32, (8, NZ), 0)


def turn(block, shift):
    shift = shift % 8
    return pltpu.roll(block, shift, 0) if shift else block


def put(total, block, shift, low, high, sub):
    return jnp.where((sub >= low) & (sub < high), turn(block, shift), total)


def pack_edges(slots, tile, sub):
    top = jnp.zeros((8, NZ), F32)
    bottom = top
    for key, k, off in slots:
        low8, high8 = tile(key)
        top = put(top, high8, off + k, off, off + k, sub)
        bottom = put(bottom, low8, off, off, off + k, sub)
    return top, bottom


def halo_block(above, below, k, off, sub):
    block = put(jnp.zeros((8, NZ), F32), above, -off, 0, k, sub)
    return put(block, below, 8 - k - off, 8 - k, 8, sub)


def lane_masks(shape):
    z = lax.broadcasted_iota(jnp.int32, shape, 1)
    return z == 0, z == NZ - 1


def copies(pairs, sem):
    started = [pltpu.make_async_copy(a, b, sem.at[i]) for i, (a, b) in enumerate(pairs)]
    for copy in started:
        copy.start()
    return started


def wait_all(started):
    for copy in started:
        copy.wait()


def fill_velocity(group, info, vt, ra, rb, yc, yd, vw, sem):
    px, py = info[2], info[3]
    pairs = []
    for j in range(4):
        pairs.append((vt.at[4 * group + j], vw.at[j, :, 0:CX, 0:CY]))
    for j, k, off in V_SLOTS:
        to_a = jnp.where(px == 0, CX, WX - k)
        to_b = jnp.where(px == 0, WX - k, CX)
        pairs.append((ra.at[group, :, off : off + k], vw.at[j, :, pl.ds(to_a, k), 0:CY]))
        pairs.append((rb.at[group, :, off : off + k], vw.at[j, :, pl.ds(to_b, k), 0:CY]))
    started = copies(pairs, sem)
    sub = rows8()
    zero_row = jnp.zeros((WY, NZ), F32)
    zero_tile = jnp.zeros((8, NZ), F32)
    for j in range(4):
        k = 3 - j
        for d in range(3):
            for x in range(CX + k, WX - k):
                vw[j, d, x] = zero_row

    def one(i, carry):
        x = jnp.where(i < CX + 3, i, i + 2)
        for d in range(3):
            c, e = yc[d, i], yd[d, i]
            above = jnp.where(py == 0, c, e)
            below = jnp.where(py == 0, e, c)
            for j, k, off in V_SLOTS:
                vw[j, d, x, CY:WY] = halo_block(above, below, k, off, sub)
            vw[3, d, x, CY:WY] = zero_tile
        return carry

    lax.fori_loop(0, CX, one, 0)
    for i in range(CX, VX):
        x = i if i < CX + 3 else i + 2
        for d in range(3):
            c, e = yc[d, i], yd[d, i]
            above = jnp.where(py == 0, c, e)
            below = jnp.where(py == 0, e, c)
            for j, k, off in V_SLOTS:
                if x < CX + k or x >= WX - k:
                    vw[j, d, x, CY:WY] = halo_block(above, below, k, off, sub)
    return started


def fill_image(info, win, yc, yd, image):
    py = info[3]
    sub = rows8()

    def one(i, carry):
        c, e = yc[i], yd[i]
        above = jnp.where(py == 0, c, e)
        below = jnp.where(py == 0, e, c)
        image[i, 0:CY] = win[i]
        image[i + 12, 0:CY] = win[i + 12]
        image[i, CY:WY] = halo_block(above, below, 4, 0, sub)
        image[i + 12, CY:WY] = halo_block(above, below, 4, 4, sub)
        return carry

    lax.fori_loop(0, 12, one, 0)


def advance(src, dst, vw, j, reach):
    first, last = lane_masks((WY, NZ))

    def one(i, carry):
        x = lax.rem(i - reach + WX, WX)
        xm = lax.rem(x + WX - 1, WX)
        xp = lax.rem(x + 1, WX)
        c = src[x]
        v0, v1, v2 = vw[j, 0, x], vw[j, 1, x], vw[j, 2, x]
        flow = v0 * jnp.where(v0 > 0.0, c - src[xm], src[xp] - c)
        flow += v1 * jnp.where(v1 > 0.0, c - pltpu.roll(c, 1, 0), pltpu.roll(c, WY - 1, 0) - c)
        behind = jnp.where(first, 0.0, pltpu.roll(c, 1, 1))
        beyond = jnp.where(last, 0.0, pltpu.roll(c, NZ - 1, 1))
        flow += v2 * jnp.where(v2 > 0.0, c - behind, beyond - c)
        dst[x] = c - STEP * flow
        return carry

    lax.fori_loop(0, CX + 2 * reach, one, 0)


def scatter(src, dst, vw, j, reach):
    first, last = lane_masks((WY, NZ))

    def one(i, carry):
        x = lax.rem(i - reach + WX, WX)
        xm = lax.rem(x + WX - 1, WX)
        xp = lax.rem(x + 1, WX)
        c = src[x]
        v0, v1, v2 = vw[j, 0, x], vw[j, 1, x], vw[j, 2, x]
        change = (jnp.abs(v0) + jnp.abs(v1) + jnp.abs(v2)) * c
        change -= jnp.maximum(vw[j, 0, xp], 0.0) * src[xp]
        change += jnp.minimum(vw[j, 0, xm], 0.0) * src[xm]
        change -= pltpu.roll(jnp.maximum(v1, 0.0) * c, WY - 1, 0)
        change += pltpu.roll(jnp.minimum(v1, 0.0) * c, 1, 0)
        change -= jnp.where(last, 0.0, pltpu.roll(jnp.maximum(v2, 0.0) * c, NZ - 1, 1))
        change += jnp.where(first, 0.0, pltpu.roll(jnp.minimum(v2, 0.0) * c, 1, 1))
        dst[x] = c - STEP * change
        return carry

    lax.fori_loop(0, CX + 2 * reach, one, 0)


def clear_halo(ref, x_rows=True):
    zero_row = jnp.zeros((WY, NZ), F32)
    for x in range(CX, WX):
        ref[x] = zero_row


def repack(velocity):
    def kernel(src, dst, sem):
        pairs = []
        for c in range(NY // CY):
            for d in range(3):
                pairs.append((src.at[0, d, :, c * CY : (c + 1) * CY], dst.at[c, d]))
        wait_all(copies(pairs, sem))

    return pl.pallas_call(
        kernel,
        out_shape=sds(NY // CY, 3, CX, CY, NZ),
        in_specs=[anywhere()],
        out_specs=anywhere(),
        scratch_shapes=[pltpu.SemaphoreType.DMA((24,))],
        compiler_params=params(),
    )(velocity)


def template(info, table, atlas, labels):
    def kernel(info, table, atlas, labels, tmpl, ea, eb):
        def one(x, carry):
            lab = labels[x]
            value = jnp.zeros((CY, NZ), F32)
            for l in range(64):
                value = jnp.where(lab == l, table[l], value)
            tmpl[x] = atlas[x] + value
            return carry

        lax.fori_loop(0, CX, one, 0)
        px = info[2]
        ea[...] = tmpl[pl.ds(jnp.where(px == 0, CX - DEPTH, 0), DEPTH)]
        eb[...] = tmpl[pl.ds(jnp.where(px == 0, 0, CX - DEPTH), DEPTH)]

    return pl.pallas_call(
        kernel,
        out_shape=[sds(CX, CY, NZ), sds(DEPTH, CY, NZ), sds(DEPTH, CY, NZ)],
        in_specs=[scalars(), scalars(), whole(), whole()],
        out_specs=[whole()] * 3,
        compiler_params=params(),
    )(info, table, atlas, labels)


def image_edges(info, tile, ra, rb):
    def kernel(info, tile, ra, rb, win, ec, ed):
        px, py = info[2], info[3]
        win[0:CX] = tile[...]
        win[pl.ds(jnp.where(px == 0, CX, WX - DEPTH), DEPTH)] = ra[...]
        win[pl.ds(jnp.where(px == 0, WX - DEPTH, CX), DEPTH)] = rb[...]
        sub = rows8()

        def one(i, carry):
            def tile_of(key):
                return win[i + key, 0:8], win[i + key, 8:16]

            top, bottom = pack_edges(((0, 4, 0), (12, 4, 4)), tile_of, sub)
            ec[i] = jnp.where(py == 0, top, bottom)
            ed[i] = jnp.where(py == 0, bottom, top)
            return carry

        lax.fori_loop(0, 12, one, 0)

    return pl.pallas_call(
        kernel,
        out_shape=[sds(WX, CY, NZ), sds(12, 8, NZ), sds(12, 8, NZ)],
        in_specs=[scalars()] + [whole()] * 3,
        out_specs=[whole()] * 3,
        compiler_params=params(),
    )(info, tile, ra, rb)


def velocity_faces(info, vt):
    def kernel(info, vt, ea, eb, sem):
        px = info[2]
        pairs = []
        for g in range(2):
            for j, k, off in V_SLOTS:
                top = jnp.where(px == 0, CX - k, 0)
                bottom = jnp.where(px == 0, 0, CX - k)
                pairs.append((vt.at[4 * g + j, :, pl.ds(top, k)], ea.at[g, :, off : off + k]))
                pairs.append((vt.at[4 * g + j, :, pl.ds(bottom, k)], eb.at[g, :, off : off + k]))
        wait_all(copies(pairs, sem))

    return pl.pallas_call(
        kernel,
        out_shape=[sds(2, 3, V_ROWS, CY, NZ)] * 2,
        in_specs=[scalars(), anywhere()],
        out_specs=[anywhere()] * 2,
        scratch_shapes=[pltpu.SemaphoreType.DMA((12,))],
        compiler_params=params(),
    )(info, vt)


def velocity_edges(info, vt, ra, rb, group):
    def kernel(info, vt, ra, rb, ec, ed):
        px, py = info[2], info[3]
        sub = rows8()

        def emit(i, slots, tile_of):
            top, bottom = pack_edges(slots, tile_of, sub)
            ec[0, i] = jnp.where(py == 0, top, bottom)
            ed[0, i] = jnp.where(py == 0, bottom, top)

        def one(x, carry):
            emit(x, V_SLOTS, lambda j: (vt[j, 0, x, 0:8], vt[j, 0, x, 8:16]))
            return carry

        lax.fori_loop(0, CX, one, 0)
        for i in range(3):
            up, down = [], []
            for j, k, off in V_SLOTS:
                if i < k:
                    up.append((j, k, off))
                if i >= 3 - k:
                    down.append((j, k, off))

            def tile_up(j):
                row = V_SLOTS[j][2] + i
                a, b = ra[0, 0, row], rb[0, 0, row]
                value = jnp.where(px == 0, a, b)
                return value[0:8], value[8:16]

            def tile_down(j):
                row = V_SLOTS[j][2] + i - (3 - V_SLOTS[j][1])
                a, b = ra[0, 0, row], rb[0, 0, row]
                value = jnp.where(px == 0, b, a)
                return value[0:8], value[8:16]

            emit(CX + i, up, tile_up)
            emit(CX + 3 + i, down, tile_down)

    return pl.pallas_call(
        kernel,
        grid=(3,),
        out_shape=[sds(3, VX, 8, NZ)] * 2,
        in_specs=[
            scalars(),
            pl.BlockSpec((4, 1, CX, CY, NZ), lambda d: (group, d, 0, 0, 0)),
            pl.BlockSpec((1, 1, V_ROWS, CY, NZ), lambda d: (group, d, 0, 0, 0)),
            pl.BlockSpec((1, 1, V_ROWS, CY, NZ), lambda d: (group, d, 0, 0, 0)),
        ],
        out_specs=[pl.BlockSpec((1, VX, 8, NZ), lambda d: (d, 0, 0, 0))] * 2,
        compiler_params=params(),
    )(info, vt, ra, rb)


def forward_first(info, win, ic, idd, vt, ra, rb, yc, yd):
    def kernel(info, win, ic, idd, vt, ra, rb, yc, yd, states, ea, eb, i4, vw, image, sem, osem):
        started = fill_velocity(0, info, vt, ra, rb, yc, yd, vw, sem)
        fill_image(info, win, ic, idd, image.at[0])
        wait_all(started)
        out = []
        for j in range(4):
            advance(image.at[j], image.at[j + 1], vw, j, 3 - j)
            out.append(pltpu.make_async_copy(image.at[j, 0:CX, 0:CY], states.at[j], osem.at[j]))
            out[-1].start()
        px = info[2]
        last = image.at[4]
        i4[...] = last[0:CX, 0:CY]
        ea[...] = last[pl.ds(jnp.where(px == 0, CX - DEPTH, 0), DEPTH), 0:CY]
        eb[...] = last[pl.ds(jnp.where(px == 0, 0, CX - DEPTH), DEPTH), 0:CY]
        wait_all(out)

    return pl.pallas_call(
        kernel,
        out_shape=[sds(NT, CX, CY, NZ), sds(DEPTH, CY, NZ), sds(DEPTH, CY, NZ), sds(CX, CY, NZ)],
        in_specs=[scalars()] + [whole()] * 3 + [anywhere()] * 3 + [whole()] * 2,
        out_specs=[anywhere()] + [whole()] * 3,
        scratch_shapes=[
            VMEM((4, 3, WX, WY, NZ), F32),
            VMEM((5, WX, WY, NZ), F32),
            pltpu.SemaphoreType.DMA((10,)),
            pltpu.SemaphoreType.DMA((4,)),
        ],
        compiler_params=params(),
    )(info, win, ic, idd, vt, ra, rb, yc, yd)


def send_rows(info, widths, source, ea, eb):
    px = info[2]
    off = 0
    for n, k in enumerate(widths):
        top = jnp.where(px == 0, CX, WX - k)
        bottom = jnp.where(px == 0, WX - k, CX)
        ea[off : off + k] = source(n)[pl.ds(top, k)]
        eb[off : off + k] = source(n)[pl.ds(bottom, k)]
        off += k


MID_WIDTHS = (4, 3, 2, 1)
MID_SLOTS = ((0, 4, 0), (1, 3, 4), (3, 1, 7))
END_WIDTHS = (3, 2, 1)
END_SLOTS = ((0, 3, 0), (1, 2, 3), (2, 1, 5), (3, 2, 6))


def forward_second(info, win, ic, idd, target, vt, ra, rb, yc, yd, states):
    def kernel(info, win, ic, idd, target, vt, ra, rb, yc, yd, states_in, states, costates, lw, ea, eb, vw, image, lam, sem, osem):
        started = fill_velocity(1, info, vt, ra, rb, yc, yd, vw, sem)
        fill_image(info, win, ic, idd, image.at[0])
        for n in range(4):
            clear_halo(lam.at[n])
        wait_all(started)
        out = []
        for j in range(4):
            advance(image.at[j], image.at[j + 1], vw, j, 3 - j)
            out.append(pltpu.make_async_copy(image.at[j, 0:CX, 0:CY], states.at[4 + j], osem.at[j]))
            out[-1].start()
        count = info[4]
        inside = lax.broadcasted_iota(jnp.int32, (CY, NZ), 0) * NZ + lax.broadcasted_iota(jnp.int32, (CY, NZ), 1)
        zero = jnp.zeros((8, NZ), F32)

        def one(x, carry):
            value = image[4, x, 0:CY] - target[x]
            lam[0, x, 0:CY] = jnp.where(inside + x * (CY * NZ) < count, value, 0.0)
            lam[0, x, CY:WY] = zero
            return carry

        lax.fori_loop(0, CX, one, 0)
        out.append(pltpu.make_async_copy(lam.at[0, 0:CX, 0:CY], costates.at[7], osem.at[4]))
        out[-1].start()
        for n in range(4):
            scatter(lam.at[n], lam.at[n + 1], vw, 3 - n, n + 1)
        for n in range(4):
            lw[n] = lam[4 - n, 0:CX]
        send_rows(info, MID_WIDTHS, lambda n: lam.at[4 - n], ea, eb)
        wait_all(out)

    return pl.pallas_call(
        kernel,
        out_shape=[
            sds(NT, CX, CY, NZ),
            sds(NT, CX, CY, NZ),
            sds(4, CX, WY, NZ),
            sds(10, WY, NZ),
            sds(10, WY, NZ),
        ],
        in_specs=[scalars()] + [whole()] * 4 + [anywhere()] * 3 + [whole()] * 2 + [anywhere()],
        out_specs=[anywhere()] * 2 + [whole()] * 3,
        scratch_shapes=[
            VMEM((4, 3, WX, WY, NZ), F32),
            VMEM((5, WX, WY, NZ), F32),
            VMEM((5, WX, WY, NZ), F32),
            pltpu.SemaphoreType.DMA((10,)),
            pltpu.SemaphoreType.DMA((5,)),
        ],
        input_output_aliases={10: 0},
        compiler_params=params(),
    )(info, win, ic, idd, target, vt, ra, rb, yc, yd, states)


def costate_edges(info, lw, ra, rb, widths, slots):
    def kernel(info, lw_in, ra, rb, lw, ec, ed):
        px, py = info[2], info[3]
        lw[...] = lw_in[...]
        off = 0
        for n, k in enumerate(widths):
            for i in range(k):
                to_a = jnp.where(px == 0, CX - k, 0) + i
                to_b = jnp.where(px == 0, 0, CX - k) + i
                lw[n, to_a] = lw[n, to_a] + ra[off + i]
                lw[n, to_b] = lw[n, to_b] + rb[off + i]
            off += k
        sub = rows8()

        def one(x, carry):
            top = jnp.zeros((8, NZ), F32)
            bottom = top
            for n, k, off in slots:
                block = lw[n, x, CY:WY]
                top = put(top, block, off, off, off + k, sub)
                bottom = put(bottom, block, off + k, off, off + k, sub)
            ec[x] = jnp.where(py == 0, top, bottom)
            ed[x] = jnp.where(py == 0, bottom, top)
            return carry

        lax.fori_loop(0, CX, one, 0)

    return pl.pallas_call(
        kernel,
        out_shape=[sds(4, CX, WY, NZ), sds(CX, 8, NZ), sds(CX, 8, NZ)],
        in_specs=[scalars()] + [whole()] * 3,
        out_specs=[whole()] * 3,
        compiler_params=params(),
    )(info, lw, ra, rb)


def take(c, e, py, k, off, sub):
    below = jnp.where(py == 0, e, c)
    above = jnp.where(py == 0, c, e)
    zero = jnp.zeros((8, NZ), F32)
    return put(zero, below, -off, 0, k, sub), put(zero, above, 8 - k - off, 8 - k, 8, sub)


def backward_second(info, lw, lc, ld, vt, ra, rb, yc, yd, costates):
    def kernel(info, lw, lc, ld, vt, ra, rb, yc, yd, costates_in, costates, lw2, ea, eb, vw, lam, done, sem, osem):
        started = fill_velocity(0, info, vt, ra, rb, yc, yd, vw, sem)
        for n in range(3):
            clear_halo(lam.at[n])
        py = info[3]
        sub = rows8()
        zero = jnp.zeros((8, NZ), F32)

        def one(x, carry):
            c, e = lc[x], ld[x]
            for n, k, off in MID_SLOTS:
                low, high = take(c, e, py, k, off, sub)
                low, high = lw[n, x, 0:8] + low, lw[n, x, 8:16] + high
                if n == 0:
                    lam[0, x, 0:8] = low
                    lam[0, x, 8:16] = high
                    lam[0, x, CY:WY] = zero
                else:
                    done[(n - 1) // 2, x, 0:8] = low
                    done[(n - 1) // 2, x, 8:16] = high
            return carry

        lax.fori_loop(0, CX, one, 0)
        out = [
            pltpu.make_async_copy(lam.at[0, 0:CX, 0:CY], costates.at[3], osem.at[0]),
            pltpu.make_async_copy(done.at[0], costates.at[4], osem.at[1]),
            pltpu.make_async_copy(done.at[1], costates.at[6], osem.at[2]),
        ]
        for copy in out:
            copy.start()
        wait_all(started)
        for n in range(3):
            scatter(lam.at[n], lam.at[n + 1], vw, 3 - n, n + 1)
        for n in range(3):
            lw2[n] = lam[3 - n, 0:CX]
        lw2[3] = lw[2]
        send_rows(info, END_WIDTHS, lambda n: lam.at[3 - n], ea, eb)
        wait_all(out)

    return pl.pallas_call(
        kernel,
        out_shape=[sds(NT, CX, CY, NZ), sds(4, CX, WY, NZ), sds(6, WY, NZ), sds(6, WY, NZ)],
        in_specs=[scalars()] + [whole()] * 3 + [anywhere()] * 3 + [whole()] * 2 + [anywhere()],
        out_specs=[anywhere()] + [whole()] * 3,
        scratch_shapes=[
            VMEM((4, 3, WX, WY, NZ), F32),
            VMEM((4, WX, WY, NZ), F32),
            VMEM((2, CX, CY, NZ), F32),
            pltpu.SemaphoreType.DMA((10,)),
            pltpu.SemaphoreType.DMA((3,)),
        ],
        input_output_aliases={9: 0},
        compiler_params=params(),
    )(info, lw, lc, ld, vt, ra, rb, yc, yd, costates)


def costate_finish(info, lw, lc, ld, costates):
    def kernel(info, lw, lc, ld, costates_in, costates, done, sem):
        py = info[3]
        sub = rows8()

        def one(x, carry):
            c, e = lc[x], ld[x]
            for n, k, off in END_SLOTS:
                low, high = take(c, e, py, k, off, sub)
                done[n, x, 0:8] = lw[n, x, 0:8] + low
                done[n, x, 8:16] = lw[n, x, 8:16] + high
            return carry

        lax.fori_loop(0, CX, one, 0)
        wait_all(copies([(done.at[n], costates.at[m]) for n, m in enumerate((0, 1, 2, 5))], sem))

    return pl.pallas_call(
        kernel,
        out_shape=sds(NT, CX, CY, NZ),
        in_specs=[scalars()] + [whole()] * 3 + [anywhere()],
        out_specs=anywhere(),
        scratch_shapes=[VMEM((4, CX, CY, NZ), F32), pltpu.SemaphoreType.DMA((4,))],
        input_output_aliases={4: 0},
        compiler_params=params(),
    )(info, lw, lc, ld, costates)


def finish(info, weight, velocity, va, vb, image, ia, ib, costate, la, lb):
    def kernel(info, weight, vel, va, vb, image, ia, ib, costate, la, lb, out, islab, lslab, grad, soft, sem):
        d = pl.program_id(0)
        px = info[2]
        coef = weight[0]

        @pl.when(d == 0)
        def _():
            pairs = []
            i_a, i_b = jnp.where(px == 0, CX + 3, 0), jnp.where(px == 0, 0, CX + 3)
            l_a, l_b = jnp.where(px == 0, CX + 2, 0), jnp.where(px == 0, 0, CX + 2)
            for c in range(NY // CY):
                y = slice(c * CY, (c + 1) * CY)
                pairs += [
                    (image.at[c], islab.at[3 : CX + 3, y]),
                    (ia.at[c], islab.at[pl.ds(i_a, 3), y]),
                    (ib.at[c], islab.at[pl.ds(i_b, 3), y]),
                    (costate.at[c], lslab.at[2 : CX + 2, y]),
                    (la.at[c], lslab.at[pl.ds(l_a, 2), y]),
                    (lb.at[c], lslab.at[pl.ds(l_b, 2), y]),
                ]
            wait_all(copies(pairs, sem))

        first, last = lane_masks((NY, NZ))
        y = lax.broadcasted_iota(jnp.int32, (NY, NZ), 0)
        bottom, top = y == 0, y == NY - 1

        def row(r, v, direction):
            c = islab[r + 1]
            if direction == 0:
                behind, beyond = islab[r], islab[r + 2]
            elif direction == 1:
                behind = jnp.where(bottom, 0.0, pltpu.roll(c, 1, 0))
                beyond = jnp.where(top, 0.0, pltpu.roll(c, NY - 1, 0))
            else:
                behind = jnp.where(first, 0.0, pltpu.roll(c, 1, 1))
                beyond = jnp.where(last, 0.0, pltpu.roll(c, NZ - 1, 1))
            slope = jnp.where(v > 0.0, c - behind, beyond - c)
            grad[r] = (coef * lslab[r]) * slope

        for direction in range(3):

            @pl.when(d == direction)
            def _(direction=direction):
                for i in range(2):
                    row(i, jnp.where(px == 0, vb[0, i], va[0, i]), direction)
                    row(CX + 2 + i, jnp.where(px == 0, va[0, i], vb[0, i]), direction)

                def one(x, carry):
                    row(x + 2, vel[0, 0, x], direction)
                    return carry

                lax.fori_loop(0, CX, one, 0)

        def sweep(ref, r):
            c = ref[r]
            near = ref[r - 1] + ref[r + 1]
            near += jnp.where(bottom, 0.0, pltpu.roll(c, 1, 0)) + jnp.where(top, 0.0, pltpu.roll(c, NY - 1, 0))
            near += jnp.where(first, 0.0, pltpu.roll(c, 1, 1)) + jnp.where(last, 0.0, pltpu.roll(c, NZ - 1, 1))
            return c + KAPPA * (near - 6.0 * c)

        def once(r, carry):
            soft[r] = sweep(grad, r + 1)
            return carry

        lax.fori_loop(0, CX + 2, once, 0)
        zero = jnp.zeros((NY, NZ), F32)

        @pl.when(info[0] == 0)
        def _():
            soft[0] = zero

        @pl.when(info[0] == info[5] - 1)
        def _():
            soft[CX + 1] = zero

        def twice(x, carry):
            out[0, 0, x] = vel[0, 0, x] + sweep(soft, x + 1)
            return carry

        lax.fori_loop(0, CX, twice, 0)

    face = pl.BlockSpec((1, 2, NY, NZ), lambda d: (d, 0, 0, 0))
    slab = pl.BlockSpec((1, 1, CX, NY, NZ), lambda d: (0, d, 0, 0, 0))
    return pl.pallas_call(
        kernel,
        grid=(3,),
        out_shape=sds(1, 3, CX, NY, NZ),
        in_specs=[scalars(), scalars(), slab, face, face] + [anywhere()] * 6,
        out_specs=slab,
        scratch_shapes=[
            VMEM((CX + 6, NY, NZ), F32),
            VMEM((CX + 4, NY, NZ), F32),
            VMEM((CX + 4, NY, NZ), F32),
            VMEM((CX + 2, NY, NZ), F32),
            pltpu.SemaphoreType.DMA((48,)),
        ],
        compiler_params=params(),
    )(info, weight, velocity, va, vb, image, ia, ib, costate, la, lb)


def edge_rows(value, dim, k, px):
    length = value.shape[dim]
    high = lax.slice_in_dim(value, length - k, length, axis=dim)
    low = lax.slice_in_dim(value, 0, k, axis=dim)
    return jnp.where(px == 0, high, low), jnp.where(px == 0, low, high)


def shards(velocity, atlas_image, target, labels, label_table, counts):
    s, c = lax.axis_index("space"), lax.axis_index("cuts")
    px, py = s % 2, c % 2
    info = jnp.stack([s, c, px, py, counts[0], jnp.int32(lax.axis_size("space")), s, s]).astype(jnp.int32)
    tiled = lax.all_to_all(repack(velocity), "cuts", split_axis=0, concat_axis=0, tiled=True)

    total = total_of(jnp.broadcast_to(counts.astype(F32)[:, None], (1, 128)))[0, 0]
    cells = CX * CY * NZ * lax.axis_size("space") * lax.axis_size("cuts")
    weight = jnp.reshape(-STEP * DATA_WEIGHT * (cells / total), (1,)).astype(F32)
    tile, ea, eb = template(info, label_table, atlas_image, labels)
    win, ec, ed = image_edges(info, tile, *swap(ea, eb, "space"))
    ic, idd = swap(ec, ed, "cuts")
    ova, ovb = edge_rows(velocity[0], 1, 2, px)
    ova, ovb = swap(ova, ovb, "space")

    fa, fb = velocity_faces(info, tiled)
    fa, fb = swap(fa, fb, "space")
    y0 = swap(*velocity_edges(info, tiled, fa, fb, 0), "cuts")
    y1 = swap(*velocity_edges(info, tiled, fa, fb, 1), "cuts")

    states, ea, eb, i4 = forward_first(info, win, ic, idd, tiled, fa, fb, *y0)
    win, ec, ed = image_edges(info, i4, *swap(ea, eb, "space"))
    ic, idd = swap(ec, ed, "cuts")
    states, costates, lw, ea, eb = forward_second(info, win, ic, idd, target, tiled, fa, fb, *y1, states)
    image = lax.all_to_all(states, "cuts", split_axis=0, concat_axis=0, tiled=True)
    lw, ec, ed = costate_edges(info, lw, *swap(ea, eb, "space"), MID_WIDTHS, MID_SLOTS)
    ec, ed = swap(ec, ed, "cuts")
    costates, lw, ea, eb = backward_second(info, lw, ec, ed, tiled, fa, fb, *y0, costates)
    lw, ec, ed = costate_edges(info, lw, *swap(ea, eb, "space"), END_WIDTHS, END_SLOTS)
    ec, ed = swap(ec, ed, "cuts")
    costates = costate_finish(info, lw, ec, ed, costates)
    costate = lax.all_to_all(costates, "cuts", split_axis=0, concat_axis=0, tiled=True)

    ia, ib = swap(*edge_rows(image, 1, 3, px), "space")
    la, lb = swap(*edge_rows(costate, 1, 2, px), "space")
    return finish(info, weight, velocity, ova, ovb, image, ia, ib, costate, la, lb)


def solution(mesh):
    in_specs = (
        P("cuts", None, "space", None, None),
        P("space", "cuts", None),
        P("space", "cuts", None),
        P("space", "cuts", None),
        P(),
        P(("space", "cuts")),
    )
    out_specs = P("cuts", None, "space", None, None)
    return jax.shard_map(shards, mesh=mesh, in_specs=in_specs, out_specs=out_specs, check_vma=False)
```

time: 771 us -> 612 us (0.79)
  the two profiles are of different devices: /device:TPU:15 before, /device:TPU:93 now
where the time goes in v1:
time: 612 us; the launch traced here: 604 us
  Pallas kernels  324 us (53%)
  waiting for transfers between devices  184 us (30%)
  starting transfers between devices  83.4 us (14%)
  local copies, waits for them, and re-layouts  7.76 us (1%)
    pallas_call x1, Pallas kernels, repack(): pl.pallas_call(kernel, out_shape=sds(NY // CY, 3, CX, CY, NZ), in_specs=[...  192 us
    all_to_all x1, waiting for transfers between devices, shards(): lax.all_to_all(repack(velocity), 'cuts', split_axis=0, concat_axis=0, til...  90.6 us
    ppermute x14, waiting for transfers between devices, swap(): lax.ppermute(odd, axis, swaps(size, 1))  47.2 us
    ppermute x14, starting transfers between devices, swap(): lax.ppermute(odd, axis, swaps(size, 1))  38.7 us
    pallas_call x1, Pallas kernels, velocity_faces(): pl.pallas_call(kernel, out_shape=[sds(2, 3, V_ROWS, CY, NZ)] * 2, in_spec...  37.6 us
    pallas_call x1, Pallas kernels, finish(): pl.pallas_call(kernel, grid=(3,), out_shape=sds(1, 3, CX, NY, NZ), in_spe...  27 us
    ppermute x7, waiting for transfers between devices, total_of(): lax.ppermute(value, axis, [(i, i ^ reach) for i in range(size)])  25.9 us
    ppermute x14, waiting for transfers between devices, swap(): lax.ppermute(even, axis, swaps(size, 0))  20.1 us
  transfers between devices with their start and end apart: 38, of which 23 were waited for; matrix products, arithmetic and copies ran while one was open for 1% of the time, Pallas kernels for 7%

profile of v1, /device:TPU:93, one launch (start us, length us, event | category | flops | bytes accessed | tf_op | source)
XLA Modules:
  0.0 604.3 jit_solution(2893809835297340939)
XLA Ops:
  0.0 191.9 %shard_map.66 = f32[8,3,16,16,256]{4,3,2,1,0:T(8,128)} custom-call(f32[1,3,16,128,256]{4,3,2,1,0:T(8,128)} %vel.1), custom_call_target="tpu_custom_call" | custom-call | tf_op jit(solution)/shard_map/pallas_call | solution.py:230
  191.9 5.2 all-to-all-start
  198.4 90.6 %all-to-all-done.vt = f32[8,3,16,16,256]{4,3,2,1,0:T(8,128)} async-done(((f32[8,3,16,16,256]{4,3,2,1,0:T(8,128)}), f32[8,3,16,16,256]{4,3,2,1,0:T(8,128)}, u32[]{:S(2)}, u32[]{:S(2)}) %all-to-all-start) | async-done | bytes 6291488 | tf_op jit(solution)/shard_map/all_to_all | solution.py:710
  289.0 37.6 %shard_map.67 = (f32[2,3,6,16,256]{4,3,2,1,0:T(8,128)}, f32[2,3,6,16,256]{4,3,2,1,0:T(8,128)}) custom-call(s32[8]{0:T(128)} %stack.21.info, f32[8,3,16,16,256]{4,3,2,1,0:T(8,128)} %all-to-all-done.vt), custom_call_target="tpu_custom_call" | custom-call | tf_op jit(solution)/shard_map/pallas_call | solution.py:304
  331.4 8.6 %collective-permute-done.14.rb = f32[2,3,6,16,256]{4,3,2,1,0:T(8,128)S(1)} collective-permute-done((f32[2,3,6,16,256]{4,3,2,1,0:T(8,128)}, f32[2,3,6,16,256]{4,3,2,1,0:T(8,128)S(1)}, u32[]{:S(2)}, u32[]{:S(2)}) %collective-permute-start.14) | collective-permute-done | bytes 589856 | tf_op jit(solution)/shard_map/ppermute | solution.py:55
  347.0 3.9 shard_map.71
  352.0 4.9 collective-permute-start.22
  370.8 4.2 collective-permute-done.11.ic
  377.2 5.4 collective-permute-done.12.idd
  383.7 12.0 %shard_map.69 = (f32[8,16,16,256]{3,2,1,0:T(8,128)}, f32[4,16,256]{2,1,0:T(8,128)}, f32[4,16,256]{2,1,0:T(8,128)}, f32[16,16,256]{2,1,0:T(8,128)}) custom-call(s32[8]{0:T(128)} %stack.21.info, f32[24,16,256]{2,1,0:T(8,128)} %get-tuple-element.42.win, f32[12,8,256]{2,1,0:T(8,128)} %copy-done.22, f32[12,8,256]{2,1,0:T(8,128)} %copy-done.23, ...), custom_call_target="tpu_custom_call" | custom-call | tf_op jit(solution)/shard_map/pallas_call | solution.py:384
  411.1 4.0 collective-permute-done.20.idd
  415.7 20.0 %shard_map.72 = (f32[8,16,16,256]{3,2,1,0:T(8,128)}, f32[8,16,16,256]{3,2,1,0:T(8,128)}, f32[4,16,24,256]{3,2,1,0:T(8,128)}, f32[10,24,256]{2,1,0:T(8,128)}, f32[10,24,256]{2,1,0:T(8,128)}) custom-call(s32[8]{0:T(128)} %stack.21.info, f32[24,16,256]{2,1,0:T(8,128)} %get-tuple-element.52.win, ...), custom_call_target="tpu_custom_call", output_to_operand_aliasing={{0}: (10, {})} | custom-call | tf_op jit(solution)/shard_map/pallas_call | solution.py:448
  435.8 4.1 all-to-all-start.1
  443.5 5.6 collective-permute-done.26.rb
  457.2 9.7 %collective-permute-done.27.lc = f32[16,8,256]{2,1,0:T(8,128)S(1)} collective-permute-done((f32[16,8,256]{2,1,0:T(8,128)}, f32[16,8,256]{2,1,0:T(8,128)S(1)}, u32[]{:S(2)}, u32[]{:S(2)}) %collective-permute-start.27) | collective-permute-done | bytes 131104 | tf_op jit(solution)/shard_map/ppermute | solution.py:55
  466.9 4.3 collective-permute-done.28.ld
  471.8 11.2 %shard_map.74 = (f32[8,16,16,256]{3,2,1,0:T(8,128)}, f32[4,16,24,256]{3,2,1,0:T(8,128)}, f32[6,24,256]{2,1,0:T(8,128)}, f32[6,24,256]{2,1,0:T(8,128)}) custom-call(s32[8]{0:T(128)} %stack.21.info, f32[4,16,24,256]{3,2,1,0:T(8,128)} %get-tuple-element.62.lw, f32[16,8,256]{2,1,0:T(8,128)} %copy-done.16, ...), custom_call_target="tpu_custom_call", output_to_operand_aliasing={{0}: (9, {})} | custom-call | tf_op jit(solution)/shard_map/pallas_call | solution.py:554
  485.5 4.7 collective-permute-done.30.rb
  499.3 4.0 collective-permute-done.32.ld
  506.7 4.3 all-to-all-start.2
  515.5 19.3 %collective-permute-done = f32[1,128]{1,0:T(1,128)S(1)} collective-permute-done((f32[1,128]{1,0:T(1,128)S(1)}, f32[1,128]{1,0:T(1,128)S(1)}, u32[]{:S(2)}, u32[]{:S(2)}) %collective-permute-start) | collective-permute-done | bytes 544 | tf_op jit(solution)/shard_map/ppermute | solution.py:63
  541.1 4.3 collective-permute-start.3
  549.1 8.8 %collective-permute-start.5 = (f32[1,128]{1,0:T(1,128)S(1)}, f32[1,128]{1,0:T(1,128)S(1)}, u32[]{:S(2)}, u32[]{:S(2)}) collective-permute-start(f32[1,128]{1,0:T(1,128)S(1)} %add.34), channel_id=1, source_target_pairs={{0,32},{8,40},{16,48},{24,56},{32,0},{40,8},{48,16},{56,24},{64,96... | collective-permute-start | bytes 1544 | tf_op jit(solution)/shard_map/ppermute | solution.py:63
  577.3 27.0 %shard_map.77 = f32[1,3,16,128,256]{4,3,2,1,0:T(8,128)} custom-call(s32[8]{0:T(128)} %stack.21.info, f32[1]{0:T(128)} %bitcast.5.weight, f32[1,3,16,128,256]{4,3,2,1,0:T(8,128)} %vel.1, f32[3,2,128,256]{3,2,1,0:T(8,128)} %copy-done.5, f32[3,2,128,256]{3,2,1,0:T(8,128)} %collective-permute-done.8.vb, f32[8,16,16,256]{3,2,1,0:T(8,128)} %copy-done.2, ...), custom_call_target="tpu_custom_call" | custom-call | tf_op jit(solution)/shard_map/pallas_call | solution.py:682
  (138 shorter events, 107.3 us)
Async XLA Ops:
  191.9 97.1 %all-to-all-start = ((f32[8,3,16,16,256]{4,3,2,1,0:T(8,128)}), f32[8,3,16,16,256]{4,3,2,1,0:T(8,128)}, u32[]{:S(2)}, u32[]{:S(2)}) async-start(f32[8,3,16,16,256]{4,3,2,1,0:T(8,128)} %shard_map.66), calls=%async_computation | async-start | bytes 12582912 | tf_op jit(solution)/shard_map/all_to_all | solution.py:710
  328.6 11.4 %collective-permute-start.14 = (f32[2,3,6,16,256]{4,3,2,1,0:T(8,128)}, f32[2,3,6,16,256]{4,3,2,1,0:T(8,128)S(1)}, u32[]{:S(2)}, u32[]{:S(2)}) collective-permute-start(f32[2,3,6,16,256]{4,3,2,1,0:T(8,128)} %get-tuple-element.46), channel_id=1, source_target_pairs={{8,16},{16,8},{24,32},{32,24},{40,48},{48,40},{56,64},{64,56},{72,... | collective-permute-start | bytes 1769480 | tf_op jit(solution)/shard_map/ppermute | solution.py:55
  344.7 38.0 %collective-permute-start.15 = (f32[3,22,8,256]{3,2,1,0:T(8,128)}, f32[3,22,8,256]{3,2,1,0:T(8,128)S(1)}, u32[]{:S(2)}, u32[]{:S(2)}) collective-permute-start(f32[3,22,8,256]{3,2,1,0:T(8,128)} %get-tuple-element.47), channel_id=1, source_target_pairs={{0,1},{1,0},{2,3},{3,2},{4,5},{5,4},{6,7},{7,6},{8,9},{9,8},{10,11... | collective-permute-start | bytes 1622024 | tf_op jit(solution)/shard_map/ppermute | solution.py:55
  344.7 38.0 %collective-permute-start.16 = (f32[3,22,8,256]{3,2,1,0:T(8,128)}, f32[3,22,8,256]{3,2,1,0:T(8,128)S(1)}, u32[]{:S(2)}, u32[]{:S(2)}) collective-permute-start(f32[3,22,8,256]{3,2,1,0:T(8,128)} %get-tuple-element.48), channel_id=1, source_target_pairs={{1,2},{2,1},{3,4},{4,3},{5,6},{6,5},{9,10},{10,9},{11,12},{12,11},... | collective-permute-start | bytes 1622024 | tf_op jit(solution)/shard_map/ppermute | solution.py:55
  350.9 57.8 %collective-permute-start.21 = (f32[3,22,8,256]{3,2,1,0:T(8,128)}, f32[3,22,8,256]{3,2,1,0:T(8,128)S(1)}, u32[]{:S(2)}, u32[]{:S(2)}) collective-permute-start(f32[3,22,8,256]{3,2,1,0:T(8,128)} %get-tuple-element.55), channel_id=1, source_target_pairs={{0,1},{1,0},{2,3},{3,2},{4,5},{5,4},{6,7},{7,6},{8,9},{9,8},{10,11... | collective-permute-start | bytes 1622024 | tf_op jit(solution)/shard_map/ppermute | solution.py:55
  352.0 56.7 %collective-permute-start.22 = (f32[3,22,8,256]{3,2,1,0:T(8,128)}, f32[3,22,8,256]{3,2,1,0:T(8,128)S(1)}, u32[]{:S(2)}, u32[]{:S(2)}) collective-permute-start(f32[3,22,8,256]{3,2,1,0:T(8,128)} %get-tuple-element.56), channel_id=1, source_target_pairs={{1,2},{2,1},{3,4},{4,3},{5,6},{6,5},{9,10},{10,9},{11,12},{12,11},... | collective-permute-start | bytes 1622024 | tf_op jit(solution)/shard_map/ppermute | solution.py:55
  375.0 7.7 %collective-permute-start.12 = (f32[12,8,256]{2,1,0:T(8,128)}, f32[12,8,256]{2,1,0:T(8,128)S(1)}, u32[]{:S(2)}, u32[]{:S(2)}) collective-permute-start(f32[12,8,256]{2,1,0:T(8,128)} %get-tuple-element.44), channel_id=1, source_target_pairs={{1,2},{2,1},{3,4},{4,3},{5,6},{6,5},{9,10},{10,9},{11,12},{12,11},... | collective-permute-start | bytes 294920 | tf_op jit(solution)/shard_map/ppermute | solution.py:55
  406.5 8.6 %collective-permute-start.20 = (f32[12,8,256]{2,1,0:T(8,128)}, f32[12,8,256]{2,1,0:T(8,128)S(1)}, u32[]{:S(2)}, u32[]{:S(2)}) collective-permute-start(f32[12,8,256]{2,1,0:T(8,128)} %get-tuple-element.54), channel_id=1, source_target_pairs={{1,2},{2,1},{3,4},{4,3},{5,6},{6,5},{9,10},{10,9},{11,12},{12,11},... | collective-permute-start | bytes 294920 | tf_op jit(solution)/shard_map/ppermute | solution.py:55
  435.8 70.9 %all-to-all-start.1 = ((f32[8,16,16,256]{3,2,1,0:T(8,128)}), f32[8,16,16,256]{3,2,1,0:T(8,128)S(1)}, u32[]{:S(2)}, u32[]{:S(2)}) async-start(f32[8,16,16,256]{3,2,1,0:T(8,128)} %get-tuple-element.58), calls=%async_computation.1 | async-start | bytes 4194304 | tf_op jit(solution)/shard_map/all_to_all | solution.py:730
  441.3 7.8 %collective-permute-start.26 = (f32[10,24,256]{2,1,0:T(8,128)S(1)}, f32[10,24,256]{2,1,0:T(8,128)S(1)}, u32[]{:S(2)}, u32[]{:S(2)}) collective-permute-start(f32[10,24,256]{2,1,0:T(8,128)S(1)} %copy-done.28), channel_id=1, source_target_pairs={{8,16},{16,8},{24,32},{32,24},{40,48},{48,40},{56,64},{64,56},{72,... | collective-permute-start | bytes 737288 | tf_op jit(solution)/shard_map/ppermute | solution.py:55
  452.9 13.9 %collective-permute-start.27 = (f32[16,8,256]{2,1,0:T(8,128)}, f32[16,8,256]{2,1,0:T(8,128)S(1)}, u32[]{:S(2)}, u32[]{:S(2)}) collective-permute-start(f32[16,8,256]{2,1,0:T(8,128)} %get-tuple-element.63), channel_id=1, source_target_pairs={{0,1},{1,0},{2,3},{3,2},{4,5},{5,4},{6,7},{7,6},{8,9},{9,8},{10,11... | collective-permute-start | bytes 393224 | tf_op jit(solution)/shard_map/ppermute | solution.py:55
  453.5 17.7 %collective-permute-start.28 = (f32[16,8,256]{2,1,0:T(8,128)}, f32[16,8,256]{2,1,0:T(8,128)S(1)}, u32[]{:S(2)}, u32[]{:S(2)}) collective-permute-start(f32[16,8,256]{2,1,0:T(8,128)} %get-tuple-element.64), channel_id=1, source_target_pairs={{1,2},{2,1},{3,4},{4,3},{5,6},{6,5},{9,10},{10,9},{11,12},{12,11},... | collective-permute-start | bytes 393224 | tf_op jit(solution)/shard_map/ppermute | solution.py:55
  483.6 6.7 %collective-permute-start.30 = (f32[6,24,256]{2,1,0:T(8,128)}, f32[6,24,256]{2,1,0:T(8,128)S(1)}, u32[]{:S(2)}, u32[]{:S(2)}) collective-permute-start(f32[6,24,256]{2,1,0:T(8,128)} %get-tuple-element.68), channel_id=1, source_target_pairs={{8,16},{16,8},{24,32},{32,24},{40,48},{48,40},{56,64},{64,56},{72,... | collective-permute-start | bytes 442376 | tf_op jit(solution)/shard_map/ppermute | solution.py:55
  494.0 9.3 %collective-permute-start.32 = (f32[16,8,256]{2,1,0:T(8,128)}, f32[16,8,256]{2,1,0:T(8,128)S(1)}, u32[]{:S(2)}, u32[]{:S(2)}) collective-permute-start(f32[16,8,256]{2,1,0:T(8,128)} %get-tuple-element.71), channel_id=1, source_target_pairs={{1,2},{2,1},{3,4},{4,3},{5,6},{6,5},{9,10},{10,9},{11,12},{12,11},... | collective-permute-start | bytes 393224 | tf_op jit(solution)/shard_map/ppermute | solution.py:55
  506.7 59.9 %all-to-all-start.2 = ((f32[8,16,16,256]{3,2,1,0:T(8,128)}), f32[8,16,16,256]{3,2,1,0:T(8,128)}, u32[]{:S(2)}, u32[]{:S(2)}) async-start(f32[8,16,16,256]{3,2,1,0:T(8,128)} %shard_map.76), calls=%async_computation.2 | async-start | bytes 4194304 | tf_op jit(solution)/shard_map/all_to_all | solution.py:737
  511.0 23.8 %collective-permute-start = (f32[1,128]{1,0:T(1,128)S(1)}, f32[1,128]{1,0:T(1,128)S(1)}, u32[]{:S(2)}, u32[]{:S(2)}) collective-permute-start(f32[1,128]{1,0:T(1,128)S(1)} %broadcast_in_dim.9), channel_id=1, source_target_pairs={{0,1},{1,0},{2,3},{3,2},{4,5},{5,4},{6,7},{7,6},{8,9},{9,8},{10,11... | collective-permute-start | bytes 1544 | tf_op jit(solution)/shard_map/ppermute | solution.py:63
  513.9 53.9 %collective-permute-start.7 = (f32[3,2,128,256]{3,2,1,0:T(8,128)}, f32[3,2,128,256]{3,2,1,0:T(8,128)S(1)}, u32[]{:S(2)}, u32[]{:S(2)}) collective-permute-start(f32[3,2,128,256]{3,2,1,0:T(8,128)} %get-tuple-element.74), channel_id=1, source_target_pairs={{0,8},{8,0},{16,24},{24,16},{32,40},{40,32},{48,56},{56,48},{64,72... | collective-permute-start | bytes 2359304 | tf_op jit(solution)/shard_map/ppermute | solution.py:55
  536.0 35.6 %collective-permute-start.8 = (f32[3,2,128,256]{3,2,1,0:T(8,128)}, f32[3,2,128,256]{3,2,1,0:T(8,128)}, u32[]{:S(2)}, u32[]{:S(2)}) collective-permute-start(f32[3,2,128,256]{3,2,1,0:T(8,128)} %get-tuple-element.73), channel_id=1, source_target_pairs={{8,16},{16,8},{24,32},{32,24},{40,48},{48,40},{56,64},{64,56},{72,... | collective-permute-start | bytes 2359304 | tf_op jit(solution)/shard_map/ppermute | solution.py:55
  549.1 9.7 %collective-permute-start.5 = (f32[1,128]{1,0:T(1,128)S(1)}, f32[1,128]{1,0:T(1,128)S(1)}, u32[]{:S(2)}, u32[]{:S(2)}) collective-permute-start(f32[1,128]{1,0:T(1,128)S(1)} %add.34), channel_id=1, source_target_pairs={{0,32},{8,40},{16,48},{24,56},{32,0},{40,8},{48,16},{56,24},{64,96... | collective-permute-start | bytes 1544 | tf_op jit(solution)/shard_map/ppermute | solution.py:63
  558.9 8.9 %collective-permute-start.6 = (f32[1,128]{1,0:T(1,128)S(1)}, f32[1,128]{1,0:T(1,128)S(1)}, u32[]{:S(2)}, u32[]{:S(2)}) collective-permute-start(f32[1,128]{1,0:T(1,128)S(1)} %add.35), channel_id=1, source_target_pairs={{0,64},{8,72},{16,80},{24,88},{32,96},{40,104},{48,112},{56,120},{... | collective-permute-start | bytes 1544 | tf_op jit(solution)/shard_map/ppermute | solution.py:63
  562.0 9.6 %collective-permute-start.23 = (f32[8,3,16,256]{3,2,1,0:T(8,128)}, f32[8,3,16,256]{3,2,1,0:T(8,128)S(1)}, u32[]{:S(2)}, u32[]{:S(2)}) collective-permute-start(f32[8,3,16,256]{3,2,1,0:T(8,128)} %get-tuple-element.78), channel_id=1, source_target_pairs={{0,8},{8,0},{16,24},{24,16},{32,40},{40,32},{48,56},{56,48},{64,72... | collective-permute-start | bytes 1179656 | tf_op jit(solution)/shard_map/ppermute | solution.py:55
  564.7 9.4 %collective-permute-start.24 = (f32[8,3,16,256]{3,2,1,0:T(8,128)S(1)}, f32[8,3,16,256]{3,2,1,0:T(8,128)S(1)}, u32[]{:S(2)}, u32[]{:S(2)}) collective-permute-start(f32[8,3,16,256]{3,2,1,0:T(8,128)S(1)} %get-tuple-element.77), channel_id=1, source_target_pairs={{8,16},{16,8},{24,32},{32,24},{40,48},{48,40},{56,64},{64,56},{72,... | collective-permute-start | bytes 1179656 | tf_op jit(solution)/shard_map/ppermute | solution.py:55
  567.7 6.4 %collective-permute-start.33 = (f32[8,2,16,256]{3,2,1,0:T(8,128)S(1)}, f32[8,2,16,256]{3,2,1,0:T(8,128)S(1)}, u32[]{:S(2)}, u32[]{:S(2)}) collective-permute-start(f32[8,2,16,256]{3,2,1,0:T(8,128)S(1)} %get-tuple-element.76), channel_id=1, source_target_pairs={{0,8},{8,0},{16,24},{24,16},{32,40},{40,32},{48,56},{56,48},{64,72... | collective-permute-start | bytes 786440 | tf_op jit(solution)/shard_map/ppermute | solution.py:55
  567.8 8.8 %collective-permute-start.34 = (f32[8,2,16,256]{3,2,1,0:T(8,128)S(1)}, f32[8,2,16,256]{3,2,1,0:T(8,128)S(1)}, u32[]{:S(2)}, u32[]{:S(2)}) collective-permute-start(f32[8,2,16,256]{3,2,1,0:T(8,128)S(1)} %get-tuple-element.75), channel_id=1, source_target_pairs={{8,16},{16,8},{24,32},{32,24},{40,48},{48,40},{56,64},{64,56},{72,... | collective-permute-start | bytes 786440 | tf_op jit(solution)/shard_map/ppermute | solution.py:55
  (44 other events, 206.2 us)

commit v2 on v1

v2 whole, which is shorter than its diff:
```python
import functools

import jax
import jax.numpy as jnp
from jax import lax
from jax.experimental import pallas as pl
from jax.experimental.pallas import tpu as pltpu
from jax.sharding import PartitionSpec as P

F32 = jnp.float32
NT = 8
STEP = 1.0 / NT
DATA_WEIGHT = 4.0
KAPPA = 0.125
CX, CY, NZ = 16, 16, 256
NY = 128
DEPTH = 4
WX, WY = CX + 2 * DEPTH, CY + 2 * DEPTH
V_SLOTS = ((0, 3, 0), (1, 2, 3), (2, 1, 5))
V_ROWS = 6
VX = CX + 6
VBLOCKS = 3 * CX + 1
FACE = 2 * 3 * V_ROWS
VMEM = pltpu.VMEM
ANY = pl.ANY


def whole():
    return pl.BlockSpec(memory_space=VMEM)


def anywhere():
    return pl.BlockSpec(memory_space=ANY)


def scalars():
    return pl.BlockSpec(memory_space=pltpu.SMEM)


def params(mib=28):
    return pltpu.CompilerParams(vmem_limit_bytes=mib * 1024 * 1024)


def sds(*shape):
    return jax.ShapeDtypeStruct(shape, F32)


def swaps(size, first):
    pairs = []
    for i in range(first, size - 1, 2):
        pairs += [(i, i + 1), (i + 1, i)]
    return pairs


def swap(even, odd, axis):
    size = lax.axis_size(axis)
    return lax.ppermute(even, axis, swaps(size, 0)), lax.ppermute(odd, axis, swaps(size, 1))


def xor_swap(value, reach):
    size = lax.axis_size("space")
    return value + lax.ppermute(value, "space", [(i, i ^ reach) for i in range(size)])


def rows8():
    return lax.broadcasted_iota(jnp.int32, (8, NZ), 0)


def turn(block, shift):
    shift = shift % 8
    return pltpu.roll(block, shift, 0) if shift else block


def put(total, block, shift, low, high, sub):
    return jnp.where((sub >= low) & (sub < high), turn(block, shift), total)


def pack_edges(slots, tile, sub):
    top = jnp.zeros((8, NZ), F32)
    bottom = top
    for key, k, off in slots:
        low8, high8 = tile(key)
        top = put(top, high8, off + k, off, off + k, sub)
        bottom = put(bottom, low8, off, off, off + k, sub)
    return top, bottom


def halo_block(above, below, k, off, sub):
    block = put(jnp.zeros((8, NZ), F32), above, -off, 0, k, sub)
    return put(block, below, 8 - k - off, 8 - k, 8, sub)


def lane_masks(shape):
    z = lax.broadcasted_iota(jnp.int32, shape, 1)
    return z == 0, z == NZ - 1


def copies(pairs, sem):
    started = [pltpu.make_async_copy(a, b, sem.at[i]) for i, (a, b) in enumerate(pairs)]
    for copy in started:
        copy.start()
    return started


def wait_all(started):
    for copy in started:
        copy.wait()


def fill_velocity(group, info, vt, ra, rb, yc, yd, vw, sem):
    px, py = info[2], info[3]
    pairs = []
    for d in range(3):
        for j in range(4):
            pairs.append((vt.at[4 * group + j, d * CX : (d + 1) * CX], vw.at[j, d, 0:CX, 0:CY]))
        for j, k, off in V_SLOTS:
            to_a = jnp.where(px == 0, CX, WX - k)
            to_b = jnp.where(px == 0, WX - k, CX)
            row = (group * 3 + d) * V_ROWS + off
            pairs.append((ra.at[row : row + k], vw.at[j, d, pl.ds(to_a, k), 0:CY]))
            pairs.append((rb.at[row : row + k], vw.at[j, d, pl.ds(to_b, k), 0:CY]))
    started = copies(pairs, sem)
    sub = rows8()
    zero_row = jnp.zeros((WY, NZ), F32)
    zero_tile = jnp.zeros((8, NZ), F32)
    for j in range(4):
        k = 3 - j
        for d in range(3):
            for x in range(CX + k, WX - k):
                vw[j, d, x] = zero_row

    def blocks(d, i, x, keep):
        c, e = yc[d, i], yd[d, i]
        above = jnp.where(py == 0, c, e)
        below = jnp.where(py == 0, e, c)
        for j, k, off in V_SLOTS:
            if keep(k):
                vw[j, d, x, CY:WY] = halo_block(above, below, k, off, sub)

    def one(i, carry):
        for d in range(3):
            for r in range(2):
                blocks(d, 2 * i + r, 2 * i + r, lambda k: True)
                vw[3, d, 2 * i + r, CY:WY] = zero_tile
        return carry

    lax.fori_loop(0, CX // 2, one, 0)
    for i in range(CX, VX):
        x = i if i < CX + 3 else i + 2
        for d in range(3):
            blocks(d, i, x, lambda k: x < CX + k or x >= WX - k)
    return started


FILL_COPIES = 30


def fill_image(info, win, yc, yd, image):
    py = info[3]
    sub = rows8()

    def one(i, carry):
        c, e = yc[i], yd[i]
        above = jnp.where(py == 0, c, e)
        below = jnp.where(py == 0, e, c)
        image[i, 0:CY] = win[i]
        image[i + 12, 0:CY] = win[i + 12]
        image[i, CY:WY] = halo_block(above, below, 4, 0, sub)
        image[i + 12, CY:WY] = halo_block(above, below, 4, 4, sub)
        return carry

    lax.fori_loop(0, 12, one, 0)


ROWS = 2


def sweep_rows(reach, row, dst):
    turns = -(-(CX + 2 * reach) // ROWS)

    def one(i, carry):
        xs = [lax.rem(i * ROWS + r - reach + WX, WX) for r in range(ROWS)]
        values = [row(x, lax.rem(x + WX - 1, WX), lax.rem(x + 1, WX)) for x in xs]
        for x, value in zip(xs, values):
            dst[x] = value
        return carry

    lax.fori_loop(0, turns, one, 0)


def advance(src, dst, vw, j, reach):
    first, last = lane_masks((WY, NZ))

    def row(x, xm, xp):
        c = src[x]
        v0, v1, v2 = vw[j, 0, x], vw[j, 1, x], vw[j, 2, x]
        flow = v0 * jnp.where(v0 > 0.0, c - src[xm], src[xp] - c)
        flow += v1 * jnp.where(v1 > 0.0, c - pltpu.roll(c, 1, 0), pltpu.roll(c, WY - 1, 0) - c)
        behind = jnp.where(first, 0.0, pltpu.roll(c, 1, 1))
        beyond = jnp.where(last, 0.0, pltpu.roll(c, NZ - 1, 1))
        flow += v2 * jnp.where(v2 > 0.0, c - behind, beyond - c)
        return c - STEP * flow

    sweep_rows(reach, row, dst)


def scatter(src, dst, vw, j, reach):
    first, last = lane_masks((WY, NZ))

    def row(x, xm, xp):
        c = src[x]
        v0, v1, v2 = vw[j, 0, x], vw[j, 1, x], vw[j, 2, x]
        change = (jnp.abs(v0) + jnp.abs(v1) + jnp.abs(v2)) * c
        change -= jnp.maximum(vw[j, 0, xp], 0.0) * src[xp]
        change += jnp.minimum(vw[j, 0, xm], 0.0) * src[xm]
        change -= pltpu.roll(jnp.maximum(v1, 0.0) * c, WY - 1, 0)
        change += pltpu.roll(jnp.minimum(v1, 0.0) * c, 1, 0)
        change -= jnp.where(last, 0.0, pltpu.roll(jnp.maximum(v2, 0.0) * c, NZ - 1, 1))
        change += jnp.where(first, 0.0, pltpu.roll(jnp.minimum(v2, 0.0) * c, 1, 1))
        return c - STEP * change

    sweep_rows(reach, row, dst)


def clear_halo(ref, x_rows=True):
    zero_row = jnp.zeros((WY, NZ), F32)
    for x in range(CX, WX):
        ref[x] = zero_row


def repack(velocity, counts):
    tiles = NY // CY

    def kernel(counts, src, dst, held, note, isem, osem):
        value = jnp.full((CY, NZ), counts[0], jnp.int32).astype(F32)
        note[0] = value
        arrive, leave = [], []
        for c in range(tiles):
            for d in range(3):
                n = c * 3 + d
                copy = pltpu.make_async_copy(src.at[0, d, :, c * CY : (c + 1) * CY], held.at[c, d], isem.at[n])
                copy.start()
                arrive.append(copy)
        for c in range(tiles):
            copy = pltpu.make_async_copy(note, dst.at[c, 3 * CX : VBLOCKS], osem.at[24 + c])
            copy.start()
            leave.append(copy)
            for d in range(3):
                n = c * 3 + d
                arrive[n].wait()
                copy = pltpu.make_async_copy(held.at[c, d], dst.at[c, d * CX : (d + 1) * CX], osem.at[n])
                copy.start()
                leave.append(copy)
        wait_all(leave)

    return pl.pallas_call(
        kernel,
        out_shape=sds(tiles, VBLOCKS, CY, NZ),
        in_specs=[scalars(), anywhere()],
        out_specs=anywhere(),
        scratch_shapes=[
            VMEM((tiles, 3, CX, CY, NZ), F32),
            VMEM((1, CY, NZ), F32),
            pltpu.SemaphoreType.DMA((24,)),
            pltpu.SemaphoreType.DMA((32,)),
        ],
        compiler_params=params(),
    )(counts, velocity)


def template(info, table, atlas, labels):
    def kernel(info, table, atlas, labels, tmpl):
        def one(x, carry):
            lab = labels[x]
            value = jnp.zeros((CY, NZ), F32)
            for l in range(64):
                value = jnp.where(lab == l, table[l], value)
            tmpl[x] = atlas[x] + value
            return carry

        lax.fori_loop(0, CX, one, 0)

    return pl.pallas_call(
        kernel,
        out_shape=sds(CX, CY, NZ),
        in_specs=[scalars(), scalars(), whole(), whole()],
        out_specs=whole(),
        compiler_params=params(),
    )(info, table, atlas, labels)


def image_edges(info, tile, ra, rb):
    def kernel(info, tile, ra, rb, win, ec, ed):
        px, py = info[2], info[3]
        win[0:CX] = tile[...]
        win[pl.ds(jnp.where(px == 0, CX, WX - DEPTH), DEPTH)] = ra[...]
        win[pl.ds(jnp.where(px == 0, WX - DEPTH, CX), DEPTH)] = rb[...]
        sub = rows8()

        def one(i, carry):
            def tile_of(key):
                return win[i + key, 0:8], win[i + key, 8:16]

            top, bottom = pack_edges(((0, 4, 0), (12, 4, 4)), tile_of, sub)
            ec[i] = jnp.where(py == 0, top, bottom)
            ed[i] = jnp.where(py == 0, bottom, top)
            return carry

        lax.fori_loop(0, 12, one, 0)

    return pl.pallas_call(
        kernel,
        out_shape=[sds(WX, CY, NZ), sds(12, 8, NZ), sds(12, 8, NZ)],
        in_specs=[scalars()] + [whole()] * 3,
        out_specs=[whole()] * 3,
        compiler_params=params(),
    )(info, tile, ra, rb)


def faces(info, vt, tile, *before):
    def kernel(info, vt, tile, *refs):
        ea, eb, sem = refs[-3:]
        px = info[2]
        pairs = []
        for g in range(2):
            for d in range(3):
                for j, k, off in V_SLOTS:
                    top = jnp.where(px == 0, CX - k, 0) + d * CX
                    bottom = jnp.where(px == 0, 0, CX - k) + d * CX
                    row = (g * 3 + d) * V_ROWS + off
                    pairs.append((vt.at[4 * g + j, pl.ds(top, k)], ea.at[row : row + k]))
                    pairs.append((vt.at[4 * g + j, pl.ds(bottom, k)], eb.at[row : row + k]))
        started = copies(pairs, sem)
        ea[FACE : FACE + DEPTH] = tile[pl.ds(jnp.where(px == 0, CX - DEPTH, 0), DEPTH)]
        eb[FACE : FACE + DEPTH] = tile[pl.ds(jnp.where(px == 0, 0, CX - DEPTH), DEPTH)]
        wait_all(started)

    return pl.pallas_call(
        kernel,
        out_shape=[sds(FACE + DEPTH, CY, NZ)] * 2,
        in_specs=[scalars(), anywhere(), whole()] + [anywhere()] * len(before),
        out_specs=[whole()] * 2,
        scratch_shapes=[pltpu.SemaphoreType.DMA((36,))],
        compiler_params=params(),
    )(info, vt, tile, *before)


def velocity_edges(info, vt, ra, rb, group, tile=None):
    with_image = tile is not None
    rows = VX + 4 if with_image else VX

    def kernel(info, vt, ra, rb, va, vb, *refs):
        ec, ed = refs[-2:]
        px, py = info[2], info[3]
        sub = rows8()

        def emit(i, slots, tile_of):
            top, bottom = pack_edges(slots, tile_of, sub)
            ec[0, i] = jnp.where(py == 0, top, bottom)
            ed[0, i] = jnp.where(py == 0, bottom, top)

        def one(i, carry):
            for r in range(2):
                x = 2 * i + r
                emit(x, V_SLOTS, lambda j: (vt[j, x, 0:8], vt[j, x, 8:16]))
            return carry

        lax.fori_loop(0, CX // 2, one, 0)
        for i in range(3):
            up, down = [], []
            for j, k, off in V_SLOTS:
                if i < k:
                    up.append((j, k, off))
                if i >= 3 - k:
                    down.append((j, k, off))

            def halves(value):
                return value[0:8], value[8:16]

            def tile_up(j):
                row = V_SLOTS[j][2] + i
                return halves(jnp.where(px == 0, ra[row], rb[row]))

            def tile_down(j):
                row = V_SLOTS[j][2] + i - (3 - V_SLOTS[j][1])
                return halves(jnp.where(px == 0, rb[row], ra[row]))

            emit(CX + i, up, tile_up)
            emit(CX + 3 + i, down, tile_down)
        if with_image:
            own = refs[0]
            d = pl.program_id(0)
            for i in range(4):
                other = jnp.where(px == d - 1, va[i], vb[i])
                other = jnp.where(d == 0, own[12 + i], other)
                near = own[4 * d + i]
                pair = ((near[0:8], near[8:16]), (other[0:8], other[8:16]))
                emit(VX + i, ((0, 4, 0), (1, 4, 4)), lambda key: pair[key])

    image_face = pl.BlockSpec((DEPTH, CY, NZ), lambda d: (FACE // DEPTH, 0, 0))
    face = pl.BlockSpec((V_ROWS, CY, NZ), lambda d: (group * 3 + d, 0, 0))
    return pl.pallas_call(
        kernel,
        grid=(3,),
        out_shape=[sds(3, rows, 8, NZ)] * 2,
        in_specs=[
            scalars(),
            pl.BlockSpec((4, CX, CY, NZ), lambda d: (group, d, 0, 0)),
            face,
            face,
            image_face,
            image_face,
        ]
        + ([pl.BlockSpec((CX, CY, NZ), lambda d: (0, 0, 0))] if with_image else []),
        out_specs=[pl.BlockSpec((1, rows, 8, NZ), lambda d: (d, 0, 0, 0))] * 2,
        compiler_params=params(),
    )(info, vt, ra, rb, ra, rb, *((tile,) if with_image else ()))


def forward_first(info, tile, vt, ra, rb, yc, yd, *before):
    def kernel(info, tile, vt, ra, rb, yc, yd, *refs):
        pack, ea, eb, i4, vw, image, halos, hsem, sem, osem = refs[len(before) :]
        px, py = info[2], info[3]
        pair = copies([(ra.at[FACE : FACE + DEPTH], halos.at[0]), (rb.at[FACE : FACE + DEPTH], halos.at[1])], hsem)
        started = fill_velocity(0, info, vt, ra, rb, yc, yd, vw, sem)
        image[0, 0:CX, 0:CY] = tile[...]
        wait_all(pair)
        image[0, pl.ds(jnp.where(px == 0, CX, WX - DEPTH), DEPTH), 0:CY] = halos[0]
        image[0, pl.ds(jnp.where(px == 0, WX - DEPTH, CX), DEPTH), 0:CY] = halos[1]
        sub = rows8()
        for j in range(12):
            c, e = yc[j // 4, VX + j % 4], yd[j // 4, VX + j % 4]
            above = jnp.where(py == 0, c, e)
            below = jnp.where(py == 0, e, c)
            image[0, j, CY:WY] = halo_block(above, below, 4, 0, sub)
            image[0, j + 12, CY:WY] = halo_block(above, below, 4, 4, sub)
        wait_all(started)
        out = []
        for j in range(4):
            advance(image.at[j], image.at[j + 1], vw, j, 3 - j)
            out.append(pltpu.make_async_copy(image.at[j, 0:CX, 0:CY], pack.at[j, 0], osem.at[j]))
            out[-1].start()
        last = image.at[4]
        i4[...] = last[0:CX, 0:CY]
        ea[...] = last[pl.ds(jnp.where(px == 0, CX - DEPTH, 0), DEPTH), 0:CY]
        eb[...] = last[pl.ds(jnp.where(px == 0, 0, CX - DEPTH), DEPTH), 0:CY]
        wait_all(out)

    return pl.pallas_call(
        kernel,
        out_shape=[
            sds(NT, 2, CX, CY, NZ),
            sds(DEPTH, CY, NZ),
            sds(DEPTH, CY, NZ),
            sds(CX, CY, NZ),
            sds(4, 3, WX, WY, NZ),
        ],
        in_specs=[scalars(), whole()] + [anywhere()] * 3 + [whole()] * 2 + [anywhere()] * len(before),
        out_specs=[anywhere()] + [whole()] * 4,
        scratch_shapes=[
            VMEM((5, WX, WY, NZ), F32),
            VMEM((2, DEPTH, CY, NZ), F32),
            pltpu.SemaphoreType.DMA((2,)),
            pltpu.SemaphoreType.DMA((FILL_COPIES,)),
            pltpu.SemaphoreType.DMA((4,)),
        ],
        compiler_params=params(),
    )(info, tile, vt, ra, rb, yc, yd, *before)


def window(info, vt, ra, rb, yc, yd, group):
    def kernel(info, vt, ra, rb, yc, yd, vw, sem):
        wait_all(fill_velocity(group, info, vt, ra, rb, yc, yd, vw, sem))

    return pl.pallas_call(
        kernel,
        out_shape=sds(4, 3, WX, WY, NZ),
        in_specs=[scalars()] + [anywhere()] * 3 + [whole()] * 2,
        out_specs=whole(),
        scratch_shapes=[pltpu.SemaphoreType.DMA((FILL_COPIES,))],
        compiler_params=params(),
    )(info, vt, ra, rb, yc, yd)


def send_rows(info, widths, source, ea, eb):
    px = info[2]
    off = 0
    for n, k in enumerate(widths):
        top = jnp.where(px == 0, CX, WX - k)
        bottom = jnp.where(px == 0, WX - k, CX)
        ea[off : off + k] = source(n)[pl.ds(top, k)]
        eb[off : off + k] = source(n)[pl.ds(bottom, k)]
        off += k


MID_WIDTHS = (4, 3, 2, 1)
MID_SLOTS = ((0, 4, 0), (1, 3, 4), (3, 1, 7))
END_WIDTHS = (3, 2, 1)
END_SLOTS = ((0, 3, 0), (1, 2, 3), (2, 1, 5), (3, 2, 6))


def forward_second(info, win, ic, idd, target, vw, pack, *before):
    def kernel(info, win, ic, idd, target, vw, pack_in, *refs):
        pack, lw, ea, eb, image, lam, osem = refs[len(before) :]
        fill_image(info, win, ic, idd, image.at[0])
        for n in range(4):
            clear_halo(lam.at[n])
        out = []
        for j in range(4):
            advance(image.at[j], image.at[j + 1], vw, j, 3 - j)
            out.append(pltpu.make_async_copy(image.at[j, 0:CX, 0:CY], pack.at[4 + j, 0], osem.at[j]))
            out[-1].start()
        count = info[4]
        inside = lax.broadcasted_iota(jnp.int32, (CY, NZ), 0) * NZ + lax.broadcasted_iota(jnp.int32, (CY, NZ), 1)
        zero = jnp.zeros((8, NZ), F32)

        def one(x, carry):
            value = image[4, x, 0:CY] - target[x]
            lam[0, x, 0:CY] = jnp.where(inside + x * (CY * NZ) < count, value, 0.0)
            lam[0, x, CY:WY] = zero
            return carry

        lax.fori_loop(0, CX, one, 0)
        out.append(pltpu.make_async_copy(lam.at[0, 0:CX, 0:CY], pack.at[7, 1], osem.at[4]))
        out[-1].start()
        for n in range(4):
            scatter(lam.at[n], lam.at[n + 1], vw, 3 - n, n + 1)
        for n in range(4):
            lw[n] = lam[4 - n, 0:CX]
        send_rows(info, MID_WIDTHS, lambda n: lam.at[4 - n], ea, eb)
        wait_all(out)

    return pl.pallas_call(
        kernel,
        out_shape=[sds(NT, 2, CX, CY, NZ), sds(4, CX, WY, NZ), sds(10, WY, NZ), sds(10, WY, NZ)],
        in_specs=[scalars()] + [whole()] * 5 + [anywhere()] * (1 + len(before)),
        out_specs=[anywhere()] + [whole()] * 3,
        scratch_shapes=[
            VMEM((5, WX, WY, NZ), F32),
            VMEM((5, WX, WY, NZ), F32),
            pltpu.SemaphoreType.DMA((5,)),
        ],
        input_output_aliases={6: 0},
        compiler_params=params(),
    )(info, win, ic, idd, target, vw, pack, *before)


def costate_edges(info, lw, ra, rb, widths, slots):
    def kernel(info, lw_in, ra, rb, lw, ec, ed):
        px, py = info[2], info[3]
        off = 0
        for n, k in enumerate(widths):
            for i in range(k):
                to_a = jnp.where(px == 0, CX - k, 0) + i
                to_b = jnp.where(px == 0, 0, CX - k) + i
                lw[n, to_a] = lw[n, to_a] + ra[off + i]
                lw[n, to_b] = lw[n, to_b] + rb[off + i]
            off += k
        sub = rows8()

        def one(x, carry):
            top = jnp.zeros((8, NZ), F32)
            bottom = top
            for n, k, off in slots:
                block = lw[n, x, CY:WY]
                top = put(top, block, off, off, off + k, sub)
                bottom = put(bottom, block, off + k, off, off + k, sub)
            ec[x] = jnp.where(py == 0, top, bottom)
            ed[x] = jnp.where(py == 0, bottom, top)
            return carry

        lax.fori_loop(0, CX, one, 0)

    return pl.pallas_call(
        kernel,
        out_shape=[sds(4, CX, WY, NZ), sds(CX, 8, NZ), sds(CX, 8, NZ)],
        in_specs=[scalars()] + [whole()] * 3,
        out_specs=[whole()] * 3,
        input_output_aliases={1: 0},
        compiler_params=params(),
    )(info, lw, ra, rb)


def take(c, e, py, k, off, sub):
    below = jnp.where(py == 0, e, c)
    above = jnp.where(py == 0, c, e)
    zero = jnp.zeros((8, NZ), F32)
    return put(zero, below, -off, 0, k, sub), put(zero, above, 8 - k - off, 8 - k, 8, sub)


def backward_second(info, lw, lc, ld, vw, pack, *before):
    def kernel(info, lw, lc, ld, vw, pack_in, *refs):
        pack, lw2, ea, eb, lam, done, osem = refs[len(before) :]
        for n in range(3):
            clear_halo(lam.at[n])
        py = info[3]
        sub = rows8()
        zero = jnp.zeros((8, NZ), F32)

        def one(x, carry):
            c, e = lc[x], ld[x]
            for n, k, off in MID_SLOTS:
                low, high = take(c, e, py, k, off, sub)
                low, high = lw[n, x, 0:8] + low, lw[n, x, 8:16] + high
                if n == 0:
                    lam[0, x, 0:8] = low
                    lam[0, x, 8:16] = high
                    lam[0, x, CY:WY] = zero
                else:
                    done[(n - 1) // 2, x, 0:8] = low
                    done[(n - 1) // 2, x, 8:16] = high
            return carry

        lax.fori_loop(0, CX, one, 0)
        out = [
            pltpu.make_async_copy(lam.at[0, 0:CX, 0:CY], pack.at[3, 1], osem.at[0]),
            pltpu.make_async_copy(done.at[0], pack.at[4, 1], osem.at[1]),
            pltpu.make_async_copy(done.at[1], pack.at[6, 1], osem.at[2]),
        ]
        for copy in out:
            copy.start()
        for n in range(3):
            scatter(lam.at[n], lam.at[n + 1], vw, 3 - n, n + 1)
        for n in range(3):
            lw2[n] = lam[3 - n, 0:CX]
        lw2[3] = lw[2]
        send_rows(info, END_WIDTHS, lambda n: lam.at[3 - n], ea, eb)
        wait_all(out)

    return pl.pallas_call(
        kernel,
        out_shape=[sds(NT, 2, CX, CY, NZ), sds(4, CX, WY, NZ), sds(6, WY, NZ), sds(6, WY, NZ)],
        in_specs=[scalars()] + [whole()] * 4 + [anywhere()] * (1 + len(before)),
        out_specs=[anywhere()] + [whole()] * 3,
        scratch_shapes=[
            VMEM((4, WX, WY, NZ), F32),
            VMEM((2, CX, CY, NZ), F32),
            pltpu.SemaphoreType.DMA((3,)),
        ],
        input_output_aliases={5: 0},
        compiler_params=params(),
    )(info, lw, lc, ld, vw, pack, *before)


def costate_finish(info, lw, lc, ld, pack, *before):
    def kernel(info, lw, lc, ld, pack_in, *refs):
        pack, done, sem = refs[len(before) :]
        py = info[3]
        sub = rows8()

        def one(x, carry):
            c, e = lc[x], ld[x]
            for n, k, off in END_SLOTS:
                low, high = take(c, e, py, k, off, sub)
                done[n, x, 0:8] = lw[n, x, 0:8] + low
                done[n, x, 8:16] = lw[n, x, 8:16] + high
            return carry

        lax.fori_loop(0, CX, one, 0)
        wait_all(copies([(done.at[n], pack.at[m, 1]) for n, m in enumerate((0, 1, 2, 5))], sem))

    return pl.pallas_call(
        kernel,
        out_shape=sds(NT, 2, CX, CY, NZ),
        in_specs=[scalars()] + [whole()] * 3 + [anywhere()] * (1 + len(before)),
        out_specs=anywhere(),
        scratch_shapes=[VMEM((4, CX, CY, NZ), F32), pltpu.SemaphoreType.DMA((4,))],
        input_output_aliases={4: 0},
        compiler_params=params(),
    )(info, lw, lc, ld, pack, *before)


def masks(shape):
    first, last = lane_masks(shape)
    y = lax.broadcasted_iota(jnp.int32, shape, 0)
    return first, last, y == 0, y == NY - 1


def shifted(c, m):
    first, last, bottom, top = m
    return (
        jnp.where(bottom, 0.0, pltpu.roll(c, 1, 0)),
        jnp.where(top, 0.0, pltpu.roll(c, NY - 1, 0)),
        jnp.where(first, 0.0, pltpu.roll(c, 1, 1)),
        jnp.where(last, 0.0, pltpu.roll(c, NZ - 1, 1)),
    )


def smooth(before, c, after, m):
    near = before + after
    for value in shifted(c, m):
        near += value
    return c + KAPPA * (near - 6.0 * c)


def slope(v, before, c, after, direction, m):
    if direction == 0:
        return jnp.where(v > 0.0, c - before, after - c)
    first, last, bottom, top = m
    axis, size, low, high = (0, NY, bottom, top) if direction == 1 else (1, NZ, first, last)
    behind = jnp.where(low, 0.0, pltpu.roll(c, 1, axis))
    beyond = jnp.where(high, 0.0, pltpu.roll(c, size - 1, axis))
    return jnp.where(v > 0.0, c - behind, beyond - c)


def finish_inside(weight, velocity, pack):
    def kernel(weight, vel, pack, out, keep_c, keep_s, islab, lslab, grad, soft, sem):
        d = pl.program_id(0)
        coef = weight[0]

        @pl.when(d == 0)
        def _():
            pairs = []
            for c in range(NY // CY):
                y = slice(c * CY, (c + 1) * CY)
                pairs += [(pack.at[c, 0], islab.at[:, y]), (pack.at[c, 1], lslab.at[:, y])]
            wait_all(copies(pairs, sem))

        m = masks((NY, NZ))
        for direction in range(3):

            @pl.when(d == direction)
            def _(direction=direction):
                def one(x, carry):
                    g = slope(vel[0, 0, x], islab[x - 1], islab[x], islab[x + 1], direction, m)
                    grad[x] = (coef * lslab[x]) * g
                    return carry

                lax.fori_loop(1, CX - 1, one, 0)

        def once(x, carry):
            soft[x] = smooth(grad[x - 1], grad[x], grad[x + 1], m)
            return carry

        lax.fori_loop(2, CX - 2, once, 0)

        def twice(x, carry):
            out[0, 0, x] = vel[0, 0, x] + smooth(soft[x - 1], soft[x], soft[x + 1], m)
            return carry

        lax.fori_loop(3, CX - 3, twice, 0)
        for n, (x, y) in enumerate(((1, 2), (2, 3), (13, 12), (14, 13))):
            keep_c[0, n] = grad[x]
            keep_s[0, n] = soft[y]

    slab = pl.BlockSpec((1, 1, CX, NY, NZ), lambda d: (0, d, 0, 0, 0))
    kept = pl.BlockSpec((1, 4, NY, NZ), lambda d: (d, 0, 0, 0))
    return pl.pallas_call(
        kernel,
        grid=(3,),
        out_shape=[sds(1, 3, CX, NY, NZ), sds(3, 4, NY, NZ), sds(3, 4, NY, NZ)],
        in_specs=[scalars(), slab, anywhere()],
        out_specs=[slab, kept, kept],
        scratch_shapes=[VMEM((CX, NY, NZ), F32)] * 4 + [pltpu.SemaphoreType.DMA((16,))],
        compiler_params=params(),
    )(weight, velocity, pack)


def finish_edges(info, weight, velocity, va, vb, pack, fa, fb, keep_c, keep_s, partial):
    def kernel(info, weight, vel, va, vb, pack, fa, fb, keep_c, keep_s, partial, out, slabs, vrows, grad, soft, result, sem, vsem, osem):
        d = pl.program_id(0)
        px = info[2]
        coef = weight[0]

        @pl.when(d == 0)
        def _():
            pairs = []
            above, below = jnp.where(px == 0, 1, 0), jnp.where(px == 0, 0, 1)
            hi, hl = jnp.where(px == 0, 2, 0), jnp.where(px == 0, 6, 5)
            bi, bl = jnp.where(px == 0, 0, 2), jnp.where(px == 0, 5, 6)
            for c in range(NY // CY):
                y = slice(c * CY, (c + 1) * CY)
                pairs += [
                    (pack.at[c, 0, 0:2], slabs.at[0, 3:5, y]),
                    (pack.at[c, 1, 0:1], slabs.at[0, 7:8, y]),
                    (pack.at[c, 0, CX - 2 : CX], slabs.at[1, 0:2, y]),
                    (pack.at[c, 1, CX - 1 : CX], slabs.at[1, 5:6, y]),
                    (fa.at[c, 0:3], slabs.at[above, pl.ds(hi, 3), y]),
                    (fa.at[c, 3:5], slabs.at[above, pl.ds(hl, 2), y]),
                    (fb.at[c, 0:3], slabs.at[below, pl.ds(bi, 3), y]),
                    (fb.at[c, 3:5], slabs.at[below, pl.ds(bl, 2), y]),
                ]
            wait_all(copies(pairs, sem))

        wait_all(
            copies([(vel.at[0, d, 0:3], vrows.at[0]), (vel.at[0, d, CX - 3 : CX], vrows.at[1])], vsem)
        )
        m = masks((NY, NZ))
        for direction in range(3):

            @pl.when(d == direction)
            def _(direction=direction):
                for side in range(2):
                    for n in range(3):
                        own = n == 2 if side == 0 else n == 0
                        if own:
                            v = vrows[0, 0] if side == 0 else vrows[1, 2]
                        else:
                            k = n if side == 0 else n - 1
                            v = jnp.where((px == 0) == (side == 1), va[0, k], vb[0, k])
                        g = slope(v, slabs[side, n], slabs[side, n + 1], slabs[side, n + 2], direction, m)
                        grad[side, n] = (coef * slabs[side, 5 + n]) * g

        for n in range(2):
            grad[0, 3 + n] = keep_c[0, n]
            grad[1, 3 + n] = keep_c[0, 2 + n]
        zero = jnp.zeros((NY, NZ), F32)
        for side in range(2):
            order = [0, 1, 2, 3, 4] if side == 0 else [3, 4, 0, 1, 2]
            for n in range(3):
                soft[side, n] = smooth(grad[side, order[n]], grad[side, order[n + 1]], grad[side, order[n + 2]], m)

        @pl.when(info[0] == 0)
        def _():
            soft[0, 0] = zero

        @pl.when(info[0] == info[5] - 1)
        def _():
            soft[1, 2] = zero

        low = [soft.at[0, 0], soft.at[0, 1], soft.at[0, 2], keep_s.at[0, 0], keep_s.at[0, 1]]
        high = [keep_s.at[0, 2], keep_s.at[0, 3], soft.at[1, 0], soft.at[1, 1], soft.at[1, 2]]
        for side, rows in enumerate((low, high)):
            for n in range(3):
                result[side, n] = vrows[side, n] + smooth(rows[n][...], rows[n + 1][...], rows[n + 2][...], m)
        wait_all(
            copies([(result.at[0], out.at[0, d, 0:3]), (result.at[1], out.at[0, d, CX - 3 : CX])], osem)
        )

    face = pl.BlockSpec((1, 2, NY, NZ), lambda d: (d, 0, 0, 0))
    kept = pl.BlockSpec((1, 4, NY, NZ), lambda d: (d, 0, 0, 0))
    return pl.pallas_call(
        kernel,
        grid=(3,),
        out_shape=sds(1, 3, CX, NY, NZ),
        in_specs=[scalars(), scalars(), anywhere(), face, face] + [anywhere()] * 3 + [kept, kept, anywhere()],
        out_specs=anywhere(),
        scratch_shapes=[
            VMEM((2, 8, NY, NZ), F32),
            VMEM((2, 3, NY, NZ), F32),
            VMEM((2, 5, NY, NZ), F32),
            VMEM((2, 3, NY, NZ), F32),
            VMEM((2, 3, NY, NZ), F32),
            pltpu.SemaphoreType.DMA((64,)),
            pltpu.SemaphoreType.DMA((2,)),
            pltpu.SemaphoreType.DMA((2,)),
        ],
        input_output_aliases={10: 0},
        compiler_params=params(),
    )(info, weight, velocity, va, vb, pack, fa, fb, keep_c, keep_s, partial)


def edge_rows(value, dim, k, px):
    length = value.shape[dim]
    high = lax.slice_in_dim(value, length - k, length, axis=dim)
    low = lax.slice_in_dim(value, 0, k, axis=dim)
    return jnp.where(px == 0, high, low), jnp.where(px == 0, low, high)


def shards(velocity, atlas_image, target, labels, label_table, counts):
    s, c = lax.axis_index("space"), lax.axis_index("cuts")
    px, py = s % 2, c % 2
    info = jnp.stack([s, c, px, py, counts[0], jnp.int32(lax.axis_size("space")), s, s]).astype(jnp.int32)
    vt = lax.all_to_all(repack(velocity, counts), "cuts", split_axis=0, concat_axis=0, tiled=True)

    tile = template(info, label_table, atlas_image, labels)
    ova, ovb = edge_rows(velocity[0], 1, 2, px)
    ova, ovb = swap(ova, ovb, "space")

    fa, fb = swap(*faces(info, vt, tile, ova, ovb), "space")
    total = jnp.broadcast_to(jnp.sum(vt[:, 3 * CX, 0, 0]), (1, 128))
    y0 = swap(*velocity_edges(info, vt, fa, fb, 0, tile), "cuts")
    y1 = swap(*velocity_edges(info, vt, fa, fb, 1), "cuts")
    pack, ea, eb, i4, vw0 = forward_first(info, tile, vt, fa, fb, *y0)
    total = xor_swap(total, 1)
    win, ec, ed = image_edges(info, i4, *swap(ea, eb, "space"))
    vw1 = window(info, vt, fa, fb, *y1, 1)
    ic, idd = swap(ec, ed, "cuts")
    pack, lw, ea, eb = forward_second(info, win, ic, idd, target, vw1, pack, total)
    total = xor_swap(total, 2)
    lw, ec, ed = costate_edges(info, lw, *swap(ea, eb, "space"), MID_WIDTHS, MID_SLOTS)
    ec, ed = swap(ec, ed, "cuts")
    pack, lw, ea, eb = backward_second(info, lw, ec, ed, vw0, pack, total)
    total = xor_swap(total, 4)
    lw, ec, ed = costate_edges(info, lw, *swap(ea, eb, "space"), END_WIDTHS, END_SLOTS)
    ec, ed = swap(ec, ed, "cuts")
    pack = costate_finish(info, lw, ec, ed, pack, total)
    total = xor_swap(total, 8)
    pack = lax.all_to_all(pack, "cuts", split_axis=0, concat_axis=0, tiled=True)

    cells = CX * CY * NZ * lax.axis_size("space") * lax.axis_size("cuts")
    weight = jnp.reshape(-STEP * DATA_WEIGHT * (cells / total[0, 0]), (1,)).astype(F32)
    rows = [jnp.concatenate([pack[:, 0, a : a + 3], pack[:, 1, b : b + 2]], axis=1) for a, b in ((CX - 3, CX - 2), (0, 0))]
    ea, eb = jnp.where(px == 0, rows[0], rows[1]), jnp.where(px == 0, rows[1], rows[0])
    fa, fb = swap(ea, eb, "space")
    partial, keep_c, keep_s = finish_inside(weight, velocity, pack)
    return finish_edges(info, weight, velocity, ova, ovb, pack, fa, fb, keep_c, keep_s, partial)


def solution(mesh):
    in_specs = (
        P("cuts", None, "space", None, None),
        P("space", "cuts", None),
        P("space", "cuts", None),
        P("space", "cuts", None),
        P(),
        P(("space", "cuts")),
    )
    out_specs = P("cuts", None, "space", None, None)
    return jax.shard_map(shards, mesh=mesh, in_specs=in_specs, out_specs=out_specs, check_vma=False)
```

time: 612 us -> 321 us (0.52)
  the two profiles are of different devices: /device:TPU:93 before, /device:TPU:7 now
where the time goes in v2:
time: 321 us; the launch traced here: 320 us
  waiting for transfers between devices  98.3 us (31%)
  starting transfers between devices  87.8 us (27%)
  Pallas kernels  63.8 us (20%)
  blocking collectives  56.9 us (18%)
  local copies, waits for them, and re-layouts  6.35 us (2%)
  other arithmetic  5.23 us (2%)
    all_to_all x1, blocking collectives, shards(): pack = lax.all_to_all(pack, 'cuts', split_axis=0, concat_axis=0, tiled=True)  56.9 us
    all_to_all x1, waiting for transfers between devices, shards(): lax.all_to_all(repack(velocity, counts), 'cuts', split_axis=0, concat_axi...  53.1 us
    ppermute x11, starting transfers between devices, swap(): lax.ppermute(even, axis, swaps(size, 0))  43.8 us
    ppermute x11, starting transfers between devices, swap(): lax.ppermute(odd, axis, swaps(size, 1))  37.8 us
    ppermute x11, waiting for transfers between devices, swap(): lax.ppermute(odd, axis, swaps(size, 1))  30.8 us
    pallas_call x1, Pallas kernels, finish_inside(): pl.pallas_call(kernel, grid=(3,), out_shape=[sds(1, 3, CX, NY, NZ), sds(3...  15.1 us
    pallas_call x1, Pallas kernels, finish_edges(): pl.pallas_call(kernel, grid=(3,), out_shape=sds(1, 3, CX, NY, NZ), in_spe...  10.7 us
    pallas_call x1, Pallas kernels, forward_second(): pl.pallas_call(kernel, out_shape=[sds(NT, 2, CX, CY, NZ), sds(4, CX, WY,...  9.6 us
  transfers between devices with their start and end apart: 27, of which 10 were waited for; matrix products, arithmetic and copies ran while one was open for 2% of the time, Pallas kernels for 10%

profile of v2, /device:TPU:7, one launch (start us, length us, event | category | flops | bytes accessed | tf_op | source)
XLA Modules:
  0.0 319.7 jit_solution(1787101714268808646)
XLA Ops:
  7.8 5.7 %all-to-all-start = ((f32[8,49,16,256]{3,2,1,0:T(8,128)}), f32[8,49,16,256]{3,2,1,0:T(8,128)}, u32[]{:S(2)}, u32[]{:S(2)}) async-start(f32[8,49,16,256]{3,2,1,0:T(8,128)} %copy-done.1), calls=%async_computation | async-start | bytes 12845056 | tf_op jit(solution)/shard_map/all_to_all | solution.py:864
  16.9 5.0 %collective-permute-start.5 = (f32[3,2,128,256]{3,2,1,0:T(8,128)S(1)}, f32[3,2,128,256]{3,2,1,0:T(8,128)S(1)}, u32[]{:S(2)}, u32[]{:S(2)}) collective-permute-start(f32[3,2,128,256]{3,2,1,0:T(8,128)S(1)} %get-tuple-element.67), channel_id=1, source_target_pairs={{8,16},{16,8},{24,32},{32,24},{40,48},{48,40},{56,64},{64,56},{72,... | collective-permute-start | bytes 2359304 | tf_op jit(solution)/shard_map/ppermute | solution.py:57
  24.0 9.9 %collective-permute-done.5.refs_1_.vb = f32[3,2,128,256]{3,2,1,0:T(8,128)S(1)} collective-permute-done((f32[3,2,128,256]{3,2,1,0:T(8,128)S(1)}, f32[3,2,128,256]{3,2,1,0:T(8,128)S(1)}, u32[]{:S(2)}, u32[]{:S(2)}) %collective-permute-start.5) | collective-permute-done | bytes 786464 | tf_op jit(solution)/shard_map/ppermute | solution.py:57
  33.9 53.1 %all-to-all-done.vt = f32[8,49,16,256]{3,2,1,0:T(8,128)} async-done(((f32[8,49,16,256]{3,2,1,0:T(8,128)}), f32[8,49,16,256]{3,2,1,0:T(8,128)}, u32[]{:S(2)}, u32[]{:S(2)}) %all-to-all-start) | async-done | bytes 6422560 | tf_op jit(solution)/shard_map/all_to_all | solution.py:864
  90.0 5.0 %collective-permute-start.7 = (f32[40,16,256]{2,1,0:T(8,128)S(1)}, f32[40,16,256]{2,1,0:T(8,128)S(1)}, u32[]{:S(2)}, u32[]{:S(2)}) collective-permute-start(f32[40,16,256]{2,1,0:T(8,128)S(1)} %get-tuple-element.37), channel_id=1, source_target_pairs={{8,16},{16,8},{24,32},{32,24},{40,48},{48,40},{56,64},{64,56},{72,... | collective-permute-start | bytes 1966088 | tf_op jit(solution)/shard_map/ppermute | solution.py:57
  95.1 10.5 %collective-permute-done.7.rb.vb = f32[40,16,256]{2,1,0:T(8,128)S(1)} collective-permute-done((f32[40,16,256]{2,1,0:T(8,128)S(1)}, f32[40,16,256]{2,1,0:T(8,128)S(1)}, u32[]{:S(2)}, u32[]{:S(2)}) %collective-permute-start.7) | collective-permute-done | bytes 655392 | tf_op jit(solution)/shard_map/ppermute | solution.py:57
  108.3 21.0 %collective-permute-start.8 = (f32[3,26,8,256]{3,2,1,0:T(8,128)S(1)}, f32[3,26,8,256]{3,2,1,0:T(8,128)S(1)}, u32[]{:S(2)}, u32[]{:S(2)}) collective-permute-start(f32[3,26,8,256]{3,2,1,0:T(8,128)S(1)} %get-tuple-element.38), channel_id=1, source_target_pairs={{0,1},{1,0},{2,3},{3,2},{4,5},{5,4},{6,7},{7,6},{8,9},{9,8},{10,11... | collective-permute-start | bytes 1916936 | tf_op jit(solution)/shard_map/ppermute | solution.py:57
  132.9 5.3 %collective-permute-start.14 = (f32[3,22,8,256]{3,2,1,0:T(8,128)S(1)}, f32[3,22,8,256]{3,2,1,0:T(8,128)S(1)}, u32[]{:S(2)}, u32[]{:S(2)}) collective-permute-start(f32[3,22,8,256]{3,2,1,0:T(8,128)S(1)} %get-tuple-element.46), channel_id=1, source_target_pairs={{0,1},{1,0},{2,3},{3,2},{4,5},{5,4},{6,7},{7,6},{8,9},{9,8},{10,11... | collective-permute-start | bytes 1622024 | tf_op jit(solution)/shard_map/ppermute | solution.py:57
  138.9 5.5 %collective-permute-done.8.yc = f32[3,26,8,256]{3,2,1,0:T(8,128)S(1)} collective-permute-done((f32[3,26,8,256]{3,2,1,0:T(8,128)S(1)}, f32[3,26,8,256]{3,2,1,0:T(8,128)S(1)}, u32[]{:S(2)}, u32[]{:S(2)}) %collective-permute-start.8) | collective-permute-done | bytes 639008 | tf_op jit(solution)/shard_map/ppermute | solution.py:57
  144.4 7.0 %shard_map.68 = (f32[8,2,16,16,256]{4,3,2,1,0:T(8,128)S(1)}, f32[4,16,256]{2,1,0:T(8,128)S(1)}, f32[4,16,256]{2,1,0:T(8,128)S(1)}, f32[16,16,256]{2,1,0:T(8,128)S(1)}, f32[4,3,24,24,256]{4,3,2,1,0:T(8,128)S(1)}) custom-call(s32[8]{0:T(128)S(1)} %stack.21.info, f32[16,16,256]{2,1,0:T(8,128)S(1)} %shard_map.65.tile.refs_0_, ...), custom_call_target="tpu_custom_call" | custom-call | tf_op jit(solution)/shard_map/pallas_call | solution.py:449
  151.5 5.6 %collective-permute-start.11 = (f32[4,16,256]{2,1,0:T(8,128)S(1)}, f32[4,16,256]{2,1,0:T(8,128)S(1)}, u32[]{:S(2)}, u32[]{:S(2)}) collective-permute-start(f32[4,16,256]{2,1,0:T(8,128)S(1)} %get-tuple-element.42), channel_id=1, source_target_pairs={{8,16},{16,8},{24,32},{32,24},{40,48},{48,40},{56,64},{64,56},{72,... | collective-permute-start | bytes 196616 | tf_op jit(solution)/shard_map/ppermute | solution.py:57
  161.4 6.0 %collective-permute-start.12 = (f32[12,8,256]{2,1,0:T(8,128)S(1)}, f32[12,8,256]{2,1,0:T(8,128)S(1)}, u32[]{:S(2)}, u32[]{:S(2)}) collective-permute-start(f32[12,8,256]{2,1,0:T(8,128)S(1)} %get-tuple-element.44), channel_id=1, source_target_pairs={{0,1},{1,0},{2,3},{3,2},{4,5},{5,4},{6,7},{7,6},{8,9},{9,8},{10,11... | collective-permute-start | bytes 294920 | tf_op jit(solution)/shard_map/ppermute | solution.py:57
  171.5 9.6 %shard_map.72 = (f32[8,2,16,16,256]{4,3,2,1,0:T(8,128)S(1)}, f32[4,16,24,256]{3,2,1,0:T(8,128)S(1)}, f32[10,24,256]{2,1,0:T(8,128)S(1)}, f32[10,24,256]{2,1,0:T(8,128)S(1)}) custom-call(s32[8]{0:T(128)S(1)} %stack.21.info, f32[24,16,256]{2,1,0:T(8,128)S(1)} %get-tuple-element.43.win, ...), custom_call_target="tpu_custom_call", output_to_operand_aliasing={{0}: (6, {})} | custom-call | tf_op jit(solution)/shard_map/pallas_call | solution.py:533
  181.2 6.2 %collective-permute-start.17 = (f32[10,24,256]{2,1,0:T(8,128)S(1)}, f32[10,24,256]{2,1,0:T(8,128)S(1)}, u32[]{:S(2)}, u32[]{:S(2)}) collective-permute-start(f32[10,24,256]{2,1,0:T(8,128)S(1)} %get-tuple-element.51), channel_id=1, source_target_pairs={{8,16},{16,8},{24,32},{32,24},{40,48},{48,40},{56,64},{64,56},{72,... | collective-permute-start | bytes 737288 | tf_op jit(solution)/shard_map/ppermute | solution.py:57
  187.5 4.8 %collective-permute-done.17.rb = f32[10,24,256]{2,1,0:T(8,128)S(1)} collective-permute-done((f32[10,24,256]{2,1,0:T(8,128)S(1)}, f32[10,24,256]{2,1,0:T(8,128)S(1)}, u32[]{:S(2)}, u32[]{:S(2)}) %collective-permute-start.17) | collective-permute-done | bytes 245792 | tf_op jit(solution)/shard_map/ppermute | solution.py:57
  193.1 4.9 %collective-permute-start.18 = (f32[16,8,256]{2,1,0:T(8,128)S(1)}, f32[16,8,256]{2,1,0:T(8,128)S(1)}, u32[]{:S(2)}, u32[]{:S(2)}) collective-permute-start(f32[16,8,256]{2,1,0:T(8,128)S(1)} %get-tuple-element.53), channel_id=1, source_target_pairs={{0,1},{1,0},{2,3},{3,2},{4,5},{5,4},{6,7},{7,6},{8,9},{9,8},{10,11... | collective-permute-start | bytes 393224 | tf_op jit(solution)/shard_map/ppermute | solution.py:57
  200.4 4.2 %shard_map.74 = (f32[8,2,16,16,256]{4,3,2,1,0:T(8,128)S(1)}, f32[4,16,24,256]{3,2,1,0:T(8,128)S(1)}, f32[6,24,256]{2,1,0:T(8,128)S(1)}, f32[6,24,256]{2,1,0:T(8,128)S(1)}) custom-call(s32[8]{0:T(128)S(1)} %stack.21.info, f32[4,16,24,256]{3,2,1,0:T(8,128)S(1)} %get-tuple-element.52.lw, ...), custom_call_target="tpu_custom_call", output_to_operand_aliasing={{0}: (5, {})} | custom-call | tf_op jit(solution)/shard_map/pallas_call | solution.py:630
  204.7 7.3 %collective-permute-start.21 = (f32[6,24,256]{2,1,0:T(8,128)S(1)}, f32[6,24,256]{2,1,0:T(8,128)S(1)}, u32[]{:S(2)}, u32[]{:S(2)}) collective-permute-start(f32[6,24,256]{2,1,0:T(8,128)S(1)} %get-tuple-element.59), channel_id=1, source_target_pairs={{8,16},{16,8},{24,32},{32,24},{40,48},{48,40},{56,64},{64,56},{72,... | collective-permute-start | bytes 442376 | tf_op jit(solution)/shard_map/ppermute | solution.py:57
  212.0 4.2 %collective-permute-done.21.rb = f32[6,24,256]{2,1,0:T(8,128)S(1)} collective-permute-done((f32[6,24,256]{2,1,0:T(8,128)S(1)}, f32[6,24,256]{2,1,0:T(8,128)S(1)}, u32[]{:S(2)}, u32[]{:S(2)}) %collective-permute-start.21) | collective-permute-done | bytes 147488 | tf_op jit(solution)/shard_map/ppermute | solution.py:57
  216.9 4.0 %collective-permute-start.22 = (f32[16,8,256]{2,1,0:T(8,128)S(1)}, f32[16,8,256]{2,1,0:T(8,128)S(1)}, u32[]{:S(2)}, u32[]{:S(2)}) collective-permute-start(f32[16,8,256]{2,1,0:T(8,128)S(1)} %get-tuple-element.61), channel_id=1, source_target_pairs={{0,1},{1,0},{2,3},{3,2},{4,5},{5,4},{6,7},{7,6},{8,9},{9,8},{10,11... | collective-permute-start | bytes 393224 | tf_op jit(solution)/shard_map/ppermute | solution.py:57
  226.4 56.9 %all_to_all.10.pack = f32[8,2,16,16,256]{4,3,2,1,0:T(8,128)S(1)} all-to-all(f32[8,2,16,16,256]{4,3,2,1,0:T(8,128)S(1)} %shard_map.76), channel_id=1, replica_groups=mesh['space'=16,'cuts'=8] {'cuts'}, dimensions={0} | all-to-all | bytes 8388608 | tf_op jit(solution)/shard_map/all_to_all | solution.py:889
  284.0 5.4 %collective-permute-start.25 = (f32[8,5,16,256]{3,2,1,0:T(8,128)S(1)}, f32[8,5,16,256]{3,2,1,0:T(8,128)S(1)}, u32[]{:S(2)}, u32[]{:S(2)}) collective-permute-start(f32[8,5,16,256]{3,2,1,0:T(8,128)S(1)} %get-tuple-element.73), channel_id=1, source_target_pairs={{8,16},{16,8},{24,32},{32,24},{40,48},{48,40},{56,64},{64,56},{72,... | collective-permute-start | bytes 1966088 | tf_op jit(solution)/shard_map/ppermute | solution.py:57
  293.7 15.1 %shard_map.77 = (f32[1,3,16,128,256]{4,3,2,1,0:T(8,128)}, f32[3,4,128,256]{3,2,1,0:T(8,128)S(1)}, f32[3,4,128,256]{3,2,1,0:T(8,128)S(1)}) custom-call(f32[1]{0:T(128)} %bitcast.4.weight, f32[1,3,16,128,256]{4,3,2,1,0:T(8,128)S(1)} %bitcast.25, f32[8,2,16,16,256]{4,3,2,1,0:T(8,128)S(1)} %all_to_all.10.pack), custom_call_target="tpu_custom_call" | custom-call | tf_op jit(solution)/shard_map/pallas_call | solution.py:748
  308.9 10.7 %shard_map.78 = f32[1,3,16,128,256]{4,3,2,1,0:T(8,128)} custom-call(s32[8]{0:T(128)S(1)} %stack.21.info, f32[1]{0:T(128)} %bitcast.4.weight, f32[1,3,16,128,256]{4,3,2,1,0:T(8,128)S(1)} %bitcast.25, f32[3,2,128,256]{3,2,1,0:T(8,128)S(1)} %collective-permute-done.4.refs_0_.va, ...), custom_call_target="tpu_custom_call", output_to_operand_aliasing={{}: (10, {})} | custom-call | tf_op jit(solution)/shard_map/pallas_call | solution.py:832
  (74 shorter events, 45.4 us)
Async XLA Ops:
  7.8 79.2 %all-to-all-start = ((f32[8,49,16,256]{3,2,1,0:T(8,128)}), f32[8,49,16,256]{3,2,1,0:T(8,128)}, u32[]{:S(2)}, u32[]{:S(2)}) async-start(f32[8,49,16,256]{3,2,1,0:T(8,128)} %copy-done.1), calls=%async_computation | async-start | bytes 12845056 | tf_op jit(solution)/shard_map/all_to_all | solution.py:864
  15.9 8.1 %collective-permute-start.4 = (f32[3,2,128,256]{3,2,1,0:T(8,128)}, f32[3,2,128,256]{3,2,1,0:T(8,128)S(1)}, u32[]{:S(2)}, u32[]{:S(2)}) collective-permute-start(f32[3,2,128,256]{3,2,1,0:T(8,128)} %get-tuple-element.68), channel_id=1, source_target_pairs={{0,8},{8,0},{16,24},{24,16},{32,40},{40,32},{48,56},{56,48},{64,72... | collective-permute-start | bytes 2359304 | tf_op jit(solution)/shard_map/ppermute | solution.py:57
  16.9 17.0 %collective-permute-start.5 = (f32[3,2,128,256]{3,2,1,0:T(8,128)S(1)}, f32[3,2,128,256]{3,2,1,0:T(8,128)S(1)}, u32[]{:S(2)}, u32[]{:S(2)}) collective-permute-start(f32[3,2,128,256]{3,2,1,0:T(8,128)S(1)} %get-tuple-element.67), channel_id=1, source_target_pairs={{8,16},{16,8},{24,32},{32,24},{40,48},{48,40},{56,64},{64,56},{72,... | collective-permute-start | bytes 2359304 | tf_op jit(solution)/shard_map/ppermute | solution.py:57
  89.1 6.0 %collective-permute-start.6 = (f32[40,16,256]{2,1,0:T(8,128)S(1)}, f32[40,16,256]{2,1,0:T(8,128)S(1)}, u32[]{:S(2)}, u32[]{:S(2)}) collective-permute-start(f32[40,16,256]{2,1,0:T(8,128)S(1)} %get-tuple-element.36), channel_id=1, source_target_pairs={{0,8},{8,0},{16,24},{24,16},{32,40},{40,32},{48,56},{56,48},{64,72... | collective-permute-start | bytes 1966088 | tf_op jit(solution)/shard_map/ppermute | solution.py:57
  90.0 15.5 %collective-permute-start.7 = (f32[40,16,256]{2,1,0:T(8,128)S(1)}, f32[40,16,256]{2,1,0:T(8,128)S(1)}, u32[]{:S(2)}, u32[]{:S(2)}) collective-permute-start(f32[40,16,256]{2,1,0:T(8,128)S(1)} %get-tuple-element.37), channel_id=1, source_target_pairs={{8,16},{16,8},{24,32},{32,24},{40,48},{48,40},{56,64},{64,56},{72,... | collective-permute-start | bytes 1966088 | tf_op jit(solution)/shard_map/ppermute | solution.py:57
  108.3 36.0 %collective-permute-start.8 = (f32[3,26,8,256]{3,2,1,0:T(8,128)S(1)}, f32[3,26,8,256]{3,2,1,0:T(8,128)S(1)}, u32[]{:S(2)}, u32[]{:S(2)}) collective-permute-start(f32[3,26,8,256]{3,2,1,0:T(8,128)S(1)} %get-tuple-element.38), channel_id=1, source_target_pairs={{0,1},{1,0},{2,3},{3,2},{4,5},{5,4},{6,7},{7,6},{8,9},{9,8},{10,11... | collective-permute-start | bytes 1916936 | tf_op jit(solution)/shard_map/ppermute | solution.py:57
  129.4 15.0 %collective-permute-start.9 = (f32[3,26,8,256]{3,2,1,0:T(8,128)S(1)}, f32[3,26,8,256]{3,2,1,0:T(8,128)S(1)}, u32[]{:S(2)}, u32[]{:S(2)}) collective-permute-start(f32[3,26,8,256]{3,2,1,0:T(8,128)S(1)} %get-tuple-element.39), channel_id=1, source_target_pairs={{1,2},{2,1},{3,4},{4,3},{5,6},{6,5},{9,10},{10,9},{11,12},{12,11},... | collective-permute-start | bytes 1916936 | tf_op jit(solution)/shard_map/ppermute | solution.py:57
  132.9 35.9 %collective-permute-start.14 = (f32[3,22,8,256]{3,2,1,0:T(8,128)S(1)}, f32[3,22,8,256]{3,2,1,0:T(8,128)S(1)}, u32[]{:S(2)}, u32[]{:S(2)}) collective-permute-start(f32[3,22,8,256]{3,2,1,0:T(8,128)S(1)} %get-tuple-element.46), channel_id=1, source_target_pairs={{0,1},{1,0},{2,3},{3,2},{4,5},{5,4},{6,7},{7,6},{8,9},{9,8},{10,11... | collective-permute-start | bytes 1622024 | tf_op jit(solution)/shard_map/ppermute | solution.py:57
  138.2 30.5 %collective-permute-start.15 = (f32[3,22,8,256]{3,2,1,0:T(8,128)S(1)}, f32[3,22,8,256]{3,2,1,0:T(8,128)S(1)}, u32[]{:S(2)}, u32[]{:S(2)}) collective-permute-start(f32[3,22,8,256]{3,2,1,0:T(8,128)S(1)} %get-tuple-element.47), channel_id=1, source_target_pairs={{1,2},{2,1},{3,4},{4,3},{5,6},{6,5},{9,10},{10,9},{11,12},{12,11},... | collective-permute-start | bytes 1622024 | tf_op jit(solution)/shard_map/ppermute | solution.py:57
  151.4 7.8 %collective-permute-start.10 = (f32[4,16,256]{2,1,0:T(8,128)S(1)}, f32[4,16,256]{2,1,0:T(8,128)S(1)}, u32[]{:S(2)}, u32[]{:S(2)}) collective-permute-start(f32[4,16,256]{2,1,0:T(8,128)S(1)} %get-tuple-element.41), channel_id=1, source_target_pairs={{0,8},{8,0},{16,24},{24,16},{32,40},{40,32},{48,56},{56,48},{64,72... | collective-permute-start | bytes 196616 | tf_op jit(solution)/shard_map/ppermute | solution.py:57
  151.5 9.2 %collective-permute-start.11 = (f32[4,16,256]{2,1,0:T(8,128)S(1)}, f32[4,16,256]{2,1,0:T(8,128)S(1)}, u32[]{:S(2)}, u32[]{:S(2)}) collective-permute-start(f32[4,16,256]{2,1,0:T(8,128)S(1)} %get-tuple-element.42), channel_id=1, source_target_pairs={{8,16},{16,8},{24,32},{32,24},{40,48},{48,40},{56,64},{64,56},{72,... | collective-permute-start | bytes 196616 | tf_op jit(solution)/shard_map/ppermute | solution.py:57
  159.2 8.9 %collective-permute-start = (f32[1,128]{1,0:T(1,128)S(1)}, f32[1,128]{1,0:T(1,128)S(1)}, u32[]{:S(2)}, u32[]{:S(2)}) collective-permute-start(f32[1,128]{1,0:T(1,128)S(1)} %broadcast_in_dim.3), channel_id=1, source_target_pairs={{0,8},{8,0},{16,24},{24,16},{32,40},{40,32},{48,56},{56,48},{64,72... | collective-permute-start | bytes 1544 | tf_op jit(solution)/shard_map/ppermute | solution.py:62
  161.4 10.1 %collective-permute-start.12 = (f32[12,8,256]{2,1,0:T(8,128)S(1)}, f32[12,8,256]{2,1,0:T(8,128)S(1)}, u32[]{:S(2)}, u32[]{:S(2)}) collective-permute-start(f32[12,8,256]{2,1,0:T(8,128)S(1)} %get-tuple-element.44), channel_id=1, source_target_pairs={{0,1},{1,0},{2,3},{3,2},{4,5},{5,4},{6,7},{7,6},{8,9},{9,8},{10,11... | collective-permute-start | bytes 294920 | tf_op jit(solution)/shard_map/ppermute | solution.py:57
  181.1 6.4 %collective-permute-start.16 = (f32[10,24,256]{2,1,0:T(8,128)S(1)}, f32[10,24,256]{2,1,0:T(8,128)S(1)}, u32[]{:S(2)}, u32[]{:S(2)}) collective-permute-start(f32[10,24,256]{2,1,0:T(8,128)S(1)} %get-tuple-element.50), channel_id=1, source_target_pairs={{0,8},{8,0},{16,24},{24,16},{32,40},{40,32},{48,56},{56,48},{64,72... | collective-permute-start | bytes 737288 | tf_op jit(solution)/shard_map/ppermute | solution.py:57
  181.2 11.1 %collective-permute-start.17 = (f32[10,24,256]{2,1,0:T(8,128)S(1)}, f32[10,24,256]{2,1,0:T(8,128)S(1)}, u32[]{:S(2)}, u32[]{:S(2)}) collective-permute-start(f32[10,24,256]{2,1,0:T(8,128)S(1)} %get-tuple-element.51), channel_id=1, source_target_pairs={{8,16},{16,8},{24,32},{32,24},{40,48},{48,40},{56,64},{64,56},{72,... | collective-permute-start | bytes 737288 | tf_op jit(solution)/shard_map/ppermute | solution.py:57
  187.4 11.3 %collective-permute-start.1 = (f32[1,128]{1,0:T(1,128)S(1)}, f32[1,128]{1,0:T(1,128)S(1)}, u32[]{:S(2)}, u32[]{:S(2)}) collective-permute-start(f32[1,128]{1,0:T(1,128)S(1)} %broadcast_add_fusion.refs_0_), channel_id=1, source_target_pairs={{0,16},{8,24},{16,0},{24,8},{32,48},{40,56},{48,32},{56,40},{64,80... | collective-permute-start | bytes 1544 | tf_op jit(solution)/shard_map/ppermute | solution.py:62
  193.1 7.3 %collective-permute-start.18 = (f32[16,8,256]{2,1,0:T(8,128)S(1)}, f32[16,8,256]{2,1,0:T(8,128)S(1)}, u32[]{:S(2)}, u32[]{:S(2)}) collective-permute-start(f32[16,8,256]{2,1,0:T(8,128)S(1)} %get-tuple-element.53), channel_id=1, source_target_pairs={{0,1},{1,0},{2,3},{3,2},{4,5},{5,4},{6,7},{7,6},{8,9},{9,8},{10,11... | collective-permute-start | bytes 393224 | tf_op jit(solution)/shard_map/ppermute | solution.py:57
  204.6 7.4 %collective-permute-start.20 = (f32[6,24,256]{2,1,0:T(8,128)S(1)}, f32[6,24,256]{2,1,0:T(8,128)S(1)}, u32[]{:S(2)}, u32[]{:S(2)}) collective-permute-start(f32[6,24,256]{2,1,0:T(8,128)S(1)} %get-tuple-element.58), channel_id=1, source_target_pairs={{0,8},{8,0},{16,24},{24,16},{32,40},{40,32},{48,56},{56,48},{64,72... | collective-permute-start | bytes 442376 | tf_op jit(solution)/shard_map/ppermute | solution.py:57
  204.7 11.5 %collective-permute-start.21 = (f32[6,24,256]{2,1,0:T(8,128)S(1)}, f32[6,24,256]{2,1,0:T(8,128)S(1)}, u32[]{:S(2)}, u32[]{:S(2)}) collective-permute-start(f32[6,24,256]{2,1,0:T(8,128)S(1)} %get-tuple-element.59), channel_id=1, source_target_pairs={{8,16},{16,8},{24,32},{32,24},{40,48},{48,40},{56,64},{64,56},{72,... | collective-permute-start | bytes 442376 | tf_op jit(solution)/shard_map/ppermute | solution.py:57
  216.9 8.6 %collective-permute-start.22 = (f32[16,8,256]{2,1,0:T(8,128)S(1)}, f32[16,8,256]{2,1,0:T(8,128)S(1)}, u32[]{:S(2)}, u32[]{:S(2)}) collective-permute-start(f32[16,8,256]{2,1,0:T(8,128)S(1)} %get-tuple-element.61), channel_id=1, source_target_pairs={{0,1},{1,0},{2,3},{3,2},{4,5},{5,4},{6,7},{7,6},{8,9},{9,8},{10,11... | collective-permute-start | bytes 393224 | tf_op jit(solution)/shard_map/ppermute | solution.py:57
  220.9 4.6 %collective-permute-start.23 = (f32[16,8,256]{2,1,0:T(8,128)S(1)}, f32[16,8,256]{2,1,0:T(8,128)S(1)}, u32[]{:S(2)}, u32[]{:S(2)}) collective-permute-start(f32[16,8,256]{2,1,0:T(8,128)S(1)} %get-tuple-element.62), channel_id=1, source_target_pairs={{1,2},{2,1},{3,4},{4,3},{5,6},{6,5},{9,10},{10,9},{11,12},{12,11},... | collective-permute-start | bytes 393224 | tf_op jit(solution)/shard_map/ppermute | solution.py:57
  283.6 25.3 %collective-permute-start.24 = (f32[8,5,16,256]{3,2,1,0:T(8,128)S(1)}, f32[8,5,16,256]{3,2,1,0:T(8,128)S(1)}, u32[]{:S(2)}, u32[]{:S(2)}) collective-permute-start(f32[8,5,16,256]{3,2,1,0:T(8,128)S(1)} %get-tuple-element.74), channel_id=1, source_target_pairs={{0,8},{8,0},{16,24},{24,16},{32,40},{40,32},{48,56},{56,48},{64,72... | collective-permute-start | bytes 1966088 | tf_op jit(solution)/shard_map/ppermute | solution.py:57
  284.0 24.9 %collective-permute-start.25 = (f32[8,5,16,256]{3,2,1,0:T(8,128)S(1)}, f32[8,5,16,256]{3,2,1,0:T(8,128)S(1)}, u32[]{:S(2)}, u32[]{:S(2)}) collective-permute-start(f32[8,5,16,256]{3,2,1,0:T(8,128)S(1)} %get-tuple-element.73), channel_id=1, source_target_pairs={{8,16},{16,8},{24,32},{32,24},{40,48},{48,40},{56,64},{64,56},{72,... | collective-permute-start | bytes 1966088 | tf_op jit(solution)/shard_map/ppermute | solution.py:57
  289.4 4.2 %collective-permute-start.3 = (f32[1,128]{1,0:T(1,128)S(1)}, f32[1,128]{1,0:T(1,128)S(1)}, u32[]{:S(2)}, u32[]{:S(2)}) collective-permute-start(f32[1,128]{1,0:T(1,128)S(1)} %add.23.refs_0_), channel_id=1, source_target_pairs={{0,64},{8,72},{16,80},{24,88},{32,96},{40,104},{48,112},{56,120},{... | collective-permute-start | bytes 1544 | tf_op jit(solution)/shard_map/ppermute | solution.py:62
  (11 other events, 196.6 us)

commit v3 on v2

v3 whole, which is shorter than its diff:
```python
import functools

import jax
import jax.numpy as jnp
from jax import lax
from jax.experimental import pallas as pl
from jax.experimental.pallas import tpu as pltpu
from jax.sharding import PartitionSpec as P

F32 = jnp.float32
NT = 8
STEP = 1.0 / NT
DATA_WEIGHT = 4.0
KAPPA = 0.125
CX, CY, NZ = 16, 16, 256
NY = 128
DEPTH = 4
WX, WY = CX + 2 * DEPTH, CY + 2 * DEPTH
V_SLOTS = ((0, 3, 0), (1, 2, 3), (2, 1, 5))
V_ROWS = 6
VX = CX + 6
VBLOCKS = 3 * CX
PBLOCKS = 2 * CX + 1
HALF = VBLOCKS // 2
RING = 4
FACE = 3 * V_ROWS
VMEM = pltpu.VMEM
ANY = pl.ANY


def whole():
    return pl.BlockSpec(memory_space=VMEM)


def anywhere():
    return pl.BlockSpec(memory_space=ANY)


def hbm():
    return pl.BlockSpec(memory_space=pltpu.HBM)


def scalars():
    return pl.BlockSpec(memory_space=pltpu.SMEM)


def params(mib=16):
    return pltpu.CompilerParams(vmem_limit_bytes=mib * 1024 * 1024)


def sds(*shape):
    return jax.ShapeDtypeStruct(shape, F32)


def swaps(size, first):
    pairs = []
    for i in range(first, size - 1, 2):
        pairs += [(i, i + 1), (i + 1, i)]
    return pairs


def swap(even, odd, axis):
    size = lax.axis_size(axis)
    return lax.ppermute(even, axis, swaps(size, 0)), lax.ppermute(odd, axis, swaps(size, 1))


def xor_swap(value, reach):
    size = lax.axis_size("space")
    return value + lax.ppermute(value, "space", [(i, i ^ reach) for i in range(size)])


def rows8():
    return lax.broadcasted_iota(jnp.int32, (8, NZ), 0)


def turn(block, shift):
    shift = shift % 8
    return pltpu.roll(block, shift, 0) if shift else block


def put(total, block, shift, low, high, sub):
    return jnp.where((sub >= low) & (sub < high), turn(block, shift), total)


def pack_edges(slots, tile, sub):
    top = jnp.zeros((8, NZ), F32)
    bottom = top
    for key, k, off in slots:
        low8, high8 = tile(key)
        top = put(top, high8, off + k, off, off + k, sub)
        bottom = put(bottom, low8, off, off, off + k, sub)
    return top, bottom


def halo_block(above, below, k, off, sub):
    block = put(jnp.zeros((8, NZ), F32), above, -off, 0, k, sub)
    return put(block, below, 8 - k - off, 8 - k, 8, sub)


def lane_masks(shape):
    z = lax.broadcasted_iota(jnp.int32, shape, 1)
    return z == 0, z == NZ - 1


def copies(pairs, sem):
    started = [pltpu.make_async_copy(a, b, sem.at[i]) for i, (a, b) in enumerate(pairs)]
    for copy in started:
        copy.start()
    return started


def wait_all(started):
    for copy in started:
        copy.wait()


def fill_velocity(group, info, vt, ra, rb, yc, yd, vw, sem):
    px, py = info[2], info[3]
    pairs = []
    for d in range(3):
        for j in range(4):
            pairs.append((vt.at[4 * group + j, d * CX : (d + 1) * CX], vw.at[j, d, 0:CX, 0:CY]))
        for j, k, off in V_SLOTS:
            to_a = jnp.where(px == 0, CX, WX - k)
            to_b = jnp.where(px == 0, WX - k, CX)
            row = d * V_ROWS + off
            pairs.append((ra.at[row : row + k], vw.at[j, d, pl.ds(to_a, k), 0:CY]))
            pairs.append((rb.at[row : row + k], vw.at[j, d, pl.ds(to_b, k), 0:CY]))
    started = copies(pairs, sem)
    sub = rows8()
    zero_row = jnp.zeros((WY, NZ), F32)
    zero_tile = jnp.zeros((8, NZ), F32)
    for j in range(4):
        k = 3 - j
        for d in range(3):
            for x in range(CX + k, WX - k):
                vw[j, d, x] = zero_row

    def blocks(d, i, x, keep):
        c, e = yc[d, i], yd[d, i]
        above = jnp.where(py == 0, c, e)
        below = jnp.where(py == 0, e, c)
        for j, k, off in V_SLOTS:
            if keep(k):
                vw[j, d, x, CY:WY] = halo_block(above, below, k, off, sub)

    def one(i, carry):
        for d in range(3):
            for r in range(2):
                blocks(d, 2 * i + r, 2 * i + r, lambda k: True)
                vw[3, d, 2 * i + r, CY:WY] = zero_tile
        return carry

    lax.fori_loop(0, CX // 2, one, 0)
    for i in range(CX, VX):
        x = i if i < CX + 3 else i + 2
        for d in range(3):
            blocks(d, i, x, lambda k: x < CX + k or x >= WX - k)
    return started


FILL_COPIES = 30


def fill_image(info, win, yc, yd, image):
    py = info[3]
    sub = rows8()

    def one(i, carry):
        c, e = yc[i], yd[i]
        above = jnp.where(py == 0, c, e)
        below = jnp.where(py == 0, e, c)
        image[i, 0:CY] = win[i]
        image[i + 12, 0:CY] = win[i + 12]
        image[i, CY:WY] = halo_block(above, below, 4, 0, sub)
        image[i + 12, CY:WY] = halo_block(above, below, 4, 4, sub)
        return carry

    lax.fori_loop(0, 12, one, 0)


ROWS = 2


def sweep_rows(reach, row, dst):
    turns = -(-(CX + 2 * reach) // ROWS)

    def one(i, carry):
        xs = [lax.rem(i * ROWS + r - reach + WX, WX) for r in range(ROWS)]
        values = [row(x, lax.rem(x + WX - 1, WX), lax.rem(x + 1, WX)) for x in xs]
        for x, value in zip(xs, values):
            dst[x] = value
        return carry

    lax.fori_loop(0, turns, one, 0)


def advance(src, dst, vw, j, reach):
    first, last = lane_masks((WY, NZ))

    def row(x, xm, xp):
        c = src[x]
        v0, v1, v2 = vw[j, 0, x], vw[j, 1, x], vw[j, 2, x]
        flow = v0 * jnp.where(v0 > 0.0, c - src[xm], src[xp] - c)
        flow += v1 * jnp.where(v1 > 0.0, c - pltpu.roll(c, 1, 0), pltpu.roll(c, WY - 1, 0) - c)
        behind = jnp.where(first, 0.0, pltpu.roll(c, 1, 1))
        beyond = jnp.where(last, 0.0, pltpu.roll(c, NZ - 1, 1))
        flow += v2 * jnp.where(v2 > 0.0, c - behind, beyond - c)
        return c - STEP * flow

    sweep_rows(reach, row, dst)


def scatter(src, dst, vw, j, reach):
    first, last = lane_masks((WY, NZ))

    def row(x, xm, xp):
        c = src[x]
        v0, v1, v2 = vw[j, 0, x], vw[j, 1, x], vw[j, 2, x]
        change = (jnp.abs(v0) + jnp.abs(v1) + jnp.abs(v2)) * c
        change -= jnp.maximum(vw[j, 0, xp], 0.0) * src[xp]
        change += jnp.minimum(vw[j, 0, xm], 0.0) * src[xm]
        change -= pltpu.roll(jnp.maximum(v1, 0.0) * c, WY - 1, 0)
        change += pltpu.roll(jnp.minimum(v1, 0.0) * c, 1, 0)
        change -= jnp.where(last, 0.0, pltpu.roll(jnp.maximum(v2, 0.0) * c, NZ - 1, 1))
        change += jnp.where(first, 0.0, pltpu.roll(jnp.minimum(v2, 0.0) * c, 1, 1))
        return c - STEP * change

    sweep_rows(reach, row, dst)


def clear_halo(ref, x_rows=True):
    zero_row = jnp.zeros((WY, NZ), F32)
    for x in range(CX, WX):
        ref[x] = zero_row


def ring_pairs(up, across, size):
    pairs = []
    for i in range(size):
        ring, at = divmod(i, RING)
        pairs.append((i, ((ring + across) % 2) * RING + (at + up) % RING))
    return pairs


def shift(value, up, across):
    return lax.ppermute(value, "cuts", ring_pairs(up, across, lax.axis_size("cuts")))


DIRECT = ((1, 1), (-1, 1), (0, 1), (1, 0), (-1, 0))


def repack(info, velocity):
    def kernel(info, src, far_a, far_b, *refs):
        direct, own = refs[:5], refs[5]
        held, isem, osem = refs[6:]
        ring, at = lax.div(info[1], RING), lax.rem(info[1], RING)

        def start_in(n, up, across):
            c = lax.rem(ring + across, 2) * RING + lax.rem(at + up + RING, RING)
            rows = pl.ds(pl.multiple_of(c * CY, CY), CY)
            for d in range(3):
                copy = pltpu.make_async_copy(src.at[0, d, :, rows], held.at[n, d * CX : (d + 1) * CX], isem.at[n * 3 + d])
                copy.start()
                arrive[n].append(copy)

        order = ((2, 0), (2, 1)) + DIRECT + ((0, 0),)
        arrive = [[] for _ in order]
        for n, (up, across) in enumerate(order):
            start_in(n, up, across)
        leave = []
        for n in range(8):
            wait_all(arrive[n])
            if n < 2:
                pairs = [(held.at[n, 0:HALF], far_a.at[n]), (held.at[n, HALF:VBLOCKS], far_b.at[n])]
            else:
                pairs = [(held.at[n], direct[n - 2] if n < 7 else own)]
            for source, target in pairs:
                copy = pltpu.make_async_copy(source, target, osem.at[len(leave)])
                copy.start()
                leave.append(copy)
        wait_all(leave)

    return pl.pallas_call(
        kernel,
        out_shape=[sds(2, HALF, CY, NZ)] * 2 + [sds(VBLOCKS, CY, NZ)] * 6,
        in_specs=[scalars(), hbm()],
        out_specs=[anywhere()] * 8,
        scratch_shapes=[
            VMEM((8, VBLOCKS, CY, NZ), F32),
            pltpu.SemaphoreType.DMA((24,)),
            pltpu.SemaphoreType.DMA((10,)),
        ],
        compiler_params=params(60),
    )(info, velocity)


def spread(far_a, far_b, direct):
    far_a, far_b = shift(far_a, 1, 0), shift(far_b, -1, 0)
    got = [shift(block, up, across) for block, (up, across) in zip(direct, DIRECT)]
    a = [shift(far_a[n], 1, n) for n in range(2)]
    b = [shift(far_b[n], -1, n) for n in range(2)]
    return got + a + b, far_a


def origins(info):
    ring, at = lax.div(info[1], RING), lax.rem(info[1], RING)
    moves = DIRECT + ((2, 0), (2, 1), (2, 0), (2, 1))
    return [lax.rem(ring + across, 2) * RING + lax.rem(at - up + RING, RING) for up, across in moves]


def template(info, table, atlas, labels, velocity, *before):
    def kernel(info, table, atlas, labels, velocity, *refs):
        tmpl, ea, eb, sem = refs[len(before) :]
        px = info[2]
        top, bottom = jnp.where(px == 0, CX - 2, 0), jnp.where(px == 0, 0, CX - 2)
        started = copies([(velocity.at[0, :, pl.ds(top, 2)], ea), (velocity.at[0, :, pl.ds(bottom, 2)], eb)], sem)

        def one(x, carry):
            lab = labels[x]
            value = jnp.zeros((CY, NZ), F32)
            for l in range(64):
                value = jnp.where(lab == l, table[l], value)
            tmpl[x] = atlas[x] + value
            return carry

        lax.fori_loop(0, CX, one, 0)
        wait_all(started)

    return pl.pallas_call(
        kernel,
        out_shape=[sds(CX, CY, NZ), sds(3, 2, NY, NZ), sds(3, 2, NY, NZ)],
        in_specs=[scalars(), scalars(), whole(), whole(), hbm()] + [anywhere()] * len(before),
        out_specs=[whole()] * 3,
        scratch_shapes=[pltpu.SemaphoreType.DMA((2,))],
        compiler_params=params(),
    )(info, table, atlas, labels, velocity, *before)


def image_edges(info, tile, ra, rb):
    def kernel(info, tile, ra, rb, win, ec, ed):
        px, py = info[2], info[3]
        win[0:CX] = tile[...]
        win[pl.ds(jnp.where(px == 0, CX, WX - DEPTH), DEPTH)] = ra[...]
        win[pl.ds(jnp.where(px == 0, WX - DEPTH, CX), DEPTH)] = rb[...]
        sub = rows8()

        def one(i, carry):
            def tile_of(key):
                return win[i + key, 0:8], win[i + key, 8:16]

            top, bottom = pack_edges(((0, 4, 0), (12, 4, 4)), tile_of, sub)
            ec[i] = jnp.where(py == 0, top, bottom)
            ed[i] = jnp.where(py == 0, bottom, top)
            return carry

        lax.fori_loop(0, 12, one, 0)

    return pl.pallas_call(
        kernel,
        out_shape=[sds(WX, CY, NZ), sds(12, 8, NZ), sds(12, 8, NZ)],
        in_specs=[scalars()] + [whole()] * 3,
        out_specs=[whole()] * 3,
        compiler_params=params(),
    )(info, tile, ra, rb)


def faces(info, own, got, tile, *before):
    def kernel(info, own, *refs):
        got, tile = refs[:9], refs[9]
        vt, ea, eb, la, lb, count, isem, sem = refs[10 + len(before) :]
        count[...] = jnp.full((8, NZ), info[4], jnp.int32).astype(F32)
        px = info[2]
        started = [pltpu.make_async_copy(own, vt.at[info[1]], isem.at[9])]
        for n, (block, t) in enumerate(zip(got, origins(info))):
            if n < 5:
                target = vt.at[t]
            else:
                target = vt.at[t, 0:HALF] if n < 7 else vt.at[t, HALF:VBLOCKS]
            started.append(pltpu.make_async_copy(block, target, isem.at[n]))
        for copy in started:
            copy.start()
        ea[FACE : FACE + DEPTH] = tile[pl.ds(jnp.where(px == 0, CX - DEPTH, 0), DEPTH)]
        eb[FACE : FACE + DEPTH] = tile[pl.ds(jnp.where(px == 0, 0, CX - DEPTH), DEPTH)]
        wait_all(started)
        for g, (to_a, to_b) in enumerate(((ea, eb), (la, lb))):
            for d in range(3):
                for j, k, off in V_SLOTS:
                    top = jnp.where(px == 0, CX - k, 0) + d * CX
                    bottom = jnp.where(px == 0, 0, CX - k) + d * CX
                    row = d * V_ROWS + off
                    to_a[row : row + k] = vt[4 * g + j, pl.ds(top, k)]
                    to_b[row : row + k] = vt[4 * g + j, pl.ds(bottom, k)]

    return pl.pallas_call(
        kernel,
        out_shape=[sds(NT, VBLOCKS, CY, NZ)] + [sds(FACE + DEPTH, CY, NZ)] * 2 + [sds(FACE, CY, NZ)] * 2 + [sds(8, NZ)],
        in_specs=[scalars()] + [anywhere()] * 10 + [whole()] + [anywhere()] * len(before),
        out_specs=[whole()] * 6,
        scratch_shapes=[pltpu.SemaphoreType.DMA((10,)), pltpu.SemaphoreType.DMA((36,))],
        compiler_params=params(),
    )(info, own, *got, tile, *before)


def velocity_edges(info, vt, ra, rb, group, tile=None):
    with_image = tile is not None
    rows = VX + 4 if with_image else VX

    def kernel(info, vt, ra, rb, *refs):
        ec, ed = refs[-2:]
        px, py = info[2], info[3]
        sub = rows8()

        def emit(d, i, slots, tile_of):
            top, bottom = pack_edges(slots, tile_of, sub)
            ec[d, i] = jnp.where(py == 0, top, bottom)
            ed[d, i] = jnp.where(py == 0, bottom, top)

        def halves(value):
            return value[0:8], value[8:16]

        def one(i, carry):
            d, x = lax.div(i, CX // 2), 2 * lax.rem(i, CX // 2)
            for r in range(2):
                row = d * CX + x + r
                emit(d, x + r, V_SLOTS, lambda j: (vt[4 * group + j, row, 0:8], vt[4 * group + j, row, 8:16]))
            return carry

        lax.fori_loop(0, 3 * CX // 2, one, 0)
        for d in range(3):
            base = d * V_ROWS
            for i in range(3):
                up, down = [], []
                for j, k, off in V_SLOTS:
                    if i < k:
                        up.append((j, k, off))
                    if i >= 3 - k:
                        down.append((j, k, off))

                def tile_up(j):
                    row = base + V_SLOTS[j][2] + i
                    return halves(jnp.where(px == 0, ra[row], rb[row]))

                def tile_down(j):
                    row = base + V_SLOTS[j][2] + i - (3 - V_SLOTS[j][1])
                    return halves(jnp.where(px == 0, rb[row], ra[row]))

                emit(d, CX + i, up, tile_up)
                emit(d, CX + 3 + i, down, tile_down)
            if with_image:
                own = refs[0]
                for i in range(4):
                    a, b = ra[FACE + i], rb[FACE + i]
                    other = own[12 + i] if d == 0 else jnp.where(px == d - 1, a, b)
                    pair = (halves(own[4 * d + i]), halves(other))
                    emit(d, VX + i, ((0, 4, 0), (1, 4, 4)), lambda key: pair[key])

    return pl.pallas_call(
        kernel,
        out_shape=[sds(3, rows, 8, NZ)] * 2,
        in_specs=[scalars()] + [whole()] * (4 if with_image else 3),
        out_specs=[whole()] * 2,
        compiler_params=params(),
    )(info, vt, ra, rb, *((tile,) if with_image else ()))


def forward_first(info, tile, vt, ra, rb, yc, yd):
    def kernel(info, tile, vt, ra, rb, yc, yd, pack, ea, eb, i4, vw, image, halos, hsem, sem, osem):
        px, py = info[2], info[3]
        pair = copies([(ra.at[FACE : FACE + DEPTH], halos.at[0]), (rb.at[FACE : FACE + DEPTH], halos.at[1])], hsem)
        started = fill_velocity(0, info, vt, ra, rb, yc, yd, vw, sem)
        image[0, 0:CX, 0:CY] = tile[...]
        wait_all(pair)
        image[0, pl.ds(jnp.where(px == 0, CX, WX - DEPTH), DEPTH), 0:CY] = halos[0]
        image[0, pl.ds(jnp.where(px == 0, WX - DEPTH, CX), DEPTH), 0:CY] = halos[1]
        sub = rows8()
        for j in range(12):
            c, e = yc[j // 4, VX + j % 4], yd[j // 4, VX + j % 4]
            above = jnp.where(py == 0, c, e)
            below = jnp.where(py == 0, e, c)
            image[0, j, CY:WY] = halo_block(above, below, 4, 0, sub)
            image[0, j + 12, CY:WY] = halo_block(above, below, 4, 4, sub)
        wait_all(started)
        out = []
        for j in range(4):
            advance(image.at[j], image.at[j + 1], vw, j, 3 - j)
            out.append(pltpu.make_async_copy(image.at[j, 0:CX, 0:CY], pack.at[j, 0:CX], osem.at[j]))
            out[-1].start()
        last = image.at[4]
        i4[...] = last[0:CX, 0:CY]
        ea[...] = last[pl.ds(jnp.where(px == 0, CX - DEPTH, 0), DEPTH), 0:CY]
        eb[...] = last[pl.ds(jnp.where(px == 0, 0, CX - DEPTH), DEPTH), 0:CY]
        wait_all(out)

    return pl.pallas_call(
        kernel,
        out_shape=[
            sds(NT, PBLOCKS, CY, NZ),
            sds(DEPTH, CY, NZ),
            sds(DEPTH, CY, NZ),
            sds(CX, CY, NZ),
            sds(4, 3, WX, WY, NZ),
        ],
        in_specs=[scalars()] + [whole()] * 6,
        out_specs=[hbm()] + [whole()] * 4,
        scratch_shapes=[
            VMEM((5, WX, WY, NZ), F32),
            VMEM((2, DEPTH, CY, NZ), F32),
            pltpu.SemaphoreType.DMA((2,)),
            pltpu.SemaphoreType.DMA((FILL_COPIES,)),
            pltpu.SemaphoreType.DMA((4,)),
        ],
        compiler_params=params(),
    )(info, tile, vt, ra, rb, yc, yd)


def window(info, vt, ra, rb, yc, yd, group):
    def kernel(info, vt, ra, rb, yc, yd, vw, sem):
        wait_all(fill_velocity(group, info, vt, ra, rb, yc, yd, vw, sem))

    return pl.pallas_call(
        kernel,
        out_shape=sds(4, 3, WX, WY, NZ),
        in_specs=[scalars()] + [whole()] * 5,
        out_specs=whole(),
        scratch_shapes=[pltpu.SemaphoreType.DMA((FILL_COPIES,))],
        compiler_params=params(),
    )(info, vt, ra, rb, yc, yd)


def send_rows(info, widths, source, ea, eb):
    px = info[2]
    off = 0
    for n, k in enumerate(widths):
        top = jnp.where(px == 0, CX, WX - k)
        bottom = jnp.where(px == 0, WX - k, CX)
        ea[off : off + k] = source(n)[pl.ds(top, k)]
        eb[off : off + k] = source(n)[pl.ds(bottom, k)]
        off += k


MID_WIDTHS = (4, 3, 2, 1)
MID_SLOTS = ((0, 4, 0), (1, 3, 4), (3, 1, 7))
END_WIDTHS = (3, 2, 1)
END_SLOTS = ((0, 3, 0), (1, 2, 3), (2, 1, 5), (3, 2, 6))


def forward_second(info, win, ic, idd, target, vw, pack, *before):
    def kernel(info, win, ic, idd, target, vw, pack_in, *refs):
        pack, lw, ea, eb, image, lam, osem = refs[len(before) :]
        fill_image(info, win, ic, idd, image.at[0])
        for n in range(4):
            clear_halo(lam.at[n])
        out = []
        for j in range(4):
            advance(image.at[j], image.at[j + 1], vw, j, 3 - j)
            out.append(pltpu.make_async_copy(image.at[j, 0:CX, 0:CY], pack.at[4 + j, 0:CX], osem.at[j]))
            out[-1].start()
        count = info[4]
        inside = lax.broadcasted_iota(jnp.int32, (CY, NZ), 0) * NZ + lax.broadcasted_iota(jnp.int32, (CY, NZ), 1)
        zero = jnp.zeros((8, NZ), F32)

        def one(x, carry):
            value = image[4, x, 0:CY] - target[x]
            lam[0, x, 0:CY] = jnp.where(inside + x * (CY * NZ) < count, value, 0.0)
            lam[0, x, CY:WY] = zero
            return carry

        lax.fori_loop(0, CX, one, 0)
        out.append(pltpu.make_async_copy(lam.at[0, 0:CX, 0:CY], pack.at[7, CX : 2 * CX], osem.at[4]))
        out[-1].start()
        for n in range(4):
            scatter(lam.at[n], lam.at[n + 1], vw, 3 - n, n + 1)
        for n in range(4):
            lw[n] = lam[4 - n, 0:CX]
        send_rows(info, MID_WIDTHS, lambda n: lam.at[4 - n], ea, eb)
        wait_all(out)

    return pl.pallas_call(
        kernel,
        out_shape=[sds(NT, PBLOCKS, CY, NZ), sds(4, CX, WY, NZ), sds(10, WY, NZ), sds(10, WY, NZ)],
        in_specs=[scalars()] + [whole()] * 5 + [hbm()] + [anywhere()] * len(before),
        out_specs=[hbm()] + [whole()] * 3,
        scratch_shapes=[
            VMEM((5, WX, WY, NZ), F32),
            VMEM((5, WX, WY, NZ), F32),
            pltpu.SemaphoreType.DMA((5,)),
        ],
        input_output_aliases={6: 0},
        compiler_params=params(),
    )(info, win, ic, idd, target, vw, pack, *before)


def costate_edges(info, lw, ra, rb, widths, slots, *before):
    def kernel(info, lw_in, ra, rb, *refs):
        lw, ec, ed = refs[len(before) :]
        px, py = info[2], info[3]
        off = 0
        for n, k in enumerate(widths):
            for i in range(k):
                to_a = jnp.where(px == 0, CX - k, 0) + i
                to_b = jnp.where(px == 0, 0, CX - k) + i
                lw[n, to_a] = lw[n, to_a] + ra[off + i]
                lw[n, to_b] = lw[n, to_b] + rb[off + i]
            off += k
        sub = rows8()

        def one(x, carry):
            top = jnp.zeros((8, NZ), F32)
            bottom = top
            for n, k, off in slots:
                block = lw[n, x, CY:WY]
                top = put(top, block, off, off, off + k, sub)
                bottom = put(bottom, block, off + k, off, off + k, sub)
            ec[x] = jnp.where(py == 0, top, bottom)
            ed[x] = jnp.where(py == 0, bottom, top)
            return carry

        lax.fori_loop(0, CX, one, 0)

    return pl.pallas_call(
        kernel,
        out_shape=[sds(4, CX, WY, NZ), sds(CX, 8, NZ), sds(CX, 8, NZ)],
        in_specs=[scalars()] + [whole()] * 3 + [anywhere()] * len(before),
        out_specs=[whole()] * 3,
        input_output_aliases={1: 0},
        compiler_params=params(),
    )(info, lw, ra, rb, *before)


def take(c, e, py, k, off, sub):
    below = jnp.where(py == 0, e, c)
    above = jnp.where(py == 0, c, e)
    zero = jnp.zeros((8, NZ), F32)
    return put(zero, below, -off, 0, k, sub), put(zero, above, 8 - k - off, 8 - k, 8, sub)


def backward_second(info, lw, lc, ld, vw, pack, *before):
    def kernel(info, lw, lc, ld, vw, pack_in, *refs):
        pack, lw2, ea, eb, lam, done, osem = refs[len(before) :]
        for n in range(3):
            clear_halo(lam.at[n])
        py = info[3]
        sub = rows8()
        zero = jnp.zeros((8, NZ), F32)

        def one(x, carry):
            c, e = lc[x], ld[x]
            for n, k, off in MID_SLOTS:
                low, high = take(c, e, py, k, off, sub)
                low, high = lw[n, x, 0:8] + low, lw[n, x, 8:16] + high
                if n == 0:
                    lam[0, x, 0:8] = low
                    lam[0, x, 8:16] = high
                    lam[0, x, CY:WY] = zero
                else:
                    done[(n - 1) // 2, x, 0:8] = low
                    done[(n - 1) // 2, x, 8:16] = high
            return carry

        lax.fori_loop(0, CX, one, 0)
        out = [
            pltpu.make_async_copy(lam.at[0, 0:CX, 0:CY], pack.at[3, CX : 2 * CX], osem.at[0]),
            pltpu.make_async_copy(done.at[0], pack.at[4, CX : 2 * CX], osem.at[1]),
            pltpu.make_async_copy(done.at[1], pack.at[6, CX : 2 * CX], osem.at[2]),
        ]
        for copy in out:
            copy.start()
        for n in range(3):
            scatter(lam.at[n], lam.at[n + 1], vw, 3 - n, n + 1)
        for n in range(3):
            lw2[n] = lam[3 - n, 0:CX]
        lw2[3] = lw[2]
        send_rows(info, END_WIDTHS, lambda n: lam.at[3 - n], ea, eb)
        wait_all(out)

    return pl.pallas_call(
        kernel,
        out_shape=[sds(NT, PBLOCKS, CY, NZ), sds(4, CX, WY, NZ), sds(6, WY, NZ), sds(6, WY, NZ)],
        in_specs=[scalars()] + [whole()] * 4 + [hbm()] + [anywhere()] * len(before),
        out_specs=[hbm()] + [whole()] * 3,
        scratch_shapes=[
            VMEM((4, WX, WY, NZ), F32),
            VMEM((2, CX, CY, NZ), F32),
            pltpu.SemaphoreType.DMA((3,)),
        ],
        input_output_aliases={5: 0},
        compiler_params=params(),
    )(info, lw, lc, ld, vw, pack, *before)


def costate_finish(info, lw, lc, ld, total, pack):
    def kernel(info, lw, lc, ld, total, pack_in, pack, done, note, sem):
        note[0] = jnp.broadcast_to(total[0:1], (CY, NZ))
        started = copies([(note, pack.at[t, 2 * CX : PBLOCKS]) for t in range(NT)], sem.at[pl.ds(4, NT)])
        py = info[3]
        sub = rows8()

        def one(x, carry):
            c, e = lc[x], ld[x]
            for n, k, off in END_SLOTS:
                low, high = take(c, e, py, k, off, sub)
                done[n, x, 0:8] = lw[n, x, 0:8] + low
                done[n, x, 8:16] = lw[n, x, 8:16] + high
            return carry

        lax.fori_loop(0, CX, one, 0)
        wait_all(copies([(done.at[n], pack.at[m, CX : 2 * CX]) for n, m in enumerate((0, 1, 2, 5))], sem))
        wait_all(started)

    return pl.pallas_call(
        kernel,
        out_shape=sds(NT, PBLOCKS, CY, NZ),
        in_specs=[scalars()] + [whole()] * 4 + [hbm()],
        out_specs=hbm(),
        scratch_shapes=[VMEM((4, CX, CY, NZ), F32), VMEM((1, CY, NZ), F32), pltpu.SemaphoreType.DMA((4 + NT,))],
        input_output_aliases={5: 0},
        compiler_params=params(58),
    )(info, lw, lc, ld, total, pack)


PAD = 8
PY = NY + 2 * PAD
CHUNK = 32


def clear_pads(ref, lead):
    zero = jnp.zeros((PAD, NZ), F32)
    for index in lead:
        ref[(*index, slice(0, PAD))] = zero
        ref[(*index, slice(PAD + NY, PY))] = zero


def part(ref, index, y, move=0):
    return ref[(*index, slice(PAD + y + move, PAD + y + move + CHUNK))]


def smooth(ref, before, at, after, y, m):
    first, last = m
    c = part(ref, at, y)
    near = part(ref, before, y) + part(ref, after, y)
    near += part(ref, at, y, -1) + part(ref, at, y, 1)
    near += jnp.where(first, 0.0, pltpu.roll(c, 1, 1)) + jnp.where(last, 0.0, pltpu.roll(c, NZ - 1, 1))
    return (1.0 - 6.0 * KAPPA) * c + KAPPA * near


def slope(v, ref, before, at, after, direction, y, m):
    first, last = m
    c = part(ref, at, y)
    if direction == 0:
        behind, beyond = part(ref, before, y), part(ref, after, y)
    elif direction == 1:
        behind, beyond = part(ref, at, y, -1), part(ref, at, y, 1)
    else:
        behind = jnp.where(first, 0.0, pltpu.roll(c, 1, 1))
        beyond = jnp.where(last, 0.0, pltpu.roll(c, NZ - 1, 1))
    return jnp.where(v > 0.0, c - behind, beyond - c)


CHUNKS = tuple(range(0, NY, CHUNK))


def coefficient(notes, cells):
    total = notes[0, 0, 0:8]
    for c in range(1, NY // CY):
        total += notes[c, 0, 0:8]
    return ((-STEP * DATA_WEIGHT) * (cells / total))[0:1]


def finish_inside(velocity, pack, cells):
    def kernel(vel, pack, out, keep_c, keep_s, islab, lslab, grad, soft, notes, sem):
        d = pl.program_id(0)

        @pl.when(d == 0)
        def _():
            pairs = []
            for c in range(NY // CY):
                y = slice(c * CY, (c + 1) * CY)
                padded = slice(PAD + c * CY, PAD + (c + 1) * CY)
                pairs += [
                    (pack.at[c, 0:CX], islab.at[:, padded]),
                    (pack.at[c, CX : 2 * CX], lslab.at[:, y]),
                    (pack.at[c, 2 * CX : PBLOCKS], notes.at[c]),
                ]
            started = copies(pairs, sem)
            for ref in (islab, grad, soft):
                clear_pads(ref, [(x,) for x in range(CX)])
            wait_all(started)

        coef = coefficient(notes, cells)
        m = lane_masks((CHUNK, NZ))
        for direction in range(3):

            @pl.when(d == direction)
            def _(direction=direction):
                def one(x, carry):
                    for y in CHUNKS:
                        rows = slice(y, y + CHUNK)
                        g = slope(vel[0, 0, x, rows], islab, (x - 1,), (x,), (x + 1,), direction, y, m)
                        grad[x, PAD + y : PAD + y + CHUNK] = (coef * lslab[x, rows]) * g
                    return carry

                lax.fori_loop(1, CX - 1, one, 0)

        def once(x, carry):
            for y in CHUNKS:
                soft[x, PAD + y : PAD + y + CHUNK] = smooth(grad, (x - 1,), (x,), (x + 1,), y, m)
            return carry

        lax.fori_loop(2, CX - 2, once, 0)

        def twice(x, carry):
            for y in CHUNKS:
                rows = slice(y, y + CHUNK)
                out[0, 0, x, rows] = vel[0, 0, x, rows] + smooth(soft, (x - 1,), (x,), (x + 1,), y, m)
            return carry

        lax.fori_loop(3, CX - 3, twice, 0)
        for n, (x, y) in enumerate(((1, 2), (2, 3), (13, 12), (14, 13))):
            keep_c[0, n] = grad[x, PAD : PAD + NY]
            keep_s[0, n] = soft[y, PAD : PAD + NY]

    slab = pl.BlockSpec((1, 1, CX, NY, NZ), lambda d: (0, d, 0, 0, 0))
    kept = pl.BlockSpec((1, 4, NY, NZ), lambda d: (d, 0, 0, 0))
    return pl.pallas_call(
        kernel,
        grid=(3,),
        out_shape=[sds(1, 3, CX, NY, NZ), sds(3, 4, NY, NZ), sds(3, 4, NY, NZ)],
        in_specs=[slab, hbm()],
        out_specs=[slab, kept, kept],
        scratch_shapes=[VMEM((CX, PY, NZ), F32), VMEM((CX, NY, NZ), F32), VMEM((CX, PY, NZ), F32), VMEM((CX, PY, NZ), F32)]
        + [VMEM((8, 1, CY, NZ), F32), pltpu.SemaphoreType.DMA((24,))],
        compiler_params=params(60),
    )(velocity, pack)


def finish_edges(info, velocity, va, vb, pack, fa, fb, keep_c, keep_s, partial, cells):
    def kernel(info, vel, va, vb, pack, fa, fb, keep_c, keep_s, partial, out, slabs, all_rows, grad, soft, all_results, notes, sem, osem):
        d = pl.program_id(0)
        px = info[2]

        @pl.when(d == 0)
        def _():
            pairs = []
            above, below = jnp.where(px == 0, 1, 0), jnp.where(px == 0, 0, 1)
            hi, hl = jnp.where(px == 0, 2, 0), jnp.where(px == 0, 6, 5)
            bi, bl = jnp.where(px == 0, 0, 2), jnp.where(px == 0, 5, 6)
            for c in range(NY // CY):
                y = slice(PAD + c * CY, PAD + (c + 1) * CY)
                pairs += [
                    (pack.at[c, 0:2], slabs.at[0, 3:5, y]),
                    (pack.at[c, CX : CX + 1], slabs.at[0, 7:8, y]),
                    (pack.at[c, CX - 2 : CX], slabs.at[1, 0:2, y]),
                    (pack.at[c, 2 * CX - 1 : 2 * CX], slabs.at[1, 5:6, y]),
                    (pack.at[c, 2 * CX : PBLOCKS], notes.at[c]),
                    (fa.at[c, 0:3], slabs.at[above, pl.ds(hi, 3), y]),
                    (fa.at[c, 3:5], slabs.at[above, pl.ds(hl, 2), y]),
                    (fb.at[c, 0:3], slabs.at[below, pl.ds(bi, 3), y]),
                    (fb.at[c, 3:5], slabs.at[below, pl.ds(bl, 2), y]),
                ]
            for n in range(3):
                pairs += [(vel.at[0, n, 0:3], all_rows.at[n, 0]), (vel.at[0, n, CX - 3 : CX], all_rows.at[n, 1])]
            started = copies(pairs, sem)
            clear_pads(slabs, [(side, n) for side in range(2) for n in range(5)])
            for ref in (grad, soft):
                clear_pads(ref, [(side, n) for side in range(2) for n in range(5)])
            wait_all(started)

        vrows, result = all_rows.at[d], all_results.at[d]

        coef = coefficient(notes, cells)
        m = lane_masks((CHUNK, NZ))
        for direction in range(3):

            @pl.when(d == direction)
            def _(direction=direction):
                for side in range(2):
                    for n in range(3):
                        own = n == 2 if side == 0 else n == 0
                        for y in CHUNKS:
                            rows = slice(y, y + CHUNK)
                            if own:
                                v = vrows[0, 0, rows] if side == 0 else vrows[1, 2, rows]
                            else:
                                k = n if side == 0 else n - 1
                                v = jnp.where((px == 0) == (side == 1), va[0, k, rows], vb[0, k, rows])
                            g = slope(v, slabs, (side, n), (side, n + 1), (side, n + 2), direction, y, m)
                            grad[side, n, PAD + y : PAD + y + CHUNK] = (coef * part(slabs, (side, 5 + n), y)) * g

        inner = slice(PAD, PAD + NY)
        for n in range(2):
            grad[0, 3 + n, inner] = keep_c[0, n]
            grad[1, 3 + n, inner] = keep_c[0, 2 + n]
            soft[0, 3 + n, inner] = keep_s[0, n]
            soft[1, n, inner] = keep_s[0, 2 + n]
        zero = jnp.zeros((NY, NZ), F32)
        for side in range(2):
            order = [0, 1, 2, 3, 4] if side == 0 else [3, 4, 0, 1, 2]
            for n in range(3):
                at = [(side, order[n + k]) for k in range(3)]
                for y in CHUNKS:
                    soft[side, n + 2 * side, PAD + y : PAD + y + CHUNK] = smooth(grad, *at, y, m)

        @pl.when(info[0] == 0)
        def _():
            soft[0, 0, inner] = zero

        @pl.when(info[0] == info[5] - 1)
        def _():
            soft[1, 4, inner] = zero

        for side in range(2):
            for n in range(3):
                for y in CHUNKS:
                    rows = slice(y, y + CHUNK)
                    value = smooth(soft, (side, n), (side, n + 1), (side, n + 2), y, m)
                    result[side, n, rows] = vrows[side, n, rows] + value

        def leave(n):
            low, high = all_results.at[n, 0], all_results.at[n, 1]
            return [
                pltpu.make_async_copy(low, out.at[0, n, 0:3], osem.at[n, 0]),
                pltpu.make_async_copy(high, out.at[0, n, CX - 3 : CX], osem.at[n, 1]),
            ]

        for n in range(3):

            @pl.when(d == n)
            def _(n=n):
                for copy in leave(n):
                    copy.start()

        @pl.when(d == 2)
        def _():
            for n in range(3):
                wait_all(leave(n))

    face = pl.BlockSpec((1, 2, NY, NZ), lambda d: (d, 0, 0, 0))
    kept = pl.BlockSpec((1, 4, NY, NZ), lambda d: (d, 0, 0, 0))
    return pl.pallas_call(
        kernel,
        grid=(3,),
        out_shape=sds(1, 3, CX, NY, NZ),
        in_specs=[scalars(), hbm(), face, face] + [hbm()] + [anywhere()] * 2 + [kept, kept, hbm()],
        out_specs=hbm(),
        scratch_shapes=[
            VMEM((2, 8, PY, NZ), F32),
            VMEM((3, 2, 3, NY, NZ), F32),
            VMEM((2, 5, PY, NZ), F32),
            VMEM((2, 5, PY, NZ), F32),
            VMEM((3, 2, 3, NY, NZ), F32),
            VMEM((8, 1, CY, NZ), F32),
            pltpu.SemaphoreType.DMA((78,)),
            pltpu.SemaphoreType.DMA((3, 2)),
        ],
        input_output_aliases={9: 0},
        compiler_params=params(60),
    )(info, velocity, va, vb, pack, fa, fb, keep_c, keep_s, partial)


def edge_rows(value, dim, k, px):
    length = value.shape[dim]
    high = lax.slice_in_dim(value, length - k, length, axis=dim)
    low = lax.slice_in_dim(value, 0, k, axis=dim)
    return jnp.where(px == 0, high, low), jnp.where(px == 0, low, high)


def shards(velocity, atlas_image, target, labels, label_table, counts):
    s, c = lax.axis_index("space"), lax.axis_index("cuts")
    px, py = s % 2, c % 2
    info = jnp.stack([s, c, px, py, counts[0], jnp.int32(lax.axis_size("space")), s, s]).astype(jnp.int32)
    far_a, far_b, *direct = repack(info, velocity)
    got, far = spread(far_a, far_b, direct[:5])

    tile, ova, ovb = template(info, label_table, atlas_image, labels, velocity, far)
    ova, ovb = swap(ova, ovb, "space")

    vt, fa, fb, ga, gb, total = faces(info, direct[5], got, tile, ova, ovb)
    fa, fb = swap(fa, fb, "space")
    ga, gb = swap(ga, gb, "space")
    y0 = swap(*velocity_edges(info, vt, fa, fb, 0, tile), "cuts")
    total = xor_swap(total, 1)
    y1 = swap(*velocity_edges(info, vt, ga, gb, 1), "cuts")
    pack, ea, eb, i4, vw0 = forward_first(info, tile, vt, fa, fb, *y0)
    win, ec, ed = image_edges(info, i4, *swap(ea, eb, "space"))
    vw1 = window(info, vt, ga, gb, *y1, 1)
    ic, idd = swap(ec, ed, "cuts")
    pack, lw, ea, eb = forward_second(info, win, ic, idd, target, vw1, pack, total)
    total = xor_swap(total, 2)
    lw, ec, ed = costate_edges(info, lw, *swap(ea, eb, "space"), MID_WIDTHS, MID_SLOTS, total)
    total = xor_swap(total, 4)
    ec, ed = swap(ec, ed, "cuts")
    pack, lw, ea, eb = backward_second(info, lw, ec, ed, vw0, pack, total)
    total = xor_swap(total, 8)
    lw, ec, ed = costate_edges(info, lw, *swap(ea, eb, "space"), END_WIDTHS, END_SLOTS)
    ec, ed = swap(ec, ed, "cuts")
    pack = costate_finish(info, lw, ec, ed, total, pack)
    pack = lax.all_to_all(pack, "cuts", split_axis=0, concat_axis=0, tiled=True)

    cells = float(CX * CY * NZ * lax.axis_size("space") * lax.axis_size("cuts"))
    rows = [jnp.concatenate([pack[:, a : a + 3], pack[:, b : b + 2]], axis=1) for a, b in ((CX - 3, 2 * CX - 2), (0, CX))]
    ea, eb = jnp.where(px == 0, rows[0], rows[1]), jnp.where(px == 0, rows[1], rows[0])
    fa, fb = swap(ea, eb, "space")
    partial, keep_c, keep_s = finish_inside(velocity, pack, cells)
    return finish_edges(info, velocity, ova, ovb, pack, fa, fb, keep_c, keep_s, partial, cells)


def solution(mesh):
    in_specs = (
        P("cuts", None, "space", None, None),
        P("space", "cuts", None),
        P("space", "cuts", None),
        P("space", "cuts", None),
        P(),
        P(("space", "cuts")),
    )
    out_specs = P("cuts", None, "space", None, None)
    return jax.shard_map(shards, mesh=mesh, in_specs=in_specs, out_specs=out_specs, check_vma=False)
```

time: 321 us -> 316 us (0.984)
  the two profiles are of different devices: /device:TPU:7 before, /device:TPU:93 now
where the time goes in v3:
time: 316 us; the launch traced here: 315 us
  waiting for transfers between devices  156 us (49%)
  starting transfers between devices  77.7 us (25%)
  Pallas kernels  68.2 us (22%)
  local copies, waits for them, and re-layouts  10.7 us (3%)
    all_to_all x1, waiting for transfers between devices, shards(): pack = lax.all_to_all(pack, 'cuts', split_axis=0, concat_axis=0, tiled=True)  60.6 us
    ppermute x11, waiting for transfers between devices, shift(): lax.ppermute(value, 'cuts', ring_pairs(up, across, lax.axis_size('cuts')))  60.5 us
    ppermute x12, starting transfers between devices, swap(): lax.ppermute(odd, axis, swaps(size, 1))  44.3 us
    pallas_call x1, Pallas kernels, finish_inside(): pl.pallas_call(kernel, grid=(3,), out_shape=[sds(1, 3, CX, NY, NZ), sds(3...  18.7 us
    ppermute x12, waiting for transfers between devices, swap(): lax.ppermute(odd, axis, swaps(size, 1))  17.5 us
    ppermute x12, starting transfers between devices, swap(): lax.ppermute(even, axis, swaps(size, 0))  12.1 us
    ppermute x11, starting transfers between devices, shift(): lax.ppermute(value, 'cuts', ring_pairs(up, across, lax.axis_size('cuts')))  12.1 us
    pallas_call x1, Pallas kernels, finish_edges(): pl.pallas_call(kernel, grid=(3,), out_shape=sds(1, 3, CX, NY, NZ), in_spe...  9.78 us
  transfers between devices with their start and end apart: 40, of which 19 were waited for; matrix products, arithmetic and copies ran while one was open for 0% of the time, Pallas kernels for 10%

profile of v3, /device:TPU:93, one launch (start us, length us, event | category | flops | bytes accessed | tf_op | source)
XLA Modules:
  0.0 315.1 jit_solution(12479075037173025847)
XLA Ops:
  1.4 6.5 %shard_map.64 = (f32[2,24,16,256]{3,2,1,0:T(8,128)}, f32[2,24,16,256]{3,2,1,0:T(8,128)}, f32[48,16,256]{2,1,0:T(8,128)}, f32[48,16,256]{2,1,0:T(8,128)}, f32[48,...) custom-call(s32[8]{0:T(128)} %stack.21.info, ...), custom_call_target="tpu_custom_call" | custom-call | tf_op jit(solution)/shard_map/pallas_call | solution.py:284
  13.2 13.4 %collective-permute-done.refs_0_ = f32[2,24,16,256]{3,2,1,0:T(8,128)S(1)} collective-permute-done((f32[2,24,16,256]{3,2,1,0:T(8,128)}, f32[2,24,16,256]{3,2,1,0:T(8,128)S(1)}, u32[]{:S(2)}, u32[]{:S(2)}) %collective-permute-start) | collective-permute-done | bytes 786464 | tf_op jit(solution)/shard_map/ppermute | solution.py:247
  27.9 20.0 %collective-permute-done.3.refs_0_ = f32[48,16,256]{2,1,0:T(8,128)S(1)} collective-permute-done((f32[48,16,256]{2,1,0:T(8,128)}, f32[48,16,256]{2,1,0:T(8,128)S(1)}, u32[]{:S(2)}, u32[]{:S(2)}) %collective-permute-start.3) | collective-permute-done | bytes 786464 | tf_op jit(solution)/shard_map/ppermute | solution.py:247
  55.8 6.4 %collective-permute-done.5.refs_2_ = f32[48,16,256]{2,1,0:T(8,128)S(1)} collective-permute-done((f32[48,16,256]{2,1,0:T(8,128)}, f32[48,16,256]{2,1,0:T(8,128)S(1)}, u32[]{:S(2)}, u32[]{:S(2)}) %collective-permute-start.5) | collective-permute-done | bytes 786464 | tf_op jit(solution)/shard_map/ppermute | solution.py:247
  72.5 9.2 %collective-permute-done.9.refs_6_ = f32[24,16,256]{2,1,0:T(8,128)S(1)} collective-permute-done((f32[24,16,256]{2,1,0:T(8,128)S(1)}, f32[24,16,256]{2,1,0:T(8,128)S(1)}, u32[]{:S(2)}, u32[]{:S(2)}) %collective-permute-start.9) | collective-permute-done | bytes 393248 | tf_op jit(solution)/shard_map/ppermute | solution.py:247
  81.6 9.0 %collective-permute-done.12.refs_8_ = f32[24,16,256]{2,1,0:T(8,128)S(1)} collective-permute-done((f32[24,16,256]{2,1,0:T(8,128)S(1)}, f32[24,16,256]{2,1,0:T(8,128)S(1)}, u32[]{:S(2)}, u32[]{:S(2)}) %collective-permute-start.12) | collective-permute-done | bytes 393248 | tf_op jit(solution)/shard_map/ppermute | solution.py:247
  93.9 8.6 %collective-permute-start.14 = (f32[22,16,256]{2,1,0:T(8,128)S(1)}, f32[22,16,256]{2,1,0:T(8,128)S(1)}, u32[]{:S(2)}, u32[]{:S(2)}) collective-permute-start(f32[22,16,256]{2,1,0:T(8,128)S(1)} %get-tuple-element.64), channel_id=1, source_target_pairs={{8,16},{16,8},{24,32},{32,24},{40,48},{48,40},{56,64},{64,56},{72,... | collective-permute-start | bytes 1081352 | tf_op jit(solution)/shard_map/ppermute | solution.py:64
  109.0 3.4 %collective-permute-start.16 = (f32[3,26,8,256]{3,2,1,0:T(8,128)S(1)}, f32[3,26,8,256]{3,2,1,0:T(8,128)S(1)}, u32[]{:S(2)}, u32[]{:S(2)}) collective-permute-start(f32[3,26,8,256]{3,2,1,0:T(8,128)S(1)} %get-tuple-element.66), channel_id=1, source_target_pairs={{1,2},{2,1},{3,4},{4,3},{5,6},{6,5},{9,10},{10,9},{11,12},{12,11},... | collective-permute-start | bytes 1916936 | tf_op jit(solution)/shard_map/ppermute | solution.py:64
  113.5 4.0 %collective-permute-start.24 = (f32[3,22,8,256]{3,2,1,0:T(8,128)S(1)}, f32[3,22,8,256]{3,2,1,0:T(8,128)S(1)}, u32[]{:S(2)}, u32[]{:S(2)}) collective-permute-start(f32[3,22,8,256]{3,2,1,0:T(8,128)S(1)} %get-tuple-element.76), channel_id=1, source_target_pairs={{1,2},{2,1},{3,4},{4,3},{5,6},{6,5},{9,10},{10,9},{11,12},{12,11},... | collective-permute-start | bytes 1622024 | tf_op jit(solution)/shard_map/ppermute | solution.py:64
  117.4 8.0 %collective-permute-done.15.yc = f32[3,26,8,256]{3,2,1,0:T(8,128)S(1)} collective-permute-done((f32[3,26,8,256]{3,2,1,0:T(8,128)S(1)}, f32[3,26,8,256]{3,2,1,0:T(8,128)S(1)}, u32[]{:S(2)}, u32[]{:S(2)}) %collective-permute-start.15) | collective-permute-done | bytes 639008 | tf_op jit(solution)/shard_map/ppermute | solution.py:64
  125.4 4.0 %collective-permute-done.16.yd = f32[3,26,8,256]{3,2,1,0:T(8,128)S(1)} collective-permute-done((f32[3,26,8,256]{3,2,1,0:T(8,128)S(1)}, f32[3,26,8,256]{3,2,1,0:T(8,128)S(1)}, u32[]{:S(2)}, u32[]{:S(2)}) %collective-permute-start.16) | collective-permute-done | bytes 639008 | tf_op jit(solution)/shard_map/ppermute | solution.py:64
  129.4 6.2 %shard_map.68 = (f32[8,33,16,256]{3,2,1,0:T(8,128)S(1)}, f32[4,16,256]{2,1,0:T(8,128)S(1)}, f32[4,16,256]{2,1,0:T(8,128)S(1)}, f32[16,16,256]{2,1,0:T(8,128)S(1)}, f32[4,3,24,24,256]{4,3,2,1,0:T(8,128)S(1)}) custom-call(s32[8]{0:T(128)S(1)} %copy-done.9, f32[16,16,256]{2,1,0:T(8,128)S(1)} %get-tuple-element.54.refs_9_.refs_0_.tile, ...), custom_call_target="tpu_custom_call" | custom-call | tf_op jit(solution)/shard_map/pallas_call | solution.py:495
  135.7 3.4 %collective-permute-start.18 = (f32[4,16,256]{2,1,0:T(8,128)S(1)}, f32[4,16,256]{2,1,0:T(8,128)S(1)}, u32[]{:S(2)}, u32[]{:S(2)}) collective-permute-start(f32[4,16,256]{2,1,0:T(8,128)S(1)} %get-tuple-element.69), channel_id=1, source_target_pairs={{8,16},{16,8},{24,32},{32,24},{40,48},{48,40},{56,64},{64,56},{72,... | collective-permute-start | bytes 196616 | tf_op jit(solution)/shard_map/ppermute | solution.py:64
  150.1 9.7 %shard_map.72 = (f32[8,33,16,256]{3,2,1,0:T(8,128)S(1)}, f32[4,16,24,256]{3,2,1,0:T(8,128)S(1)}, f32[10,24,256]{2,1,0:T(8,128)S(1)}, f32[10,24,256]{2,1,0:T(8,128)S(1)}) custom-call(s32[8]{0:T(128)S(1)} %copy-done.9, f32[24,16,256]{2,1,0:T(8,128)S(1)} %get-tuple-element.70.win, ...), custom_call_target="tpu_custom_call", output_to_operand_aliasing={{0}: (6, {})} | custom-call | tf_op jit(solution)/shard_map/pallas_call | solution.py:579
  173.2 3.7 %collective-permute-start.31 = (f32[8,256]{1,0:T(8,128)S(1)}, f32[8,256]{1,0:T(8,128)S(1)}, u32[]{:S(2)}, u32[]{:S(2)}) collective-permute-start(f32[8,256]{1,0:T(8,128)S(1)} %add.22.refs_0_), channel_id=1, source_target_pairs={{0,32},{8,40},{16,48},{24,56},{32,0},{40,8},{48,16},{56,24},{64,96... | collective-permute-start | bytes 24584 | tf_op jit(solution)/shard_map/ppermute | solution.py:69
  178.3 4.2 %shard_map.74 = (f32[8,33,16,256]{3,2,1,0:T(8,128)S(1)}, f32[4,16,24,256]{3,2,1,0:T(8,128)S(1)}, f32[6,24,256]{2,1,0:T(8,128)S(1)}, f32[6,24,256]{2,1,0:T(8,128)S(1)}) custom-call(s32[8]{0:T(128)S(1)} %copy-done.9, f32[4,16,24,256]{3,2,1,0:T(8,128)S(1)} %get-tuple-element.82.lw, ...), custom_call_target="tpu_custom_call", output_to_operand_aliasing={{0}: (5, {})} | custom-call | tf_op jit(solution)/shard_map/pallas_call | solution.py:677
  184.5 4.5 %collective-permute-start.32 = (f32[6,24,256]{2,1,0:T(8,128)S(1)}, f32[6,24,256]{2,1,0:T(8,128)S(1)}, u32[]{:S(2)}, u32[]{:S(2)}) collective-permute-start(f32[6,24,256]{2,1,0:T(8,128)S(1)} %get-tuple-element.88), channel_id=1, source_target_pairs={{0,8},{8,0},{16,24},{24,16},{32,40},{40,32},{48,56},{56,48},{64,72... | collective-permute-start | bytes 442376 | tf_op jit(solution)/shard_map/ppermute | solution.py:64
  191.0 4.5 %collective-permute-done.33.rb = f32[6,24,256]{2,1,0:T(8,128)S(1)} collective-permute-done((f32[6,24,256]{2,1,0:T(8,128)S(1)}, f32[6,24,256]{2,1,0:T(8,128)S(1)}, u32[]{:S(2)}, u32[]{:S(2)}) %collective-permute-start.33) | collective-permute-done | bytes 147488 | tf_op jit(solution)/shard_map/ppermute | solution.py:64
  200.9 4.3 %collective-permute-done.36 = f32[8,256]{1,0:T(8,128)S(1)} collective-permute-done((f32[8,256]{1,0:T(8,128)S(1)}, f32[8,256]{1,0:T(8,128)S(1)}, u32[]{:S(2)}, u32[]{:S(2)}) %collective-permute-start.36) | collective-permute-done | bytes 8224 | tf_op jit(solution)/shard_map/ppermute | solution.py:69
  210.0 4.5 %all-to-all-start = ((f32[8,33,16,256]{3,2,1,0:T(8,128)}), f32[8,33,16,256]{3,2,1,0:T(8,128)}, u32[]{:S(2)}, u32[]{:S(2)}) async-start(f32[8,33,16,256]{3,2,1,0:T(8,128)} %shard_map.76), calls=%async_computation | async-start | bytes 8650752 | tf_op jit(solution)/shard_map/all_to_all | solution.py:998
  214.5 60.6 %all-to-all-done.pack = f32[8,33,16,256]{3,2,1,0:T(8,128)} async-done(((f32[8,33,16,256]{3,2,1,0:T(8,128)}), f32[8,33,16,256]{3,2,1,0:T(8,128)}, u32[]{:S(2)}, u32[]{:S(2)}) %all-to-all-start) | async-done | bytes 4325408 | tf_op jit(solution)/shard_map/all_to_all | solution.py:998
  280.0 5.4 %collective-permute-start.38 = (f32[8,5,16,256]{3,2,1,0:T(8,128)S(1)}, f32[8,5,16,256]{3,2,1,0:T(8,128)S(1)}, u32[]{:S(2)}, u32[]{:S(2)}) collective-permute-start(f32[8,5,16,256]{3,2,1,0:T(8,128)S(1)} %get-tuple-element.101), channel_id=1, source_target_pairs={{8,16},{16,8},{24,32},{32,24},{40,48},{48,40},{56,64},{64,56},{72,... | collective-permute-start | bytes 1966088 | tf_op jit(solution)/shard_map/ppermute | solution.py:64
  285.5 18.7 %shard_map.77 = (f32[1,3,16,128,256]{4,3,2,1,0:T(8,128)}, f32[3,4,128,256]{3,2,1,0:T(8,128)}, f32[3,4,128,256]{3,2,1,0:T(8,128)}) custom-call(f32[1,3,16,128,256]{4,3,2,1,0:T(8,128)} %vel.3, f32[8,33,16,256]{3,2,1,0:T(8,128)} %all-to-all-done.pack), custom_call_target="tpu_custom_call" | custom-call | tf_op jit(solution)/shard_map/pallas_call | solution.py:825
  305.2 9.8 %shard_map.78 = f32[1,3,16,128,256]{4,3,2,1,0:T(8,128)} custom-call(s32[8]{0:T(128)} %stack.21.info, f32[1,3,16,128,256]{4,3,2,1,0:T(8,128)} %vel.3, f32[3,2,128,256]{3,2,1,0:T(8,128)} %copy-done.3, f32[3,2,128,256]{3,2,1,0:T(8,128)} %copy-done.4, f32[8,33,16,256]{3,2,1,0:T(8,128)} %all-to-all-done.pack, ...), custom_call_target="tpu_custom_call", output_to_operand_aliasing={{}: (9, {})} | custom-call | tf_op jit(solution)/shard_map/pallas_call | solution.py:940
  (111 shorter events, 81.6 us)
Async XLA Ops:
  7.9 18.7 %collective-permute-start = (f32[2,24,16,256]{3,2,1,0:T(8,128)}, f32[2,24,16,256]{3,2,1,0:T(8,128)S(1)}, u32[]{:S(2)}, u32[]{:S(2)}) collective-permute-start(f32[2,24,16,256]{3,2,1,0:T(8,128)} %get-tuple-element.51), channel_id=1, source_target_pairs={{0,1},{1,2},{2,3},{3,0},{4,5},{5,6},{6,7},{7,4},{8,9},{9,10},{10,1... | collective-permute-start | bytes 2359304 | tf_op jit(solution)/shard_map/ppermute | solution.py:247
  8.0 39.9 %collective-permute-start.3 = (f32[48,16,256]{2,1,0:T(8,128)}, f32[48,16,256]{2,1,0:T(8,128)S(1)}, u32[]{:S(2)}, u32[]{:S(2)}) collective-permute-start(f32[48,16,256]{2,1,0:T(8,128)} %get-tuple-element.56), channel_id=1, source_target_pairs={{0,5},{1,6},{2,7},{3,4},{4,1},{5,2},{6,3},{7,0},{8,13},{9,14},{10,... | collective-permute-start | bytes 2359304 | tf_op jit(solution)/shard_map/ppermute | solution.py:247
  10.3 42.8 %collective-permute-start.4 = (f32[48,16,256]{2,1,0:T(8,128)}, f32[48,16,256]{2,1,0:T(8,128)S(1)}, u32[]{:S(2)}, u32[]{:S(2)}) collective-permute-start(f32[48,16,256]{2,1,0:T(8,128)} %get-tuple-element.57), channel_id=1, source_target_pairs={{0,7},{1,4},{2,5},{3,6},{4,3},{5,0},{6,1},{7,2},{8,15},{9,12},{10,... | collective-permute-start | bytes 2359304 | tf_op jit(solution)/shard_map/ppermute | solution.py:247
  10.5 51.7 %collective-permute-start.5 = (f32[48,16,256]{2,1,0:T(8,128)}, f32[48,16,256]{2,1,0:T(8,128)S(1)}, u32[]{:S(2)}, u32[]{:S(2)}) collective-permute-start(f32[48,16,256]{2,1,0:T(8,128)} %get-tuple-element.58), channel_id=1, source_target_pairs={{0,4},{1,5},{2,6},{3,7},{4,0},{5,1},{6,2},{7,3},{8,12},{9,13},{10,... | collective-permute-start | bytes 2359304 | tf_op jit(solution)/shard_map/ppermute | solution.py:247
  11.8 52.6 %collective-permute-start.10 = (f32[2,24,16,256]{3,2,1,0:T(8,128)}, f32[2,24,16,256]{3,2,1,0:T(8,128)S(1)}, u32[]{:S(2)}, u32[]{:S(2)}) collective-permute-start(f32[2,24,16,256]{3,2,1,0:T(8,128)} %get-tuple-element.61), channel_id=1, source_target_pairs={{0,3},{1,0},{2,1},{3,2},{4,7},{5,4},{6,5},{7,6},{8,11},{9,8},{10,9... | collective-permute-start | bytes 2359304 | tf_op jit(solution)/shard_map/ppermute | solution.py:247
  26.6 40.6 %collective-permute-start.6 = (f32[48,16,256]{2,1,0:T(8,128)}, f32[48,16,256]{2,1,0:T(8,128)S(1)}, u32[]{:S(2)}, u32[]{:S(2)}) collective-permute-start(f32[48,16,256]{2,1,0:T(8,128)} %get-tuple-element.59), channel_id=1, source_target_pairs={{0,1},{1,2},{2,3},{3,0},{4,5},{5,6},{6,7},{7,4},{8,9},{9,10},{10,1... | collective-permute-start | bytes 2359304 | tf_op jit(solution)/shard_map/ppermute | solution.py:247
  47.9 21.2 %collective-permute-start.7 = (f32[48,16,256]{2,1,0:T(8,128)}, f32[48,16,256]{2,1,0:T(8,128)S(1)}, u32[]{:S(2)}, u32[]{:S(2)}) collective-permute-start(f32[48,16,256]{2,1,0:T(8,128)} %get-tuple-element.60), channel_id=1, source_target_pairs={{0,3},{1,0},{2,1},{3,2},{4,7},{5,4},{6,5},{7,6},{8,11},{9,8},{10,9... | collective-permute-start | bytes 2359304 | tf_op jit(solution)/shard_map/ppermute | solution.py:247
  53.1 19.0 %collective-permute-start.8 = (f32[24,16,256]{2,1,0:T(8,128)S(1)}, f32[24,16,256]{2,1,0:T(8,128)S(1)}, u32[]{:S(2)}, u32[]{:S(2)}) collective-permute-start(f32[24,16,256]{2,1,0:T(8,128)S(1)} %get-tuple-element.106), channel_id=1, source_target_pairs={{0,1},{1,2},{2,3},{3,0},{4,5},{5,6},{6,7},{7,4},{8,9},{9,10},{10,1... | collective-permute-start | bytes 1179656 | tf_op jit(solution)/shard_map/ppermute | solution.py:247
  62.2 28.4 %collective-permute-start.1 = (f32[3,2,128,256]{3,2,1,0:T(8,128)S(1)}, f32[3,2,128,256]{3,2,1,0:T(8,128)S(1)}, u32[]{:S(2)}, u32[]{:S(2)}) collective-permute-start(f32[3,2,128,256]{3,2,1,0:T(8,128)S(1)} %get-tuple-element.52), channel_id=1, source_target_pairs={{0,8},{8,0},{16,24},{24,16},{32,40},{40,32},{48,56},{56,48},{64,72... | collective-permute-start | bytes 2359304 | tf_op jit(solution)/shard_map/ppermute | solution.py:64
  64.4 26.3 %collective-permute-start.2 = (f32[3,2,128,256]{3,2,1,0:T(8,128)S(1)}, f32[3,2,128,256]{3,2,1,0:T(8,128)S(1)}, u32[]{:S(2)}, u32[]{:S(2)}) collective-permute-start(f32[3,2,128,256]{3,2,1,0:T(8,128)S(1)} %get-tuple-element.53), channel_id=1, source_target_pairs={{8,16},{16,8},{24,32},{32,24},{40,48},{48,40},{56,64},{64,56},{72,... | collective-permute-start | bytes 2359304 | tf_op jit(solution)/shard_map/ppermute | solution.py:64
  67.2 14.4 %collective-permute-start.9 = (f32[24,16,256]{2,1,0:T(8,128)S(1)}, f32[24,16,256]{2,1,0:T(8,128)S(1)}, u32[]{:S(2)}, u32[]{:S(2)}) collective-permute-start(f32[24,16,256]{2,1,0:T(8,128)S(1)} %get-tuple-element.105), channel_id=1, source_target_pairs={{0,5},{1,6},{2,7},{3,4},{4,1},{5,2},{6,3},{7,0},{8,13},{9,14},{10,... | collective-permute-start | bytes 1179656 | tf_op jit(solution)/shard_map/ppermute | solution.py:247
  69.1 12.6 %collective-permute-start.11 = (f32[24,16,256]{2,1,0:T(8,128)S(1)}, f32[24,16,256]{2,1,0:T(8,128)S(1)}, u32[]{:S(2)}, u32[]{:S(2)}) collective-permute-start(f32[24,16,256]{2,1,0:T(8,128)S(1)} %get-tuple-element.104), channel_id=1, source_target_pairs={{0,3},{1,0},{2,1},{3,2},{4,7},{5,4},{6,5},{7,6},{8,11},{9,8},{10,9... | collective-permute-start | bytes 1179656 | tf_op jit(solution)/shard_map/ppermute | solution.py:247
  72.1 18.5 %collective-permute-start.12 = (f32[24,16,256]{2,1,0:T(8,128)S(1)}, f32[24,16,256]{2,1,0:T(8,128)S(1)}, u32[]{:S(2)}, u32[]{:S(2)}) collective-permute-start(f32[24,16,256]{2,1,0:T(8,128)S(1)} %get-tuple-element.103), channel_id=1, source_target_pairs={{0,7},{1,4},{2,5},{3,6},{4,3},{5,0},{6,1},{7,2},{8,15},{9,12},{10,... | collective-permute-start | bytes 1179656 | tf_op jit(solution)/shard_map/ppermute | solution.py:247
  92.9 11.6 %collective-permute-start.13 = (f32[22,16,256]{2,1,0:T(8,128)S(1)}, f32[22,16,256]{2,1,0:T(8,128)S(1)}, u32[]{:S(2)}, u32[]{:S(2)}) collective-permute-start(f32[22,16,256]{2,1,0:T(8,128)S(1)} %get-tuple-element.63), channel_id=1, source_target_pairs={{0,8},{8,0},{16,24},{24,16},{32,40},{40,32},{48,56},{56,48},{64,72... | collective-permute-start | bytes 1081352 | tf_op jit(solution)/shard_map/ppermute | solution.py:64
  93.9 14.0 %collective-permute-start.14 = (f32[22,16,256]{2,1,0:T(8,128)S(1)}, f32[22,16,256]{2,1,0:T(8,128)S(1)}, u32[]{:S(2)}, u32[]{:S(2)}) collective-permute-start(f32[22,16,256]{2,1,0:T(8,128)S(1)} %get-tuple-element.64), channel_id=1, source_target_pairs={{8,16},{16,8},{24,32},{32,24},{40,48},{48,40},{56,64},{64,56},{72,... | collective-permute-start | bytes 1081352 | tf_op jit(solution)/shard_map/ppermute | solution.py:64
  102.4 9.9 %collective-permute-start.21 = (f32[18,16,256]{2,1,0:T(8,128)S(1)}, f32[18,16,256]{2,1,0:T(8,128)S(1)}, u32[]{:S(2)}, u32[]{:S(2)}) collective-permute-start(f32[18,16,256]{2,1,0:T(8,128)S(1)} %get-tuple-element.73), channel_id=1, source_target_pairs={{0,8},{8,0},{16,24},{24,16},{32,40},{40,32},{48,56},{56,48},{64,72... | collective-permute-start | bytes 884744 | tf_op jit(solution)/shard_map/ppermute | solution.py:64
  102.5 9.9 %collective-permute-start.22 = (f32[18,16,256]{2,1,0:T(8,128)S(1)}, f32[18,16,256]{2,1,0:T(8,128)S(1)}, u32[]{:S(2)}, u32[]{:S(2)}) collective-permute-start(f32[18,16,256]{2,1,0:T(8,128)S(1)} %get-tuple-element.74), channel_id=1, source_target_pairs={{8,16},{16,8},{24,32},{32,24},{40,48},{48,40},{56,64},{64,56},{72,... | collective-permute-start | bytes 884744 | tf_op jit(solution)/shard_map/ppermute | solution.py:64
  108.9 16.5 %collective-permute-start.15 = (f32[3,26,8,256]{3,2,1,0:T(8,128)S(1)}, f32[3,26,8,256]{3,2,1,0:T(8,128)S(1)}, u32[]{:S(2)}, u32[]{:S(2)}) collective-permute-start(f32[3,26,8,256]{3,2,1,0:T(8,128)S(1)} %get-tuple-element.65), channel_id=1, source_target_pairs={{0,1},{1,0},{2,3},{3,2},{4,5},{5,4},{6,7},{7,6},{8,9},{9,8},{10,11... | collective-permute-start | bytes 1916936 | tf_op jit(solution)/shard_map/ppermute | solution.py:64
  109.0 20.5 %collective-permute-start.16 = (f32[3,26,8,256]{3,2,1,0:T(8,128)S(1)}, f32[3,26,8,256]{3,2,1,0:T(8,128)S(1)}, u32[]{:S(2)}, u32[]{:S(2)}) collective-permute-start(f32[3,26,8,256]{3,2,1,0:T(8,128)S(1)} %get-tuple-element.66), channel_id=1, source_target_pairs={{1,2},{2,1},{3,4},{4,3},{5,6},{6,5},{9,10},{10,9},{11,12},{12,11},... | collective-permute-start | bytes 1916936 | tf_op jit(solution)/shard_map/ppermute | solution.py:64
  113.4 33.8 %collective-permute-start.23 = (f32[3,22,8,256]{3,2,1,0:T(8,128)S(1)}, f32[3,22,8,256]{3,2,1,0:T(8,128)S(1)}, u32[]{:S(2)}, u32[]{:S(2)}) collective-permute-start(f32[3,22,8,256]{3,2,1,0:T(8,128)S(1)} %get-tuple-element.75), channel_id=1, source_target_pairs={{0,1},{1,0},{2,3},{3,2},{4,5},{5,4},{6,7},{7,6},{8,9},{9,8},{10,11... | collective-permute-start | bytes 1622024 | tf_op jit(solution)/shard_map/ppermute | solution.py:64
  113.5 33.7 %collective-permute-start.24 = (f32[3,22,8,256]{3,2,1,0:T(8,128)S(1)}, f32[3,22,8,256]{3,2,1,0:T(8,128)S(1)}, u32[]{:S(2)}, u32[]{:S(2)}) collective-permute-start(f32[3,22,8,256]{3,2,1,0:T(8,128)S(1)} %get-tuple-element.76), channel_id=1, source_target_pairs={{1,2},{2,1},{3,4},{4,3},{5,6},{6,5},{9,10},{10,9},{11,12},{12,11},... | collective-permute-start | bytes 1622024 | tf_op jit(solution)/shard_map/ppermute | solution.py:64
  210.0 65.2 %all-to-all-start = ((f32[8,33,16,256]{3,2,1,0:T(8,128)}), f32[8,33,16,256]{3,2,1,0:T(8,128)}, u32[]{:S(2)}, u32[]{:S(2)}) async-start(f32[8,33,16,256]{3,2,1,0:T(8,128)} %shard_map.76), calls=%async_computation | async-start | bytes 8650752 | tf_op jit(solution)/shard_map/all_to_all | solution.py:998
  277.5 26.6 %collective-permute-start.37 = (f32[8,5,16,256]{3,2,1,0:T(8,128)S(1)}, f32[8,5,16,256]{3,2,1,0:T(8,128)S(1)}, u32[]{:S(2)}, u32[]{:S(2)}) collective-permute-start(f32[8,5,16,256]{3,2,1,0:T(8,128)S(1)} %get-tuple-element.102), channel_id=1, source_target_pairs={{0,8},{8,0},{16,24},{24,16},{32,40},{40,32},{48,56},{56,48},{64,72... | collective-permute-start | bytes 1966088 | tf_op jit(solution)/shard_map/ppermute | solution.py:64
  280.0 24.1 %collective-permute-start.38 = (f32[8,5,16,256]{3,2,1,0:T(8,128)S(1)}, f32[8,5,16,256]{3,2,1,0:T(8,128)S(1)}, u32[]{:S(2)}, u32[]{:S(2)}) collective-permute-start(f32[8,5,16,256]{3,2,1,0:T(8,128)S(1)} %get-tuple-element.101), channel_id=1, source_target_pairs={{8,16},{16,8},{24,32},{32,24},{40,48},{48,40},{56,64},{64,56},{72,... | collective-permute-start | bytes 1966088 | tf_op jit(solution)/shard_map/ppermute | solution.py:64
  (31 other events, 380.0 us)

commit v4 on v3

--- a/solution.py
+++ b/solution.py
@@ -744,6 +744,25 @@
     return (1.0 - 6.0 * KAPPA) * c + KAPPA * near
 
 
+def third_sum(c, beside):
+    high = c.astype(jnp.bfloat16)
+    low = (c - high.astype(F32)).astype(jnp.bfloat16)
+    both = jnp.dot(jnp.concatenate([high, low], axis=0), beside, preferred_element_type=F32)
+    return both[0 : c.shape[0]] + both[c.shape[0] :]
+
+
+def smooth_rows(ref, x, rows, beside):
+    inner = slice(PAD, PAD + NY)
+    values = [ref[x + r, inner] for r in range(rows)]
+    third = third_sum(jnp.concatenate(values, axis=0), beside)
+    out = []
+    for r, c in enumerate(values):
+        near = third[r * NY : (r + 1) * NY] + ref[x + r - 1, inner] + ref[x + r + 1, inner]
+        near += ref[x + r, PAD - 1 : PAD + NY - 1] + ref[x + r, PAD + 1 : PAD + NY + 1]
+        out.append((1.0 - 6.0 * KAPPA) * c + KAPPA * near)
+    return out
+
+
 def slope(v, ref, before, at, after, direction, y, m):
     first, last = m
     c = part(ref, at, y)
@@ -768,7 +787,7 @@
 
 
 def finish_inside(velocity, pack, cells):
-    def kernel(vel, pack, out, keep_c, keep_s, islab, lslab, grad, soft, notes, sem):
+    def kernel(vel, pack, out, keep_c, keep_s, islab, lslab, grad, soft, notes, beside, sem):
         d = pl.program_id(0)
 
         @pl.when(d == 0)
@@ -783,6 +802,8 @@
                     (pack.at[c, 2 * CX : PBLOCKS], notes.at[c]),
                 ]
             started = copies(pairs, sem)
+            apart = lax.broadcasted_iota(jnp.int32, (NZ, NZ), 0) - lax.broadcasted_iota(jnp.int32, (NZ, NZ), 1)
+            beside[...] = jnp.where(jnp.abs(apart) == 1, 1.0, 0.0).astype(jnp.bfloat16)
             for ref in (islab, grad, soft):
                 clear_pads(ref, [(x,) for x in range(CX)])
             wait_all(started)
@@ -802,20 +823,23 @@
 
                 lax.fori_loop(1, CX - 1, one, 0)
 
-        def once(x, carry):
-            for y in CHUNKS:
-                soft[x, PAD + y : PAD + y + CHUNK] = smooth(grad, (x - 1,), (x,), (x + 1,), y, m)
+        near = beside[...]
+
+        def once(i, carry):
+            x = 2 + 2 * i
+            for r, value in enumerate(smooth_rows(grad, x, 2, near)):
+                soft[x + r, PAD : PAD + NY] = value
             return carry
 
-        lax.fori_loop(2, CX - 2, once, 0)
-
-        def twice(x, carry):
-            for y in CHUNKS:
-                rows = slice(y, y + CHUNK)
-                out[0, 0, x, rows] = vel[0, 0, x, rows] + smooth(soft, (x - 1,), (x,), (x + 1,), y, m)
+        lax.fori_loop(0, (CX - 4) // 2, once, 0)
+
+        def twice(i, carry):
+            x = 3 + 2 * i
+            for r, value in enumerate(smooth_rows(soft, x, 2, near)):
+                out[0, 0, x + r] = vel[0, 0, x + r] + value
             return carry
 
-        lax.fori_loop(3, CX - 3, twice, 0)
+        lax.fori_loop(0, (CX - 6) // 2, twice, 0)
         for n, (x, y) in enumerate(((1, 2), (2, 3), (13, 12), (14, 13))):
             keep_c[0, n] = grad[x, PAD : PAD + NY]
             keep_s[0, n] = soft[y, PAD : PAD + NY]
@@ -829,7 +853,7 @@
         in_specs=[slab, hbm()],
         out_specs=[slab, kept, kept],
         scratch_shapes=[VMEM((CX, PY, NZ), F32), VMEM((CX, NY, NZ), F32), VMEM((CX, PY, NZ), F32), VMEM((CX, PY, NZ), F32)]
-        + [VMEM((8, 1, CY, NZ), F32), pltpu.SemaphoreType.DMA((24,))],
+        + [VMEM((8, 1, CY, NZ), F32), VMEM((NZ, NZ), jnp.bfloat16), pltpu.SemaphoreType.DMA((24,))],
         compiler_params=params(60),
     )(velocity, pack)
 

time: 316 us -> 315 us (level)
  no operation moved by 1% of the time
where the time goes in v4:
time: 315 us; the launch traced here: 314 us
  waiting for transfers between devices  156 us (50%)
  starting transfers between devices  77.7 us (25%)
  Pallas kernels  66.9 us (21%)
  local copies, waits for them, and re-layouts  10.7 us (3%)
    all_to_all x1, waiting for transfers between devices, shards(): pack = lax.all_to_all(pack, 'cuts', split_axis=0, concat_axis=0, tiled=True)  60.6 us
    ppermute x11, waiting for transfers between devices, shift(): lax.ppermute(value, 'cuts', ring_pairs(up, across, lax.axis_size('cuts')))  60.5 us
    ppermute x12, starting transfers between devices, swap(): lax.ppermute(odd, axis, swaps(size, 1))  44.3 us
    ppermute x12, waiting for transfers between devices, swap(): lax.ppermute(odd, axis, swaps(size, 1))  17.5 us
    pallas_call x1, Pallas kernels, finish_inside(): pl.pallas_call(kernel, grid=(3,), out_shape=[sds(1, 3, CX, NY, NZ), sds(3...  17.4 us
    ppermute x12, starting transfers between devices, swap(): lax.ppermute(even, axis, swaps(size, 0))  12.1 us
    ppermute x11, starting transfers between devices, shift(): lax.ppermute(value, 'cuts', ring_pairs(up, across, lax.axis_size('cuts')))  12.1 us
    pallas_call x1, Pallas kernels, finish_edges(): pl.pallas_call(kernel, grid=(3,), out_shape=sds(1, 3, CX, NY, NZ), in_spe...  9.78 us
  transfers between devices with their start and end apart: 40, of which 19 were waited for; matrix products, arithmetic and copies ran while one was open for 0% of the time, Pallas kernels for 10%

profile of v4, /device:TPU:93, one launch (start us, length us, event | category | flops | bytes accessed | tf_op | source)
XLA Modules:
  0.0 313.9 jit_solution(11677151372809798570)
XLA Ops:
  1.4 6.5 %shard_map.64 = (f32[2,24,16,256]{3,2,1,0:T(8,128)}, f32[2,24,16,256]{3,2,1,0:T(8,128)}, f32[48,16,256]{2,1,0:T(8,128)}, f32[48,16,256]{2,1,0:T(8,128)}, f32[48,...) custom-call(s32[8]{0:T(128)} %stack.21.info, ...), custom_call_target="tpu_custom_call" | custom-call | tf_op jit(solution)/shard_map/pallas_call | solution.py:284
  13.2 13.4 %collective-permute-done.refs_0_ = f32[2,24,16,256]{3,2,1,0:T(8,128)S(1)} collective-permute-done((f32[2,24,16,256]{3,2,1,0:T(8,128)}, f32[2,24,16,256]{3,2,1,0:T(8,128)S(1)}, u32[]{:S(2)}, u32[]{:S(2)}) %collective-permute-start) | collective-permute-done | bytes 786464 | tf_op jit(solution)/shard_map/ppermute | solution.py:247
  27.9 20.0 %collective-permute-done.3.refs_0_ = f32[48,16,256]{2,1,0:T(8,128)S(1)} collective-permute-done((f32[48,16,256]{2,1,0:T(8,128)}, f32[48,16,256]{2,1,0:T(8,128)S(1)}, u32[]{:S(2)}, u32[]{:S(2)}) %collective-permute-start.3) | collective-permute-done | bytes 786464 | tf_op jit(solution)/shard_map/ppermute | solution.py:247
  55.8 6.4 %collective-permute-done.5.refs_2_ = f32[48,16,256]{2,1,0:T(8,128)S(1)} collective-permute-done((f32[48,16,256]{2,1,0:T(8,128)}, f32[48,16,256]{2,1,0:T(8,128)S(1)}, u32[]{:S(2)}, u32[]{:S(2)}) %collective-permute-start.5) | collective-permute-done | bytes 786464 | tf_op jit(solution)/shard_map/ppermute | solution.py:247
  72.5 9.2 %collective-permute-done.9.refs_6_ = f32[24,16,256]{2,1,0:T(8,128)S(1)} collective-permute-done((f32[24,16,256]{2,1,0:T(8,128)S(1)}, f32[24,16,256]{2,1,0:T(8,128)S(1)}, u32[]{:S(2)}, u32[]{:S(2)}) %collective-permute-start.9) | collective-permute-done | bytes 393248 | tf_op jit(solution)/shard_map/ppermute | solution.py:247
  81.6 9.0 %collective-permute-done.12.refs_8_ = f32[24,16,256]{2,1,0:T(8,128)S(1)} collective-permute-done((f32[24,16,256]{2,1,0:T(8,128)S(1)}, f32[24,16,256]{2,1,0:T(8,128)S(1)}, u32[]{:S(2)}, u32[]{:S(2)}) %collective-permute-start.12) | collective-permute-done | bytes 393248 | tf_op jit(solution)/shard_map/ppermute | solution.py:247
  93.9 8.6 %collective-permute-start.14 = (f32[22,16,256]{2,1,0:T(8,128)S(1)}, f32[22,16,256]{2,1,0:T(8,128)S(1)}, u32[]{:S(2)}, u32[]{:S(2)}) collective-permute-start(f32[22,16,256]{2,1,0:T(8,128)S(1)} %get-tuple-element.64), channel_id=1, source_target_pairs={{8,16},{16,8},{24,32},{32,24},{40,48},{48,40},{56,64},{64,56},{72,... | collective-permute-start | bytes 1081352 | tf_op jit(solution)/shard_map/ppermute | solution.py:64
  109.0 3.4 %collective-permute-start.16 = (f32[3,26,8,256]{3,2,1,0:T(8,128)S(1)}, f32[3,26,8,256]{3,2,1,0:T(8,128)S(1)}, u32[]{:S(2)}, u32[]{:S(2)}) collective-permute-start(f32[3,26,8,256]{3,2,1,0:T(8,128)S(1)} %get-tuple-element.66), channel_id=1, source_target_pairs={{1,2},{2,1},{3,4},{4,3},{5,6},{6,5},{9,10},{10,9},{11,12},{12,11},... | collective-permute-start | bytes 1916936 | tf_op jit(solution)/shard_map/ppermute | solution.py:64
  113.5 4.0 %collective-permute-start.24 = (f32[3,22,8,256]{3,2,1,0:T(8,128)S(1)}, f32[3,22,8,256]{3,2,1,0:T(8,128)S(1)}, u32[]{:S(2)}, u32[]{:S(2)}) collective-permute-start(f32[3,22,8,256]{3,2,1,0:T(8,128)S(1)} %get-tuple-element.76), channel_id=1, source_target_pairs={{1,2},{2,1},{3,4},{4,3},{5,6},{6,5},{9,10},{10,9},{11,12},{12,11},... | collective-permute-start | bytes 1622024 | tf_op jit(solution)/shard_map/ppermute | solution.py:64
  117.4 8.0 %collective-permute-done.15.yc = f32[3,26,8,256]{3,2,1,0:T(8,128)S(1)} collective-permute-done((f32[3,26,8,256]{3,2,1,0:T(8,128)S(1)}, f32[3,26,8,256]{3,2,1,0:T(8,128)S(1)}, u32[]{:S(2)}, u32[]{:S(2)}) %collective-permute-start.15) | collective-permute-done | bytes 639008 | tf_op jit(solution)/shard_map/ppermute | solution.py:64
  125.4 4.0 %collective-permute-done.16.yd = f32[3,26,8,256]{3,2,1,0:T(8,128)S(1)} collective-permute-done((f32[3,26,8,256]{3,2,1,0:T(8,128)S(1)}, f32[3,26,8,256]{3,2,1,0:T(8,128)S(1)}, u32[]{:S(2)}, u32[]{:S(2)}) %collective-permute-start.16) | collective-permute-done | bytes 639008 | tf_op jit(solution)/shard_map/ppermute | solution.py:64
  129.4 6.2 %shard_map.68 = (f32[8,33,16,256]{3,2,1,0:T(8,128)S(1)}, f32[4,16,256]{2,1,0:T(8,128)S(1)}, f32[4,16,256]{2,1,0:T(8,128)S(1)}, f32[16,16,256]{2,1,0:T(8,128)S(1)}, f32[4,3,24,24,256]{4,3,2,1,0:T(8,128)S(1)}) custom-call(s32[8]{0:T(128)S(1)} %copy-done.9, f32[16,16,256]{2,1,0:T(8,128)S(1)} %get-tuple-element.54.refs_9_.refs_0_.tile, ...), custom_call_target="tpu_custom_call" | custom-call | tf_op jit(solution)/shard_map/pallas_call | solution.py:495
  135.7 3.4 %collective-permute-start.18 = (f32[4,16,256]{2,1,0:T(8,128)S(1)}, f32[4,16,256]{2,1,0:T(8,128)S(1)}, u32[]{:S(2)}, u32[]{:S(2)}) collective-permute-start(f32[4,16,256]{2,1,0:T(8,128)S(1)} %get-tuple-element.69), channel_id=1, source_target_pairs={{8,16},{16,8},{24,32},{32,24},{40,48},{48,40},{56,64},{64,56},{72,... | collective-permute-start | bytes 196616 | tf_op jit(solution)/shard_map/ppermute | solution.py:64
  150.1 9.7 %shard_map.72 = (f32[8,33,16,256]{3,2,1,0:T(8,128)S(1)}, f32[4,16,24,256]{3,2,1,0:T(8,128)S(1)}, f32[10,24,256]{2,1,0:T(8,128)S(1)}, f32[10,24,256]{2,1,0:T(8,128)S(1)}) custom-call(s32[8]{0:T(128)S(1)} %copy-done.9, f32[24,16,256]{2,1,0:T(8,128)S(1)} %get-tuple-element.70.win, ...), custom_call_target="tpu_custom_call", output_to_operand_aliasing={{0}: (6, {})} | custom-call | tf_op jit(solution)/shard_map/pallas_call | solution.py:579
  173.2 3.7 %collective-permute-start.31 = (f32[8,256]{1,0:T(8,128)S(1)}, f32[8,256]{1,0:T(8,128)S(1)}, u32[]{:S(2)}, u32[]{:S(2)}) collective-permute-start(f32[8,256]{1,0:T(8,128)S(1)} %add.22.refs_0_), channel_id=1, source_target_pairs={{0,32},{8,40},{16,48},{24,56},{32,0},{40,8},{48,16},{56,24},{64,96... | collective-permute-start | bytes 24584 | tf_op jit(solution)/shard_map/ppermute | solution.py:69
  178.3 4.2 %shard_map.74 = (f32[8,33,16,256]{3,2,1,0:T(8,128)S(1)}, f32[4,16,24,256]{3,2,1,0:T(8,128)S(1)}, f32[6,24,256]{2,1,0:T(8,128)S(1)}, f32[6,24,256]{2,1,0:T(8,128)S(1)}) custom-call(s32[8]{0:T(128)S(1)} %copy-done.9, f32[4,16,24,256]{3,2,1,0:T(8,128)S(1)} %get-tuple-element.82.lw, ...), custom_call_target="tpu_custom_call", output_to_operand_aliasing={{0}: (5, {})} | custom-call | tf_op jit(solution)/shard_map/pallas_call | solution.py:677
  184.5 4.5 %collective-permute-start.32 = (f32[6,24,256]{2,1,0:T(8,128)S(1)}, f32[6,24,256]{2,1,0:T(8,128)S(1)}, u32[]{:S(2)}, u32[]{:S(2)}) collective-permute-start(f32[6,24,256]{2,1,0:T(8,128)S(1)} %get-tuple-element.88), channel_id=1, source_target_pairs={{0,8},{8,0},{16,24},{24,16},{32,40},{40,32},{48,56},{56,48},{64,72... | collective-permute-start | bytes 442376 | tf_op jit(solution)/shard_map/ppermute | solution.py:64
  191.0 4.5 %collective-permute-done.33.rb = f32[6,24,256]{2,1,0:T(8,128)S(1)} collective-permute-done((f32[6,24,256]{2,1,0:T(8,128)S(1)}, f32[6,24,256]{2,1,0:T(8,128)S(1)}, u32[]{:S(2)}, u32[]{:S(2)}) %collective-permute-start.33) | collective-permute-done | bytes 147488 | tf_op jit(solution)/shard_map/ppermute | solution.py:64
  200.9 4.3 %collective-permute-done.36 = f32[8,256]{1,0:T(8,128)S(1)} collective-permute-done((f32[8,256]{1,0:T(8,128)S(1)}, f32[8,256]{1,0:T(8,128)S(1)}, u32[]{:S(2)}, u32[]{:S(2)}) %collective-permute-start.36) | collective-permute-done | bytes 8224 | tf_op jit(solution)/shard_map/ppermute | solution.py:69
  210.0 4.5 %all-to-all-start = ((f32[8,33,16,256]{3,2,1,0:T(8,128)}), f32[8,33,16,256]{3,2,1,0:T(8,128)}, u32[]{:S(2)}, u32[]{:S(2)}) async-start(f32[8,33,16,256]{3,2,1,0:T(8,128)} %shard_map.76), calls=%async_computation | async-start | bytes 8650752 | tf_op jit(solution)/shard_map/all_to_all | solution.py:1022
  214.5 60.6 %all-to-all-done.pack = f32[8,33,16,256]{3,2,1,0:T(8,128)} async-done(((f32[8,33,16,256]{3,2,1,0:T(8,128)}), f32[8,33,16,256]{3,2,1,0:T(8,128)}, u32[]{:S(2)}, u32[]{:S(2)}) %all-to-all-start) | async-done | bytes 4325408 | tf_op jit(solution)/shard_map/all_to_all | solution.py:1022
  280.0 5.4 %collective-permute-start.38 = (f32[8,5,16,256]{3,2,1,0:T(8,128)S(1)}, f32[8,5,16,256]{3,2,1,0:T(8,128)S(1)}, u32[]{:S(2)}, u32[]{:S(2)}) collective-permute-start(f32[8,5,16,256]{3,2,1,0:T(8,128)S(1)} %get-tuple-element.101), channel_id=1, source_target_pairs={{8,16},{16,8},{24,32},{32,24},{40,48},{48,40},{56,64},{64,56},{72,... | collective-permute-start | bytes 1966088 | tf_op jit(solution)/shard_map/ppermute | solution.py:64
  285.5 17.4 %shard_map.77 = (f32[1,3,16,128,256]{4,3,2,1,0:T(8,128)}, f32[3,4,128,256]{3,2,1,0:T(8,128)}, f32[3,4,128,256]{3,2,1,0:T(8,128)}) custom-call(f32[1,3,16,128,256]{4,3,2,1,0:T(8,128)} %vel.3, f32[8,33,16,256]{3,2,1,0:T(8,128)} %all-to-all-done.pack), custom_call_target="tpu_custom_call" | custom-call | tf_op jit(solution)/shard_map/pallas_call | solution.py:849
  304.0 9.8 %shard_map.78 = f32[1,3,16,128,256]{4,3,2,1,0:T(8,128)} custom-call(s32[8]{0:T(128)} %stack.21.info, f32[1,3,16,128,256]{4,3,2,1,0:T(8,128)} %vel.3, f32[3,2,128,256]{3,2,1,0:T(8,128)} %copy-done.3, f32[3,2,128,256]{3,2,1,0:T(8,128)} %copy-done.4, f32[8,33,16,256]{3,2,1,0:T(8,128)} %all-to-all-done.pack, ...), custom_call_target="tpu_custom_call", output_to_operand_aliasing={{}: (9, {})} | custom-call | tf_op jit(solution)/shard_map/pallas_call | solution.py:964
  (111 shorter events, 81.6 us)
Async XLA Ops:
  7.9 18.7 %collective-permute-start = (f32[2,24,16,256]{3,2,1,0:T(8,128)}, f32[2,24,16,256]{3,2,1,0:T(8,128)S(1)}, u32[]{:S(2)}, u32[]{:S(2)}) collective-permute-start(f32[2,24,16,256]{3,2,1,0:T(8,128)} %get-tuple-element.51), channel_id=1, source_target_pairs={{0,1},{1,2},{2,3},{3,0},{4,5},{5,6},{6,7},{7,4},{8,9},{9,10},{10,1... | collective-permute-start | bytes 2359304 | tf_op jit(solution)/shard_map/ppermute | solution.py:247
  8.0 39.9 %collective-permute-start.3 = (f32[48,16,256]{2,1,0:T(8,128)}, f32[48,16,256]{2,1,0:T(8,128)S(1)}, u32[]{:S(2)}, u32[]{:S(2)}) collective-permute-start(f32[48,16,256]{2,1,0:T(8,128)} %get-tuple-element.56), channel_id=1, source_target_pairs={{0,5},{1,6},{2,7},{3,4},{4,1},{5,2},{6,3},{7,0},{8,13},{9,14},{10,... | collective-permute-start | bytes 2359304 | tf_op jit(solution)/shard_map/ppermute | solution.py:247
  10.3 42.8 %collective-permute-start.4 = (f32[48,16,256]{2,1,0:T(8,128)}, f32[48,16,256]{2,1,0:T(8,128)S(1)}, u32[]{:S(2)}, u32[]{:S(2)}) collective-permute-start(f32[48,16,256]{2,1,0:T(8,128)} %get-tuple-element.57), channel_id=1, source_target_pairs={{0,7},{1,4},{2,5},{3,6},{4,3},{5,0},{6,1},{7,2},{8,15},{9,12},{10,... | collective-permute-start | bytes 2359304 | tf_op jit(solution)/shard_map/ppermute | solution.py:247
  10.5 51.7 %collective-permute-start.5 = (f32[48,16,256]{2,1,0:T(8,128)}, f32[48,16,256]{2,1,0:T(8,128)S(1)}, u32[]{:S(2)}, u32[]{:S(2)}) collective-permute-start(f32[48,16,256]{2,1,0:T(8,128)} %get-tuple-element.58), channel_id=1, source_target_pairs={{0,4},{1,5},{2,6},{3,7},{4,0},{5,1},{6,2},{7,3},{8,12},{9,13},{10,... | collective-permute-start | bytes 2359304 | tf_op jit(solution)/shard_map/ppermute | solution.py:247
  11.8 52.6 %collective-permute-start.10 = (f32[2,24,16,256]{3,2,1,0:T(8,128)}, f32[2,24,16,256]{3,2,1,0:T(8,128)S(1)}, u32[]{:S(2)}, u32[]{:S(2)}) collective-permute-start(f32[2,24,16,256]{3,2,1,0:T(8,128)} %get-tuple-element.61), channel_id=1, source_target_pairs={{0,3},{1,0},{2,1},{3,2},{4,7},{5,4},{6,5},{7,6},{8,11},{9,8},{10,9... | collective-permute-start | bytes 2359304 | tf_op jit(solution)/shard_map/ppermute | solution.py:247
  26.6 40.6 %collective-permute-start.6 = (f32[48,16,256]{2,1,0:T(8,128)}, f32[48,16,256]{2,1,0:T(8,128)S(1)}, u32[]{:S(2)}, u32[]{:S(2)}) collective-permute-start(f32[48,16,256]{2,1,0:T(8,128)} %get-tuple-element.59), channel_id=1, source_target_pairs={{0,1},{1,2},{2,3},{3,0},{4,5},{5,6},{6,7},{7,4},{8,9},{9,10},{10,1... | collective-permute-start | bytes 2359304 | tf_op jit(solution)/shard_map/ppermute | solution.py:247
  47.9 21.2 %collective-permute-start.7 = (f32[48,16,256]{2,1,0:T(8,128)}, f32[48,16,256]{2,1,0:T(8,128)S(1)}, u32[]{:S(2)}, u32[]{:S(2)}) collective-permute-start(f32[48,16,256]{2,1,0:T(8,128)} %get-tuple-element.60), channel_id=1, source_target_pairs={{0,3},{1,0},{2,1},{3,2},{4,7},{5,4},{6,5},{7,6},{8,11},{9,8},{10,9... | collective-permute-start | bytes 2359304 | tf_op jit(solution)/shard_map/ppermute | solution.py:247
  53.1 19.0 %collective-permute-start.8 = (f32[24,16,256]{2,1,0:T(8,128)S(1)}, f32[24,16,256]{2,1,0:T(8,128)S(1)}, u32[]{:S(2)}, u32[]{:S(2)}) collective-permute-start(f32[24,16,256]{2,1,0:T(8,128)S(1)} %get-tuple-element.106), channel_id=1, source_target_pairs={{0,1},{1,2},{2,3},{3,0},{4,5},{5,6},{6,7},{7,4},{8,9},{9,10},{10,1... | collective-permute-start | bytes 1179656 | tf_op jit(solution)/shard_map/ppermute | solution.py:247
  62.2 28.4 %collective-permute-start.1 = (f32[3,2,128,256]{3,2,1,0:T(8,128)S(1)}, f32[3,2,128,256]{3,2,1,0:T(8,128)S(1)}, u32[]{:S(2)}, u32[]{:S(2)}) collective-permute-start(f32[3,2,128,256]{3,2,1,0:T(8,128)S(1)} %get-tuple-element.52), channel_id=1, source_target_pairs={{0,8},{8,0},{16,24},{24,16},{32,40},{40,32},{48,56},{56,48},{64,72... | collective-permute-start | bytes 2359304 | tf_op jit(solution)/shard_map/ppermute | solution.py:64
  64.4 26.3 %collective-permute-start.2 = (f32[3,2,128,256]{3,2,1,0:T(8,128)S(1)}, f32[3,2,128,256]{3,2,1,0:T(8,128)S(1)}, u32[]{:S(2)}, u32[]{:S(2)}) collective-permute-start(f32[3,2,128,256]{3,2,1,0:T(8,128)S(1)} %get-tuple-element.53), channel_id=1, source_target_pairs={{8,16},{16,8},{24,32},{32,24},{40,48},{48,40},{56,64},{64,56},{72,... | collective-permute-start | bytes 2359304 | tf_op jit(solution)/shard_map/ppermute | solution.py:64
  67.2 14.4 %collective-permute-start.9 = (f32[24,16,256]{2,1,0:T(8,128)S(1)}, f32[24,16,256]{2,1,0:T(8,128)S(1)}, u32[]{:S(2)}, u32[]{:S(2)}) collective-permute-start(f32[24,16,256]{2,1,0:T(8,128)S(1)} %get-tuple-element.105), channel_id=1, source_target_pairs={{0,5},{1,6},{2,7},{3,4},{4,1},{5,2},{6,3},{7,0},{8,13},{9,14},{10,... | collective-permute-start | bytes 1179656 | tf_op jit(solution)/shard_map/ppermute | solution.py:247
  69.1 12.6 %collective-permute-start.11 = (f32[24,16,256]{2,1,0:T(8,128)S(1)}, f32[24,16,256]{2,1,0:T(8,128)S(1)}, u32[]{:S(2)}, u32[]{:S(2)}) collective-permute-start(f32[24,16,256]{2,1,0:T(8,128)S(1)} %get-tuple-element.104), channel_id=1, source_target_pairs={{0,3},{1,0},{2,1},{3,2},{4,7},{5,4},{6,5},{7,6},{8,11},{9,8},{10,9... | collective-permute-start | bytes 1179656 | tf_op jit(solution)/shard_map/ppermute | solution.py:247
  72.1 18.5 %collective-permute-start.12 = (f32[24,16,256]{2,1,0:T(8,128)S(1)}, f32[24,16,256]{2,1,0:T(8,128)S(1)}, u32[]{:S(2)}, u32[]{:S(2)}) collective-permute-start(f32[24,16,256]{2,1,0:T(8,128)S(1)} %get-tuple-element.103), channel_id=1, source_target_pairs={{0,7},{1,4},{2,5},{3,6},{4,3},{5,0},{6,1},{7,2},{8,15},{9,12},{10,... | collective-permute-start | bytes 1179656 | tf_op jit(solution)/shard_map/ppermute | solution.py:247
  92.9 11.6 %collective-permute-start.13 = (f32[22,16,256]{2,1,0:T(8,128)S(1)}, f32[22,16,256]{2,1,0:T(8,128)S(1)}, u32[]{:S(2)}, u32[]{:S(2)}) collective-permute-start(f32[22,16,256]{2,1,0:T(8,128)S(1)} %get-tuple-element.63), channel_id=1, source_target_pairs={{0,8},{8,0},{16,24},{24,16},{32,40},{40,32},{48,56},{56,48},{64,72... | collective-permute-start | bytes 1081352 | tf_op jit(solution)/shard_map/ppermute | solution.py:64
  93.9 14.0 %collective-permute-start.14 = (f32[22,16,256]{2,1,0:T(8,128)S(1)}, f32[22,16,256]{2,1,0:T(8,128)S(1)}, u32[]{:S(2)}, u32[]{:S(2)}) collective-permute-start(f32[22,16,256]{2,1,0:T(8,128)S(1)} %get-tuple-element.64), channel_id=1, source_target_pairs={{8,16},{16,8},{24,32},{32,24},{40,48},{48,40},{56,64},{64,56},{72,... | collective-permute-start | bytes 1081352 | tf_op jit(solution)/shard_map/ppermute | solution.py:64
  102.4 9.9 %collective-permute-start.21 = (f32[18,16,256]{2,1,0:T(8,128)S(1)}, f32[18,16,256]{2,1,0:T(8,128)S(1)}, u32[]{:S(2)}, u32[]{:S(2)}) collective-permute-start(f32[18,16,256]{2,1,0:T(8,128)S(1)} %get-tuple-element.73), channel_id=1, source_target_pairs={{0,8},{8,0},{16,24},{24,16},{32,40},{40,32},{48,56},{56,48},{64,72... | collective-permute-start | bytes 884744 | tf_op jit(solution)/shard_map/ppermute | solution.py:64
  102.5 9.9 %collective-permute-start.22 = (f32[18,16,256]{2,1,0:T(8,128)S(1)}, f32[18,16,256]{2,1,0:T(8,128)S(1)}, u32[]{:S(2)}, u32[]{:S(2)}) collective-permute-start(f32[18,16,256]{2,1,0:T(8,128)S(1)} %get-tuple-element.74), channel_id=1, source_target_pairs={{8,16},{16,8},{24,32},{32,24},{40,48},{48,40},{56,64},{64,56},{72,... | collective-permute-start | bytes 884744 | tf_op jit(solution)/shard_map/ppermute | solution.py:64
  108.9 16.5 %collective-permute-start.15 = (f32[3,26,8,256]{3,2,1,0:T(8,128)S(1)}, f32[3,26,8,256]{3,2,1,0:T(8,128)S(1)}, u32[]{:S(2)}, u32[]{:S(2)}) collective-permute-start(f32[3,26,8,256]{3,2,1,0:T(8,128)S(1)} %get-tuple-element.65), channel_id=1, source_target_pairs={{0,1},{1,0},{2,3},{3,2},{4,5},{5,4},{6,7},{7,6},{8,9},{9,8},{10,11... | collective-permute-start | bytes 1916936 | tf_op jit(solution)/shard_map/ppermute | solution.py:64
  109.0 20.5 %collective-permute-start.16 = (f32[3,26,8,256]{3,2,1,0:T(8,128)S(1)}, f32[3,26,8,256]{3,2,1,0:T(8,128)S(1)}, u32[]{:S(2)}, u32[]{:S(2)}) collective-permute-start(f32[3,26,8,256]{3,2,1,0:T(8,128)S(1)} %get-tuple-element.66), channel_id=1, source_target_pairs={{1,2},{2,1},{3,4},{4,3},{5,6},{6,5},{9,10},{10,9},{11,12},{12,11},... | collective-permute-start | bytes 1916936 | tf_op jit(solution)/shard_map/ppermute | solution.py:64
  113.4 33.8 %collective-permute-start.23 = (f32[3,22,8,256]{3,2,1,0:T(8,128)S(1)}, f32[3,22,8,256]{3,2,1,0:T(8,128)S(1)}, u32[]{:S(2)}, u32[]{:S(2)}) collective-permute-start(f32[3,22,8,256]{3,2,1,0:T(8,128)S(1)} %get-tuple-element.75), channel_id=1, source_target_pairs={{0,1},{1,0},{2,3},{3,2},{4,5},{5,4},{6,7},{7,6},{8,9},{9,8},{10,11... | collective-permute-start | bytes 1622024 | tf_op jit(solution)/shard_map/ppermute | solution.py:64
  113.5 33.7 %collective-permute-start.24 = (f32[3,22,8,256]{3,2,1,0:T(8,128)S(1)}, f32[3,22,8,256]{3,2,1,0:T(8,128)S(1)}, u32[]{:S(2)}, u32[]{:S(2)}) collective-permute-start(f32[3,22,8,256]{3,2,1,0:T(8,128)S(1)} %get-tuple-element.76), channel_id=1, source_target_pairs={{1,2},{2,1},{3,4},{4,3},{5,6},{6,5},{9,10},{10,9},{11,12},{12,11},... | collective-permute-start | bytes 1622024 | tf_op jit(solution)/shard_map/ppermute | solution.py:64
  210.0 65.2 %all-to-all-start = ((f32[8,33,16,256]{3,2,1,0:T(8,128)}), f32[8,33,16,256]{3,2,1,0:T(8,128)}, u32[]{:S(2)}, u32[]{:S(2)}) async-start(f32[8,33,16,256]{3,2,1,0:T(8,128)} %shard_map.76), calls=%async_computation | async-start | bytes 8650752 | tf_op jit(solution)/shard_map/all_to_all | solution.py:1022
  277.5 25.4 %collective-permute-start.37 = (f32[8,5,16,256]{3,2,1,0:T(8,128)S(1)}, f32[8,5,16,256]{3,2,1,0:T(8,128)S(1)}, u32[]{:S(2)}, u32[]{:S(2)}) collective-permute-start(f32[8,5,16,256]{3,2,1,0:T(8,128)S(1)} %get-tuple-element.102), channel_id=1, source_target_pairs={{0,8},{8,0},{16,24},{24,16},{32,40},{40,32},{48,56},{56,48},{64,72... | collective-permute-start | bytes 1966088 | tf_op jit(solution)/shard_map/ppermute | solution.py:64
  280.0 22.9 %collective-permute-start.38 = (f32[8,5,16,256]{3,2,1,0:T(8,128)S(1)}, f32[8,5,16,256]{3,2,1,0:T(8,128)S(1)}, u32[]{:S(2)}, u32[]{:S(2)}) collective-permute-start(f32[8,5,16,256]{3,2,1,0:T(8,128)S(1)} %get-tuple-element.101), channel_id=1, source_target_pairs={{8,16},{16,8},{24,32},{32,24},{40,48},{48,40},{56,64},{64,56},{72,... | collective-permute-start | bytes 1966088 | tf_op jit(solution)/shard_map/ppermute | solution.py:64
  (31 other events, 380.0 us)
